TPU v7x, 1024 devices: a whole 4x8x16 slice. The times are simulated.
1024 devices in a mesh: dp: 32 (over y, z_hi), blk: 32 (over z_lo, x, core).
Axes of the slice: x: 4, y: 8, z: 16 (z_hi: 4, z_lo: 4; z = z_hi * 4 + z_lo), core: 2. Of those that a mesh axis runs over, the one named last changes fastest.
Arguments:
- captions: bfloat16 [32, 32, 24, 16, 1152], P('dp', 'blk')
- lengths: int32 [32, 32, 24], P('dp', 'blk'), may hold values from 4 to 16, as said below
- destination: int32 [32, 32, 24], P('dp', 'blk'), may hold values from 0 to 31, as said below
- labels: int32 [32, 32, 24], P('dp', 'blk'), may hold values from 0 to 1023
- images: bfloat16 [32, 32, 32, 1152], P('dp', 'blk')
- position: bfloat16 [16, 1152], replicated, may hold values from -6 to 6
- gain_in: float32 [1152], replicated, may hold values from 0.4 to 2.5
- gain_out: float32 [1152], replicated, may hold values from 0.4 to 2.5
- query_proj: bfloat16 [1152, 576], replicated, may hold values from -0.1875 to 0.1875
- pair_proj: bfloat16 [1152, 1152], replicated, may hold values from -0.1875 to 0.1875
- out_proj: bfloat16 [576, 1152], replicated, may hold values from -0.25 to 0.25
- head_proj: bfloat16 [1152, 1152], replicated, may hold values from -0.1875 to 0.1875
- temper: float32 [8], replicated, may hold values from 3 to 12
- logit_scale: float32 [1], replicated, may hold values from 4 to 12
- logit_bias: float32 [1], replicated, may hold values from -3 to -0.5
Outputs:
- text_grad: float32 [32, 32, 32, 1152], P('dp', 'blk')
- image_grad: float32 [32, 32, 32, 1152], P('dp', 'blk')
Inputs may be any that keep to these rules, and one draw needn't show every extreme that they name: The 24 rows of one device name different destinations; in each blk column one destination receives a row from every dp index, so at most one caption goes from one device to one destination. `lengths`: positions at and after a row's count are padding. `labels`: the paired image's row among the 1024 images of the destination's dp index, ordered by blk index and then by row.
All inputs are finite; a program needn't handle non-finite values.
Results may differ from a plain program's by a relative error of at most 0.0095.
Values may be sent and summed in bfloat16 or wider, within the bound.
No kernel may reach another device: no remote copies, remote signals or barrier semaphores. Data moves between devices by JAX's collectives and lax.ppermute only.
A program may use at most 64 MiB of HBM per device.

v0:
```python
import jax
import jax.numpy as jnp
from jax import lax
from jax.sharding import PartitionSpec as P


def layer_norm(values, gain):
    center = values - jnp.mean(values, axis=-1, keepdims=True)
    spread = jnp.mean(center * center, axis=-1, keepdims=True)
    return center * lax.rsqrt(spread + 1e-06) * gain


def unit_rows(values):
    return values * lax.rsqrt(jnp.sum(values * values, axis=-1, keepdims=True) + 1e-06)


def text_tower(tokens, counts, params):
    position, gain_in, gain_out, query_proj, pair_proj, out_proj, head_proj, temper = params
    number = tokens.shape[0]
    length = tokens.shape[1]
    width = tokens.shape[2]
    heads = temper.shape[0]
    head_size = query_proj.shape[1] // heads
    summed = tokens.astype(jnp.float32) + position.astype(jnp.float32)[None]
    normed = layer_norm(summed, gain_in).astype(jnp.bfloat16)
    paired = jnp.dot(
        normed.reshape(number * length, width), pair_proj, preferred_element_type=jnp.float32
    ).astype(jnp.bfloat16)
    paired = paired.reshape(number, length, 2, heads, head_size)
    bounded = jnp.maximum(counts, 1)
    final_pos = (bounded - 1)[:, None, None]
    normed_last = jnp.take_along_axis(normed, final_pos, axis=1)[:, 0]
    summed_last = jnp.take_along_axis(summed, final_pos, axis=1)[:, 0]
    queries = jnp.dot(normed_last, query_proj, preferred_element_type=jnp.float32).reshape(
        number, heads, head_size
    )
    query_unit = unit_rows(queries) * temper[None, :, None]
    key_unit = unit_rows(paired[:, :, 0].astype(jnp.float32))
    scores = jnp.einsum("chs,clhs->chl", query_unit, key_unit)
    visible = jnp.arange(length, dtype=jnp.int32)[None, :] < bounded[:, None]
    raised = jnp.where(visible[:, None, :], jnp.exp(scores), 0.0)
    probs = (raised / jnp.sum(raised, axis=2, keepdims=True)).astype(jnp.bfloat16)
    attended = jnp.einsum(
        "chl,clhs->chs", probs, paired[:, :, 1], preferred_element_type=jnp.float32
    )
    attended = attended.astype(jnp.bfloat16).reshape(number, heads * head_size)
    residual_out = summed_last + jnp.dot(attended, out_proj, preferred_element_type=jnp.float32)
    final_normed = layer_norm(residual_out, gain_out).astype(jnp.bfloat16)
    return unit_rows(jnp.dot(final_normed, head_proj, preferred_element_type=jnp.float32)).astype(
        jnp.bfloat16
    )


def local(
    captions,
    lengths,
    destination,
    labels,
    images,
    position,
    gain_in,
    gain_out,
    query_proj,
    pair_proj,
    out_proj,
    head_proj,
    temper,
    logit_scale,
    logit_bias,
):
    slots = lax.axis_size("dp")
    own_rows = captions[0, 0]
    row_count = lengths[0, 0]
    row_target = destination[0, 0]
    row_label = labels[0, 0]
    params = (position, gain_in, gain_out, query_proj, pair_proj, out_proj, head_proj, temper)
    routing = row_target[None, :] == jnp.arange(slots, dtype=jnp.int32)[:, None]
    route_int = routing.astype(jnp.int32)
    route_half = routing.astype(jnp.bfloat16)
    sent_label = jnp.sum(route_int * row_label[None, :], axis=1)
    flat = own_rows.reshape(own_rows.shape[0], -1)
    sent = jnp.dot(route_half, flat, preferred_element_type=jnp.float32).astype(jnp.bfloat16)
    sent = sent.reshape((slots,) + own_rows.shape[1:])
    sent_count = jnp.sum(route_int * row_count[None, :], axis=1)
    got_rows, got_count, slot_label = (
        lax.all_to_all(sent, "dp", split_axis=0, concat_axis=0, tiled=True),
        lax.all_to_all(sent_count, "dp", split_axis=0, concat_axis=0, tiled=True),
        lax.all_to_all(sent_label, "dp", split_axis=0, concat_axis=0, tiled=True),
    )
    text = text_tower(got_rows, got_count, params)
    live = (got_count > 0).astype(jnp.int32)
    image_unit = unit_rows(images[0, 0].astype(jnp.float32)).astype(jnp.bfloat16)
    image_count = image_unit.shape[0]
    scale = logit_scale[0]
    offset = logit_bias[0]
    image_index = lax.axis_index("blk") * image_count + jnp.arange(image_count, dtype=jnp.int32)

    def slope_tile(text_rows, text_label, text_live, image_rows, column_index):
        logits = (
            scale
            * lax.dot_general(
                text_rows, image_rows, (((1,), (1,)), ((), ())), preferred_element_type=jnp.float32
            )
            + offset
        )
        sign = jnp.where(text_label[:, None] == column_index[None, :], 1.0, -1.0)
        return (
            -sign / (1.0 + jnp.exp(sign * logits)) * text_live[:, None].astype(jnp.float32)
        ).astype(jnp.bfloat16)

    piece = (
        lax.all_gather(text, "blk", axis=0, tiled=True),
        lax.all_gather(slot_label, "blk", axis=0, tiled=True),
        lax.all_gather(live, "blk", axis=0, tiled=True),
    )
    slopes = slope_tile(piece[0], piece[1], piece[2], image_unit, image_index)
    image_sum = lax.dot_general(
        slopes, piece[0], (((0,), (0,)), ((), ())), preferred_element_type=jnp.float32
    )
    piece = lax.all_gather(image_unit, "blk", axis=0, tiled=True)
    column_index = jnp.arange(piece.shape[0], dtype=jnp.int32)
    slopes = slope_tile(text, slot_label, live, piece, column_index)
    text_sum = jnp.dot(slopes, piece, preferred_element_type=jnp.float32)
    return ((scale * text_sum)[None, None], (scale * image_sum)[None, None])


def solution(mesh):
    return jax.shard_map(
        local,
        mesh=mesh,
        in_specs=(
            P("dp", "blk", None, None, None),
            P("dp", "blk", None),
            P("dp", "blk", None),
            P("dp", "blk", None),
            P("dp", "blk", None, None),
            P(),
            P(),
            P(),
            P(),
            P(),
            P(),
            P(),
            P(),
            P(),
            P(),
        ),
        out_specs=(P("dp", "blk", None, None), P("dp", "blk", None, None)),
        check_vma=False,
    )
```

profile of v0, /device:TPU:1, one launch (start us, length us, event | category | flops | bytes accessed | tf_op | source)
XLA Modules:
  0.0 232.7 jit_solution(10199173037159961320)
XLA Ops:
  8.8 24.9 %all-to-all-start.1 = ((s32[32,1,1]{2,1,0:T(1,128)}), s32[32,1,1]{2,1,0:T(1,128)S(1)}, u32[]{:S(2)}, u32[]{:S(2)}) async-start(s32[32,1,1]{2,1,0:T(1,128)} %copy.42), calls=%async_computation.1 | async-start | bytes 32768 | tf_op jit(solution)/shard_map/all_to_all | solution.py:87
  33.7 1.3 copy.51
  37.5 12.0 %all-to-all-done.1 = s32[32,1,1]{2,1,0:T(1,128)S(1)} async-done(((s32[32,1,1]{2,1,0:T(1,128)}), s32[32,1,1]{2,1,0:T(1,128)S(1)}, u32[]{:S(2)}, u32[]{:S(2)}) %all-to-all-start.1) | async-done | bytes 160 | tf_op jit(solution)/shard_map/all_to_all | solution.py:87
  49.5 4.7 %all-to-all-start.2 = ((bf16[32,16,1152]{2,1,0:T(8,128)(2,1)}), bf16[32,16,1152]{2,1,0:T(8,128)(2,1)}, u32[]{:S(2)}, u32[]{:S(2)}) async-start(bf16[32,16,1152]{2,1,0:T(8,128)(2,1)} %bitcast.91), calls=%async_computation.2 | async-start | bytes 2359296 | tf_op jit(solution)/shard_map/all_to_all | solution.py:86
  55.3 31.5 %all-to-all-done.2 = bf16[32,16,1152]{2,1,0:T(8,128)(2,1)} async-done(((bf16[32,16,1152]{2,1,0:T(8,128)(2,1)}), bf16[32,16,1152]{2,1,0:T(8,128)(2,1)}, u32[]{:S(2)}, u32[]{:S(2)}) %all-to-all-start.2) | async-done | bytes 1179680 | tf_op jit(solution)/shard_map/all_to_all | solution.py:86
  86.8 2.9 %convert_add_fusion = (f32[32,16,1152]{2,1,0:T(8,128)}, f32[32,16]{1,0:T(8,128)S(1)}) fusion(bf16[32,16,1152]{2,1,0:T(8,128)(2,1)} %all-to-all-done.2, f32[16,1152]{1,0:T(8,128)S(1)} %convert_element_type.74), kind=kLoop, calls=%fused_computation.9 | loop fusion | flops 1768960 | bytes 3614720 | tf_op jit(solution)/shard_map/add | solution.py:24
  89.7 1.8 multiply_reduce_fusion
  91.5 2.8 %multiply_convert_fusion = bf16[32,16,1152]{2,1,0:T(8,128)(2,1)} fusion(bf16[32,16,1152]{2,1,0:T(8,128)(2,1)} %all-to-all-done.2, f32[1152]{0:T(1024)S(1)} %copy-done.5, f32[32,16]{1,0:T(8,128)S(1)} %add_rsqrt_fusion.1, f32[32,16]{1,0:T(8,128)S(1)} %broadcast_multiply_fusion, f32[16,1152]{1,0:T(8,128)S(1)} %convert_element_type.74), kind=kLoop, calls=%fused_computation.7 | loop fusion | flops 3538944 | bytes 2441728 | tf_op jit(solution)/shard_map/convert_element_type | solution.py:25
  94.3 1.6 gather_fusion.1
  95.9 4.2 %convolution_convert_fusion.1 = bf16[512,1152]{1,0:T(8,128)(2,1)} fusion(bf16[512,1152]{1,0:T(8,128)(2,1)} %bitcast.94, bf16[1152,1152]{1,0:T(8,128)(2,1)S(1)} %copy-done), kind=kOutput, calls=%fused_computation.4 | convolution fusion | flops 1359544320 | bytes 5013504 | tf_op jit(solution)/shard_map/dot_general | solution.py:26
  100.1 5.7 %reshape.194 = bf16[32,16,2,8,72]{4,3,2,1,0:T(8,128)(2,1)} reshape(bf16[512,1152]{1,0:T(8,128)(2,1)} %convolution_convert_fusion.1) | data formatting | bytes 2359296 | tf_op jit(solution)/shard_map/reshape | solution.py:29
  105.8 2.0 fusion.3
  107.8 2.2 multiply_reduce_fusion.3
  111.9 1.3 slice_bitcast_fusion
  113.7 1.6 gather_fusion
  115.3 1.8 fusion.65
  117.3 2.5 %multiply_reduce_fusion.1 = (f32[32]{0:T(128)S(1)}, f32[32,1152]{1,0:T(8,128)S(1)}) fusion(bf16[1152,1152]{1,0:T(8,128)(2,1)} %param.26, f32[32,1152]{1,0:T(8,128)S(1)} %get-tuple-element.14, f32[1152]{0:T(1024)S(1)} %copy-done.6, f32[32]{0:T(128)S(1)} %add_rsqrt_fusion.5, f32[32]{0:T(128)S(1)} %broadcast_multiply_fusion.1), kind=kOutput, calls=%fused_computation.53 | convolution fusion | flops 85155808 | bytes 2954112 | tf_op jit(solution)/shard_map/dot_general | solution.py:49
  121.3 10.5 %all-to-all-start = ((s32[32,1,1]{2,1,0:T(1,128)}), s32[32,1,1]{2,1,0:T(1,128)S(1)}, u32[]{:S(2)}, u32[]{:S(2)}) async-start(s32[32,1,1]{2,1,0:T(1,128)} %copy.41), calls=%async_computation | async-start | bytes 32768 | tf_op jit(solution)/shard_map/all_to_all | solution.py:88
  133.2 1.3 dynamic-slice
  135.1 12.5 %all-to-all-done = s32[32,1,1]{2,1,0:T(1,128)S(1)} async-done(((s32[32,1,1]{2,1,0:T(1,128)}), s32[32,1,1]{2,1,0:T(1,128)S(1)}, u32[]{:S(2)}, u32[]{:S(2)}) %all-to-all-start) | async-done | bytes 160 | tf_op jit(solution)/shard_map/all_to_all | solution.py:88
  148.7 43.3 %all-reduce.2 = (s32[1024]{0:T(1024)S(1)}, s32[1024]{0:T(1024)S(1)}) all-reduce(s32[1024]{0:T(1024)S(1)} %bitcast_dynamic-update-slice_fusion, s32[1024]{0:T(1024)S(1)} %dynamic-update-slice), channel_id=3, replica_groups=mesh['dp'=32,'blk'=32] {'blk'}, use_global_device_ids=true, to_apply=%add.1 | all-reduce | flops 2048 | bytes 16384
  192.0 4.4 %fusion.1 = f32[1,1,32,1152]{3,2,1,0:T(8,128)} fusion(bf16[1024,1152]{1,0:T(8,128)(2,1)} %all-gather.5.cloned.1.call-done, bf16[32,1152]{1,0:T(8,128)(2,1)} %multiply_convert_fusion.1, f32[]{:T(128)} %bitcast.87, f32[32]{0:T(128)S(1)} %get-tuple-element.10, f32[]{:T(128)} %bitcast.89, s32[32]{0:T(128)S(1)} %reduce), kind=kOutput, calls=%fused_computation.13 | convolution fusion | flops 151359488 | bytes 2580744 | tf_op jit(solution)/shard_map/dot_general | solution.py:123
  196.4 25.2 %all-gather.7.cloned.1.call-done = bf16[1024,1152]{1,0:T(8,128)(2,1)} async-done(((bf16[32,1152]{1,0:T(8,128)(2,1)}), bf16[1024,1152]{1,0:T(8,128)(2,1)}) %all-gather.7.cloned.1.call-update) | async-done | bytes 2359312 | tf_op jit(solution)/shard_map/all_gather | solution.py:112
  221.6 4.3 %fusion.2 = f32[1,1,32,1152]{3,2,1,0:T(8,128)} fusion(bf16[1024,1152]{1,0:T(8,128)(2,1)} %all-gather.7.cloned.1.call-done, bf16[32,1152]{1,0:T(8,128)(2,1)S(1)} %copy-done.2, f32[]{:T(128)} %bitcast.88, f32[1024]{0:T(1024)S(1)} %convert_element_type.97, s32[1024]{0:T(1024)S(1)} %get-tuple-element.5, f32[]{:T(128)} %bitcast.90, s32[32]{0:T(128)S(1)} %iota_add_fusion), kind=kOutput, calls=%fused_computation.14 | convolution fusion | flops 151359488 | bytes 2588808 | tf_op jit(solution)/shard_map/dot_general | solution.py:117
  (62 shorter events, 10.2 us)
Async XLA Ops:
  7.2 88.8 %copy-start = (bf16[1152,1152]{1,0:T(8,128)(2,1)S(1)}, bf16[1152,1152]{1,0:T(8,128)(2,1)}, u32[]{:S(2)}) copy-start(bf16[1152,1152]{1,0:T(8,128)(2,1)} %param.24) | copy-start | bytes 7962628
  8.8 40.7 %all-to-all-start.1 = ((s32[32,1,1]{2,1,0:T(1,128)}), s32[32,1,1]{2,1,0:T(1,128)S(1)}, u32[]{:S(2)}, u32[]{:S(2)}) async-start(s32[32,1,1]{2,1,0:T(1,128)} %copy.42), calls=%async_computation.1 | async-start | bytes 32768 | tf_op jit(solution)/shard_map/all_to_all | solution.py:87
  36.3 17.9 %copy-start.3 = (bf16[1,1,32,1152]{3,2,1,0:T(8,128)(2,1)S(1)}, bf16[1,1,32,1152]{3,2,1,0:T(8,128)(2,1)}, u32[]{:S(2)}) copy-start(bf16[1,1,32,1152]{3,2,1,0:T(8,128)(2,1)} %param.19) | copy-start | bytes 221188
  36.3 18.8 %copy-start.4 = (bf16[16,1152]{1,0:T(8,128)(2,1)S(1)}, bf16[16,1152]{1,0:T(8,128)(2,1)}, u32[]{:S(2)}) copy-start(bf16[16,1152]{1,0:T(8,128)(2,1)} %param.20) | copy-start | bytes 110596
  49.5 37.4 %all-to-all-start.2 = ((bf16[32,16,1152]{2,1,0:T(8,128)(2,1)}), bf16[32,16,1152]{2,1,0:T(8,128)(2,1)}, u32[]{:S(2)}, u32[]{:S(2)}) async-start(bf16[32,16,1152]{2,1,0:T(8,128)(2,1)} %bitcast.91), calls=%async_computation.2 | async-start | bytes 2359296 | tf_op jit(solution)/shard_map/all_to_all | solution.py:86
  54.1 137.9 %all-gather.5.cloned.1.call-start = ((), (), s32[]{:S(2)}) async-start(), calls=%async_computation.3 | async-start | bytes 2433024 | tf_op jit(solution)/shard_map/all_gather | solution.py:120
  55.1 166.5 %all-gather.7.cloned.1.call-start = ((), (), s32[]{:S(2)}) async-start(), calls=%async_computation.4 | async-start | bytes 2433024 | tf_op jit(solution)/shard_map/all_gather | solution.py:112
  55.3 36.2 %copy-start.5 = (f32[1152]{0:T(1024)S(1)}, f32[1152]{0:T(1024)}, u32[]{:S(2)}) copy-start(f32[1152]{0:T(1024)} %param.21) | copy-start | bytes 13828
  100.1 9.9 %copy-start.7 = (f32[8]{0:T(128)S(1)}, f32[8]{0:T(128)}, u32[]{:S(2)}) copy-start(f32[8]{0:T(128)} %param.27) | copy-start | bytes 100
  105.8 4.4 %copy-start.1 = (bf16[32,16,2,8,72]{4,3,2,1,0:T(8,128)(2,1)S(1)}, bf16[32,16,2,8,72]{4,3,2,1,0:T(8,128)(2,1)}, u32[]{:S(2)}) copy-start(bf16[32,16,2,8,72]{4,3,2,1,0:T(8,128)(2,1)} %reshape.194) | copy-start | bytes 3538948
  113.2 4.2 %copy-start.6 = (f32[1152]{0:T(1024)S(1)}, f32[1152]{0:T(1024)}, u32[]{:S(2)}) copy-start(f32[1152]{0:T(1024)} %param.22) | copy-start | bytes 13828
  121.3 26.4 %all-to-all-start = ((s32[32,1,1]{2,1,0:T(1,128)}), s32[32,1,1]{2,1,0:T(1,128)S(1)}, u32[]{:S(2)}, u32[]{:S(2)}) async-start(s32[32,1,1]{2,1,0:T(1,128)} %copy.41), calls=%async_computation | async-start | bytes 32768 | tf_op jit(solution)/shard_map/all_to_all | solution.py:88
  192.0 29.6 %copy-start.2 = (bf16[32,1152]{1,0:T(8,128)(2,1)S(1)}, bf16[32,1152]{1,0:T(8,128)(2,1)}, u32[]{:S(2)}) copy-start(bf16[32,1152]{1,0:T(8,128)(2,1)} %fusion.30) | copy-start | bytes 221188
Sparse Core Ops, SparseCore 0:
  58.3 94.9 all-gather.4
  156.0 65.5 all-gather.6
where the time goes:
time: 234 us; the launch traced here: 233 us
  waiting for transfers between devices  81.3 us (35%)
  blocking collectives  43.3 us (19%)
  starting transfers between devices  40.2 us (17%)
  matrix products  21.5 us (9%)
  between operations  16.3 us (7%)
  local copies, waits for them, and re-layouts  16.2 us (7%)
  other arithmetic  13.9 us (6%)
    unnamed x1, blocking collectives  43.3 us
    all_to_all x1, waiting for transfers between devices, local(): lax.all_to_all(sent, 'dp', split_axis=0, concat_axis=0, tiled=True)  31.5 us
    all_gather x1, waiting for transfers between devices, local(): lax.all_gather(text, 'blk', axis=0, tiled=True)  25.2 us
    all_to_all x1, starting transfers between devices, local(): lax.all_to_all(sent_count, 'dp', split_axis=0, concat_axis=0, tiled=True)  24.9 us
    all_to_all x1, waiting for transfers between devices, local(): lax.all_to_all(sent_label, 'dp', split_axis=0, concat_axis=0, tiled=True)  12.5 us
    all_to_all x1, waiting for transfers between devices, local(): lax.all_to_all(sent_count, 'dp', split_axis=0, concat_axis=0, tiled=True)  12 us
    all_to_all x1, starting transfers between devices, local(): lax.all_to_all(sent_label, 'dp', split_axis=0, concat_axis=0, tiled=True)  10.5 us
    reshape x1, local copies, waits for them, and re-layouts, text_tower(): paired = paired.reshape(number, length, 2, heads, head_size)  5.7 us
  transfers between devices with their start and end apart: 5, of which 4 were waited for; matrix products, arithmetic and copies ran while one was open for 20% of the time, Pallas kernels for 0%

commit v1 on v0

--- a/solution.py
+++ b/solution.py
@@ -2,6 +2,10 @@
 import jax.numpy as jnp
 from jax import lax
 from jax.sharding import PartitionSpec as P
+
+CS = 2
+XS = 4
+AUX = 128
 
 
 def layer_norm(values, gain):
@@ -51,6 +55,85 @@
     )
 
 
+def encode(captions, counts, target, label, params, slots):
+    text = text_tower(captions, counts, params)
+    number = text.shape[0]
+    column = jnp.arange(AUX, dtype=jnp.int32)[None, :]
+    high = (label // 32)[:, None]
+    low = (label % 32)[:, None]
+    aux = jnp.where(column == 0, high, jnp.where(column == 1, low, jnp.where(column == 2, 1, 0)))
+    wide = jnp.concatenate([text, aux.astype(jnp.bfloat16)], axis=1)
+    routing = (target[None, :] == jnp.arange(slots, dtype=jnp.int32)[:, None]).astype(jnp.bfloat16)
+    return jnp.dot(routing, wide, preferred_element_type=jnp.float32).astype(jnp.bfloat16)
+
+
+def slope_of(logits, same, live):
+    sign = jnp.where(same, 1.0, -1.0)
+    return (-sign / (1.0 + jnp.exp(sign * logits)) * live).astype(jnp.bfloat16)
+
+
+NT = (((1,), (1,)), ((), ()))
+
+
+def text_part(wide, image_all, scale, offset):
+    width = image_all.shape[1]
+    text = wide[:, :width]
+    aux = wide[:, width:].astype(jnp.float32)
+    label = aux[:, 0:1] * 32.0 + aux[:, 1:2]
+    live = aux[:, 2:3]
+    logits = scale * lax.dot_general(text, image_all, NT, preferred_element_type=jnp.float32) + offset
+    index = jnp.arange(image_all.shape[0], dtype=jnp.int32)[None, :].astype(jnp.float32)
+    slopes = slope_of(logits, label == index, live)
+    return scale * jnp.dot(slopes, image_all, preferred_element_type=jnp.float32)
+
+
+def image_parts(wide, images, index, scale, offset):
+    width = images.shape[1]
+    text = wide[:, :width]
+    aux = wide[:, width:].astype(jnp.float32)
+    label = (aux[:, 0] * 32.0 + aux[:, 1])[None, :]
+    live = aux[:, 2][None, :]
+    logits = scale * lax.dot_general(images, text, NT, preferred_element_type=jnp.float32) + offset
+    slopes = slope_of(logits, label == index[:, None].astype(jnp.float32), live)
+    return scale * jnp.dot(slopes, text, preferred_element_type=jnp.float32)
+
+
+def loss_grads(wide, image_unit, image_all, scale, offset):
+    blocks = lax.axis_size("blk")
+    zs = blocks // (XS * CS)
+    count, width = image_unit.shape
+    place = lambda z, x, c: (z * XS + x) * CS + c
+    pairs = [[place(z, x, c) for c in range(CS)] for z in range(zs) for x in range(XS)]
+    lines = [[place(z, x, c) for z in range(zs)] for x in range(XS) for c in range(CS)]
+    gathered = lax.all_gather(wide, "blk", axis=0, tiled=True, axis_index_groups=pairs)
+    gathered = lax.all_gather(gathered, "blk", axis=0, tiled=True, axis_index_groups=lines)
+    mine = lax.axis_index("blk")
+    my_x = (mine // CS) % XS
+    base = mine - my_x * CS
+    rows = []
+    index = []
+    for k in range(XS):
+        there = base + ((my_x + k) % XS) * CS
+        rows.append(lax.dynamic_slice_in_dim(image_all, there * count, count, axis=0))
+        index.append(there * count + jnp.arange(count, dtype=jnp.int32))
+    parts = image_parts(
+        gathered, jnp.concatenate(rows), jnp.concatenate(index), scale, offset
+    ).reshape(XS, count, width)
+    image_sum = parts[0]
+    for k in range(1, XS):
+        shift = [
+            (place(z, x, c), place(z, (x + k) % XS, c))
+            for z in range(zs)
+            for x in range(XS)
+            for c in range(CS)
+        ]
+        image_sum = image_sum + lax.ppermute(
+            parts[k].astype(jnp.bfloat16), "blk", shift
+        ).astype(jnp.float32)
+    text_sum = text_part(wide, image_all, scale, offset)
+    return text_sum, image_sum
+
+
 def local(
     captions,
     lengths,
@@ -69,59 +152,13 @@
     logit_bias,
 ):
     slots = lax.axis_size("dp")
-    own_rows = captions[0, 0]
-    row_count = lengths[0, 0]
-    row_target = destination[0, 0]
-    row_label = labels[0, 0]
     params = (position, gain_in, gain_out, query_proj, pair_proj, out_proj, head_proj, temper)
-    routing = row_target[None, :] == jnp.arange(slots, dtype=jnp.int32)[:, None]
-    route_int = routing.astype(jnp.int32)
-    route_half = routing.astype(jnp.bfloat16)
-    sent_label = jnp.sum(route_int * row_label[None, :], axis=1)
-    flat = own_rows.reshape(own_rows.shape[0], -1)
-    sent = jnp.dot(route_half, flat, preferred_element_type=jnp.float32).astype(jnp.bfloat16)
-    sent = sent.reshape((slots,) + own_rows.shape[1:])
-    sent_count = jnp.sum(route_int * row_count[None, :], axis=1)
-    got_rows, got_count, slot_label = (
-        lax.all_to_all(sent, "dp", split_axis=0, concat_axis=0, tiled=True),
-        lax.all_to_all(sent_count, "dp", split_axis=0, concat_axis=0, tiled=True),
-        lax.all_to_all(sent_label, "dp", split_axis=0, concat_axis=0, tiled=True),
-    )
-    text = text_tower(got_rows, got_count, params)
-    live = (got_count > 0).astype(jnp.int32)
     image_unit = unit_rows(images[0, 0].astype(jnp.float32)).astype(jnp.bfloat16)
-    image_count = image_unit.shape[0]
-    scale = logit_scale[0]
-    offset = logit_bias[0]
-    image_index = lax.axis_index("blk") * image_count + jnp.arange(image_count, dtype=jnp.int32)
-
-    def slope_tile(text_rows, text_label, text_live, image_rows, column_index):
-        logits = (
-            scale
-            * lax.dot_general(
-                text_rows, image_rows, (((1,), (1,)), ((), ())), preferred_element_type=jnp.float32
-            )
-            + offset
-        )
-        sign = jnp.where(text_label[:, None] == column_index[None, :], 1.0, -1.0)
-        return (
-            -sign / (1.0 + jnp.exp(sign * logits)) * text_live[:, None].astype(jnp.float32)
-        ).astype(jnp.bfloat16)
-
-    piece = (
-        lax.all_gather(text, "blk", axis=0, tiled=True),
-        lax.all_gather(slot_label, "blk", axis=0, tiled=True),
-        lax.all_gather(live, "blk", axis=0, tiled=True),
-    )
-    slopes = slope_tile(piece[0], piece[1], piece[2], image_unit, image_index)
-    image_sum = lax.dot_general(
-        slopes, piece[0], (((0,), (0,)), ((), ())), preferred_element_type=jnp.float32
-    )
-    piece = lax.all_gather(image_unit, "blk", axis=0, tiled=True)
-    column_index = jnp.arange(piece.shape[0], dtype=jnp.int32)
-    slopes = slope_tile(text, slot_label, live, piece, column_index)
-    text_sum = jnp.dot(slopes, piece, preferred_element_type=jnp.float32)
-    return ((scale * text_sum)[None, None], (scale * image_sum)[None, None])
+    image_all = lax.all_gather(image_unit, "blk", axis=0, tiled=True)
+    sent = encode(captions[0, 0], lengths[0, 0], destination[0, 0], labels[0, 0], params, slots)
+    wide = lax.all_to_all(sent, "dp", split_axis=0, concat_axis=0, tiled=True)
+    text_sum, image_sum = loss_grads(wide, image_unit, image_all, logit_scale[0], logit_bias[0])
+    return text_sum[None, None], image_sum[None, None]
 
 
 def solution(mesh):

time: 234 us -> 143 us (0.61)
  the two profiles are of different devices: /device:TPU:1 before, /device:TPU:8 now
where the time goes in v1:
time: 143 us; the launch traced here: 142 us
  starting transfers between devices  35 us (24%)
  other arithmetic  23.5 us (16%)
  blocking collectives  18.8 us (13%)
  waiting for transfers between devices  16.2 us (11%)
  local copies, waits for them, and re-layouts  16.1 us (11%)
  matrix products  16.1 us (11%)
  between operations  15.8 us (11%)
    all_to_all x1, starting transfers between devices, local(): wide = lax.all_to_all(sent, 'dp', split_axis=0, concat_axis=0, tiled=True)  24.6 us
    all_gather x1, blocking collectives, loss_grads(): lax.all_gather(gathered, 'blk', axis=0, tiled=True, axis_index_groups=lines)  16.9 us
    all_to_all x1, waiting for transfers between devices, local(): wide = lax.all_to_all(sent, 'dp', split_axis=0, concat_axis=0, tiled=True)  16.1 us
    ppermute x3, starting transfers between devices, loss_grads(): lax.ppermute(parts[k].astype(jnp.bfloat16), 'blk', shift)  10.4 us
    dot_general x1, matrix products, text_part(): jnp.dot(slopes, image_all, preferred_element_type=jnp.float32)  4.28 us
    reshape x1, local copies, waits for them, and re-layouts, text_tower(): paired = paired.reshape(number, length, 2, heads, head_size)  3.66 us
    convert_element_type x2, other arithmetic, text_tower(): normed = layer_norm(summed, gain_in).astype(jnp.bfloat16)  3.44 us
  transfers between devices with their start and end apart: 5, of which 2 were waited for; matrix products, arithmetic and copies ran while one was open for 32% of the time, Pallas kernels for 0%

profile of v1, /device:TPU:8, one launch (start us, length us, event | category | flops | bytes accessed | tf_op | source)
XLA Modules:
  0.0 141.5 jit_solution(3191756764202914896)
XLA Ops:
  8.4 1.6 %fusion.51 = bf16[32,1152]{1,0:T(8,128)(2,1)} fusion(bf16[1,1,32,1152]{3,2,1,0:T(8,128)(2,1)} %param.19, f32[32]{0:T(128)S(1)} %add_rsqrt_fusion.3), kind=kLoop, calls=%fused_computation.65 | loop fusion | flops 110592 | bytes 147584 | tf_op jit(solution)/shard_map/convert_element_type | solution.py:156
  14.6 2.5 %bitcast_add_fusion.1 = (f32[24,16,1152]{2,1,0:T(8,128)}, f32[24,16]{1,0:T(8,128)S(1)}) fusion(f32[16,1152]{1,0:T(8,128)S(1)} %convert_element_type.100, bf16[1,1,24,16,1152]{4,3,2,1,0:T(8,128)(2,1)} %param.15), kind=kLoop, calls=%fused_computation.17 | loop fusion | flops 1326720 | bytes 2729472 | tf_op jit(solution)/shard_map/add | solution.py:28
  20.9 1.4 rsqrt.54
  22.3 2.2 %multiply_convert_fusion = bf16[24,16,1152]{2,1,0:T(8,128)(2,1)} fusion(f32[1152]{0:T(1024)} %param.21, f32[24,16]{1,0:T(8,128)} %add_rsqrt_fusion.1, f32[24,16]{1,0:T(8,128)S(1)} %broadcast_multiply_fusion, f32[16,1152]{1,0:T(8,128)} %copy-done.2, bf16[1,1,24,16,1152]{4,3,2,1,0:T(8,128)(2,1)S(1)} %copy-done.1), kind=kLoop, calls=%fused_computation.18 | loop fusion | flops 2654208 | bytes 1850880 | tf_op jit(solution)/shard_map/convert_element_type | solution.py:29
  24.5 2.5 %gather_fusion.1 = bf16[24,1152]{1,0:T(8,128)(2,1)} fusion(bf16[24,16,1152]{2,1,0:T(8,128)(2,1)} %multiply_convert_fusion, s32[24]{0:T(128)S(1)} %or_bitcast_fusion), kind=kCustom, calls=%fused_computation.1 | custom fusion | bytes 110784 | tf_op jit(solution)/shard_map/jit(take_along_axis)/gather | solution.py:36
  26.9 2.7 %multiply_reduce_fusion.3 = (f32[24,8]{0,1:T(8,128)S(1)}, f32[24,8,72]{2,0,1:T(8,128)}) fusion(bf16[8,72,1152]{2,1,0:T(8,128)(2,1)} %bitcast.116, bf16[24,1152]{1,0:T(8,128)(2,1)} %gather_fusion.1, pred[24]{0:T(512)(128)(4,1)} %compare_and_fusion), kind=kOutput, calls=%fused_computation.80 | convolution fusion | flops 31905600 | bytes 1438488 | tf_op jit(solution)/shard_map/dot_general | solution.py:38
  30.9 1.4 %convolution_convert_fusion = bf16[384,1152]{1,0:T(8,128)(2,1)S(1)} fusion(bf16[384,1152]{1,0:T(8,128)(2,1)S(1)} %fusion.6, bf16[1152,1152]{1,0:T(8,128)(2,1)S(1)} %copy-done), kind=kOutput, calls=%fused_computation.3 | convolution fusion | flops 1019658240 | bytes 4423680 | tf_op jit(solution)/shard_map/dot_general | solution.py:30
  32.3 3.7 %reshape.322 = bf16[24,16,2,8,72]{4,3,2,1,0:T(8,128)(2,1)} reshape(bf16[384,1152]{1,0:T(8,128)(2,1)S(1)} %convolution_convert_fusion) | data formatting | bytes 1769472 | tf_op jit(solution)/shard_map/reshape | solution.py:33
  36.0 1.7 %fusion.7 = f32[24,16,8]{2,1,0:T(8,128)S(1)} fusion(bf16[24,16,2,8,72]{4,3,2,1,0:T(8,128)(2,1)} %reshape.322), kind=kLoop, calls=%fused_computation.20 | loop fusion | flops 660480 | bytes 454656 | tf_op jit(solution)/shard_map/reduce_sum | solution.py:18
  37.7 1.6 %convert_multiply_fusion = bf16[24,16,8,72]{3,2,1,0:T(8,128)(2,1)S(1)} fusion(f32[24,16,8]{2,1,0:T(8,128)S(1)} %add_rsqrt_fusion, bf16[24,16,2,8,72]{4,3,2,1,0:T(8,128)(2,1)} %reshape.322), kind=kLoop, calls=%fused_computation.10 | loop fusion | flops 663552 | bytes 897024 | tf_op jit(solution)/shard_map/mul | solution.py:18
  40.1 1.8 %gather_fusion = f32[24,1152]{1,0:T(8,128)S(1)} fusion(f32[24,16,1152]{2,1,0:T(8,128)} %get-tuple-element.10, s32[24]{0:T(128)S(1)} %or_bitcast_fusion), kind=kCustom, calls=%fused_computation | custom fusion | bytes 221376 | tf_op jit(solution)/shard_map/jit(take_along_axis)/gather | solution.py:37
  43.8 1.7 %fusion.101 = (f32[24]{0:T(128)S(1)}, f32[24,1152]{1,0:T(8,128)S(1)}) fusion(bf16[24,576]{1,0:T(8,128)(2,1)S(1)} %reshape.323, bf16[576,1152]{1,0:T(8,128)(2,1)} %param.25, f32[24,1152]{1,0:T(8,128)S(1)} %gather_fusion, pred[24]{0:T(512)(128)(4,1)S(1)} %copy-done.6), kind=kOutput, calls=%fused_computation.164 | convolution fusion | flops 31933416 | bytes 1576056 | tf_op jit(solution)/shard_map/dot_general | solution.py:51
  45.8 2.4 %multiply_reduce_fusion.1 = (f32[24]{0:T(128)S(1)}, f32[24,1152]{1,0:T(8,128)S(1)}) fusion(bf16[1152,1152]{1,0:T(8,128)(2,1)} %param.26, f32[24,1152]{1,0:T(8,128)S(1)} %get-tuple-element.20, f32[1152]{0:T(1024)S(1)} %copy-done.5, f32[24]{0:T(128)S(1)} %add_rsqrt_fusion.5, f32[24]{0:T(128)S(1)} %broadcast_multiply_fusion.1), kind=kOutput, calls=%fused_computation.75 | convolution fusion | flops 63866856 | bytes 2880288 | tf_op jit(solution)/shard_map/dot_general | solution.py:53
  50.4 24.6 %all-to-all-start = ((bf16[32,2,640]{2,1,0:T(2,128)(2,1)}), bf16[32,2,640]{2,1,0:T(2,128)(2,1)S(1)}, u32[]{:S(2)}, u32[]{:S(2)}) async-start(bf16[32,2,640]{2,1,0:T(2,128)(2,1)} %reshape.357), calls=%async_computation | async-start | bytes 163840 | tf_op jit(solution)/shard_map/all_to_all | solution.py:159
  77.0 16.1 %all-to-all-done = bf16[32,2,640]{2,1,0:T(2,128)(2,1)S(1)} async-done(((bf16[32,2,640]{2,1,0:T(2,128)(2,1)}), bf16[32,2,640]{2,1,0:T(2,128)(2,1)S(1)}, u32[]{:S(2)}, u32[]{:S(2)}) %all-to-all-start) | async-done | bytes 81952 | tf_op jit(solution)/shard_map/all_to_all | solution.py:159
  93.2 1.9 %all-gather = bf16[64,1,1280]{2,0,1:T(8,128)(2,1)S(1)} all-gather(bf16[32,1,1280]{2,0,1:T(8,128)(2,1)S(1)} %copy.28), channel_id=2, replica_groups={{0,1},{2,3},{4,5},{6,7},{8,9},{10,11},{12,13},{14,15},{16,17},{18,19},{..., dimensions={0}, use_global_device_ids=true | all-gather | bytes 245760 | tf_op jit(solution)/shard_map/all_gather | solution.py:108
  95.3 16.9 %all-gather.1 = bf16[256,1,1280]{2,0,1:T(8,128)(2,1)S(1)} all-gather(bf16[64,1,1280]{2,0,1:T(8,128)(2,1)S(1)} %all-gather), channel_id=3, replica_groups={{0,8,16,24},{1,9,17,25},{2,10,18,26},{3,11,19,27},{4,12,20,28},{5,13,21..., dimensions={0}, use_global_device_ids=true | all-gather | bytes 819200 | tf_op jit(solution)/shard_map/all_gather | solution.py:109
  113.1 1.7 %constant_dynamic-slice_fusion.3 = (bf16[32,1152]{1,0:T(8,128)(2,1)S(1)}, bf16[32,1152]{1,0:T(8,128)(2,1)S(1)}, bf16[32,1152]{1,0:T(8,128)(2,1)}, bf16[32,1152]{1,0:T(8,128)(2,1)}) fusion(bf16[1024,1152]{1,0:T(8,128)(2,1)} %all-gather.4.cloned.1.call-done, s32[]{:T(128)S(6)} %select_n.153, s32[]{:T(128)S(6)} %select_n.155, s32[]{:T(128)S(6)} %select_n.154, ...), kind=kLoop, calls=%fused_computation.140 | loop fusion | bytes 589840 | tf_op jit(solution)/shard_map/dynamic_slice | solution.py:117
  114.7 2.5 %fusion.102 = (bf16[128,1152]{1,0:T(8,128)(2,1)}, f32[128,1152]{1,0:T(8,128)}) fusion(bf16[256,1280]{1,0:T(8,128)(2,1)S(1)} %bitcast.118, bf16[32,1152]{1,0:T(8,128)(2,1)} %get-tuple-element.9, bf16[32,1152]{1,0:T(8,128)(2,1)S(1)} %get-tuple-element.7, bf16[32,1152]{1,0:T(8,128)(2,1)} %get-tuple-element.8, bf16[32,1152]{1,0:T(8,128)(2,1)S(1)} %get-tuple-element.6, ...), kind=kOutput, calls=%fused_computation.165 | convolution fusion | flops 152797184 | bytes 2363392 | tf_op jit(solution)/shard_map/dot_general | solution.py:98
  118.2 2.8 %collective-permute-start = (bf16[32,1152]{1,0:T(8,128)(2,1)S(1)}, bf16[32,1152]{1,0:T(8,128)(2,1)S(1)}, u32[]{:S(2)}, u32[]{:S(2)}) collective-permute-start(bf16[32,1152]{1,0:T(8,128)(2,1)S(1)} %get-tuple-element.12), channel_id=1, source_target_pairs={{0,2},{1,3},{2,4},{3,5},{4,6},{5,7},{6,0},{7,1},{8,10},{9,11},{10,... | collective-permute-start | bytes 221192 | tf_op jit(solution)/shard_map/ppermute | solution.py:130
  121.0 4.3 %collective-permute-start.2 = (bf16[32,1152]{1,0:T(8,128)(2,1)S(1)}, bf16[32,1152]{1,0:T(8,128)(2,1)S(1)}, u32[]{:S(2)}, u32[]{:S(2)}) collective-permute-start(bf16[32,1152]{1,0:T(8,128)(2,1)S(1)} %get-tuple-element.13), channel_id=1, source_target_pairs={{0,6},{1,7},{2,0},{3,1},{4,2},{5,3},{6,4},{7,5},{8,14},{9,15},{10,... | collective-permute-start | bytes 221192 | tf_op jit(solution)/shard_map/ppermute | solution.py:130
  125.3 3.3 %collective-permute-start.1 = (bf16[32,1152]{1,0:T(8,128)(2,1)S(1)}, bf16[32,1152]{1,0:T(8,128)(2,1)S(1)}, u32[]{:S(2)}, u32[]{:S(2)}) collective-permute-start(bf16[32,1152]{1,0:T(8,128)(2,1)S(1)} %get-tuple-element.14), channel_id=1, source_target_pairs={{0,4},{1,5},{2,6},{3,7},{4,0},{5,1},{6,2},{7,3},{8,12},{9,13},{10,... | collective-permute-start | bytes 221192 | tf_op jit(solution)/shard_map/ppermute | solution.py:130
  128.7 4.3 %fusion.1 = f32[1,1,32,1152]{3,2,1,0:T(8,128)} fusion(bf16[1024,1152]{1,0:T(8,128)(2,1)} %all-gather.4.cloned.1.call-done, bf16[32,1280]{1,0:T(8,128)(2,1)S(1)} %bitcast.120, f32[]{:T(128)} %bitcast.112, f32[32]{0:T(128)S(1)} %get-tuple-element.5, f32[]{:T(128)} %bitcast.114, f32[1024]{0:T(1024)S(1)} %iota_convert_fusion, f32[32]{0:T(128)S(1)} %get-tuple-element.4), kind=kOutput, calls=%fused_computation.6 | convolution fusion | flops 151359488 | bytes 4946432 | tf_op jit(solution)/shard_map/dot_general | solution.py:87
  133.1 1.6 %fusion.54 = f32[1,1,32,1152]{3,2,1,0:T(8,128)} fusion(f32[128,1152]{1,0:T(8,128)} %get-tuple-element.24, bf16[32,1152]{1,0:T(8,128)(2,1)S(1)} %collective-permute-done.2, bf16[32,1152]{1,0:T(8,128)(2,1)S(1)} %collective-permute-done.1, bf16[32,1152]{1,0:T(8,128)(2,1)S(1)} %collective-permute-done), kind=kLoop, calls=%fused_computation.69 | loop fusion | flops 221184 | bytes 516096 | tf_op jit(solution)/shard_map/broadcast_in_dim | solution.py:161
  (79 shorter events, 18.7 us)
Async XLA Ops:
  7.2 23.7 %copy-start = (bf16[1152,1152]{1,0:T(8,128)(2,1)S(1)}, bf16[1152,1152]{1,0:T(8,128)(2,1)}, u32[]{:S(2)}) copy-start(bf16[1152,1152]{1,0:T(8,128)(2,1)} %param.24) | copy-start | bytes 7962628
  7.2 10.6 %copy-start.1 = (bf16[1,1,24,16,1152]{4,3,2,1,0:T(8,128)(2,1)S(1)}, bf16[1,1,24,16,1152]{4,3,2,1,0:T(8,128)(2,1)}, u32[]{:S(2)}) copy-start(bf16[1,1,24,16,1152]{4,3,2,1,0:T(8,128)(2,1)} %param.15) | copy-start | bytes 2654212
  7.2 105.9 %all-gather.4.cloned.1.call-start = ((), (), s32[]{:S(2)}) async-start(), calls=%async_computation.1 | async-start | bytes 2433024 | tf_op jit(solution)/shard_map/all_gather | solution.py:157
  13.9 0.6 copy-start.2
  24.5 5.1 %copy-start.4 = (f32[1152]{0:T(1024)S(1)}, f32[1152]{0:T(1024)}, u32[]{:S(2)}) copy-start(f32[1152]{0:T(1024)} %param.21) | copy-start | bytes 13828
  36.0 3.3 %copy-start.3 = (f32[24,8,72]{2,0,1:T(8,128)S(1)}, f32[24,8,72]{2,0,1:T(8,128)}, u32[]{:S(2)}) copy-start(f32[24,8,72]{2,0,1:T(8,128)} %get-tuple-element.18) | copy-start | bytes 165892
  36.0 3.3 %copy-start.8 = (f32[8]{0:T(128)S(1)}, f32[8]{0:T(128)}, u32[]{:S(2)}) copy-start(f32[8]{0:T(128)} %param.27) | copy-start | bytes 100
  37.7 2.4 %copy-start.7 = (pred[24,16]{0,1:T(8,128)(4,1)S(1)}, pred[24,16]{0,1:T(8,128)(4,1)}, u32[]{:S(2)}) copy-start(pred[24,16]{0,1:T(8,128)(4,1)} %iota_compare_fusion.2) | copy-start | bytes 1156
  41.9 1.9 %copy-start.6 = (pred[24]{0:T(512)(128)(4,1)S(1)}, pred[24]{0:T(512)(128)(4,1)}, u32[]{:S(2)}) copy-start(pred[24]{0:T(512)(128)(4,1)} %compare_and_fusion) | copy-start | bytes 76
  43.3 2.5 %copy-start.5 = (f32[1152]{0:T(1024)S(1)}, f32[1152]{0:T(1024)}, u32[]{:S(2)}) copy-start(f32[1152]{0:T(1024)} %param.22) | copy-start | bytes 13828
  45.5 2.7 %copy-start.10 = (s32[1,1,24]{2,1,0:T(1,128)S(1)}, s32[1,1,24]{2,1,0:T(1,128)}, u32[]{:S(2)}) copy-start(s32[1,1,24]{2,1,0:T(1,128)} %param.18) | copy-start | bytes 292
  45.6 2.8 %copy-start.9 = (s32[1,1,24]{2,1,0:T(1,128)S(1)}, s32[1,1,24]{2,1,0:T(1,128)}, u32[]{:S(2)}) copy-start(s32[1,1,24]{2,1,0:T(1,128)} %param.17) | copy-start | bytes 292
  50.4 42.7 %all-to-all-start = ((bf16[32,2,640]{2,1,0:T(2,128)(2,1)}), bf16[32,2,640]{2,1,0:T(2,128)(2,1)S(1)}, u32[]{:S(2)}, u32[]{:S(2)}) async-start(bf16[32,2,640]{2,1,0:T(2,128)(2,1)} %reshape.357), calls=%async_computation | async-start | bytes 163840 | tf_op jit(solution)/shard_map/all_to_all | solution.py:159
  118.2 14.7 %collective-permute-start = (bf16[32,1152]{1,0:T(8,128)(2,1)S(1)}, bf16[32,1152]{1,0:T(8,128)(2,1)S(1)}, u32[]{:S(2)}, u32[]{:S(2)}) collective-permute-start(bf16[32,1152]{1,0:T(8,128)(2,1)S(1)} %get-tuple-element.12), channel_id=1, source_target_pairs={{0,2},{1,3},{2,4},{3,5},{4,6},{5,7},{6,0},{7,1},{8,10},{9,11},{10,... | collective-permute-start | bytes 221192 | tf_op jit(solution)/shard_map/ppermute | solution.py:130
  121.0 11.9 %collective-permute-start.2 = (bf16[32,1152]{1,0:T(8,128)(2,1)S(1)}, bf16[32,1152]{1,0:T(8,128)(2,1)S(1)}, u32[]{:S(2)}, u32[]{:S(2)}) collective-permute-start(bf16[32,1152]{1,0:T(8,128)(2,1)S(1)} %get-tuple-element.13), channel_id=1, source_target_pairs={{0,6},{1,7},{2,0},{3,1},{4,2},{5,3},{6,4},{7,5},{8,14},{9,15},{10,... | collective-permute-start | bytes 221192 | tf_op jit(solution)/shard_map/ppermute | solution.py:130
  125.3 7.8 %collective-permute-start.1 = (bf16[32,1152]{1,0:T(8,128)(2,1)S(1)}, bf16[32,1152]{1,0:T(8,128)(2,1)S(1)}, u32[]{:S(2)}, u32[]{:S(2)}) collective-permute-start(bf16[32,1152]{1,0:T(8,128)(2,1)S(1)} %get-tuple-element.14), channel_id=1, source_target_pairs={{0,4},{1,5},{2,6},{3,7},{4,0},{5,1},{6,2},{7,3},{8,12},{9,13},{10,... | collective-permute-start | bytes 221192 | tf_op jit(solution)/shard_map/ppermute | solution.py:130
Sparse Core Ops, SparseCore 0:
  11.3 77.5 all-gather.3

commit v2 on v0

v2 whole, which is shorter than its diff:
```python
import jax
import jax.numpy as jnp
from jax import lax
from jax.experimental import pallas as pl
from jax.experimental.pallas import tpu as pltpu
from jax.sharding import PartitionSpec as P

CS = 2
XS = 4
LANES = 128
AUX = 128
BATCHES = 8
CHUNKS = 4
NT = (((1,), (1,)), ((), ()))
TN = (((0,), (0,)), ((), ()))


def layer_norm(values, gain):
    center = values - jnp.mean(values, axis=-1, keepdims=True)
    spread = jnp.mean(center * center, axis=-1, keepdims=True)
    return center * lax.rsqrt(spread + 1e-06) * gain


def unit_rows(values):
    return values * lax.rsqrt(jnp.sum(values * values, axis=-1, keepdims=True) + 1e-06)


def split_dot(values, right, dims=(((1,), (0,)), ((), ()))):
    high = values.astype(jnp.bfloat16)
    low = (values - high.astype(jnp.float32)).astype(jnp.bfloat16)
    return lax.dot_general(high, right, dims, preferred_element_type=jnp.float32) + lax.dot_general(
        low, right, dims, preferred_element_type=jnp.float32
    )


def as_half(mask):
    return jnp.where(mask, 1.0, 0.0).astype(jnp.bfloat16)


def iota(shape, dimension):
    return lax.broadcasted_iota(jnp.int32, shape, dimension)


def tower_kernel(
    temper_ref,
    count_hbm,
    target_hbm,
    label_hbm,
    caption_hbm,
    position_hbm,
    gain_in_hbm,
    gain_out_hbm,
    query_hbm,
    pair_hbm,
    out_hbm,
    head_hbm,
    wide_ref,
    count_ref,
    target_ref,
    label_ref,
    caption_ref,
    position_ref,
    gain_in_ref,
    gain_out_ref,
    query_ref,
    pair_ref,
    out_ref,
    head_ref,
    normed_ref,
    kv_ref,
    sems,
):
    number, length, width = caption_ref.shape
    tokens = number * length
    inner = query_hbm.shape[0]
    heads = temper_ref.shape[0]
    size = inner // heads
    lead = out_ref.shape[0] - inner
    slots = wide_ref.shape[0]
    pair_copy = pltpu.make_async_copy(pair_hbm, pair_ref, sems.at[0])
    query_copy = pltpu.make_async_copy(query_hbm, query_ref, sems.at[1])
    out_copy = pltpu.make_async_copy(out_hbm, out_ref.at[pl.ds(lead, inner), :], sems.at[2])
    head_copy = pltpu.make_async_copy(head_hbm, head_ref, sems.at[3])
    group = number // BATCHES
    position_copy = pltpu.make_async_copy(position_hbm, position_ref, sems.at[4])
    gain_in_copy = pltpu.make_async_copy(gain_in_hbm, gain_in_ref, sems.at[5])
    gain_out_copy = pltpu.make_async_copy(gain_out_hbm, gain_out_ref, sems.at[6])
    count_copy = pltpu.make_async_copy(count_hbm, count_ref, sems.at[7])
    target_copy = pltpu.make_async_copy(target_hbm, target_ref, sems.at[8])
    label_copy = pltpu.make_async_copy(label_hbm, label_ref, sems.at[9])
    caption_copies = [
        pltpu.make_async_copy(
            caption_hbm.at[pl.ds(batch * group, group)],
            caption_ref.at[pl.ds(batch * group, group)],
            sems.at[10 + batch],
        )
        for batch in range(BATCHES)
    ]
    position_copy.start()
    gain_in_copy.start()
    for copy in caption_copies:
        copy.start()
    pair_copy.start()
    count_copy.start()
    label_copy.start()
    query_copy.start()
    out_copy.start()
    target_copy.start()
    gain_out_copy.start()
    head_copy.start()
    out_ref[0:lead, :] = jnp.zeros((lead, width), jnp.bfloat16)

    position_copy.wait()
    gain_in_copy.wait()
    gain_in = gain_in_ref[...]
    position = position_ref[...].astype(jnp.float32)
    for batch in range(BATCHES):
        start = batch * group
        caption_copies[batch].wait()
        summed = caption_ref[start : start + group].astype(jnp.float32) + position[None]
        normed = layer_norm(summed, gain_in[None]).astype(jnp.bfloat16)
        normed_ref[start * length : (start + group) * length, :] = normed.reshape(
            group * length, width
        )

    count_copy.wait()
    label_copy.wait()
    count_row = jnp.maximum(count_ref[...], 1).astype(jnp.float32)
    label_row = label_ref[...].astype(jnp.float32)
    diagonal = iota((number, number), 0) == iota((number, number), 1)
    count_col = jnp.sum(jnp.where(diagonal, count_row, 0.0), axis=1, keepdims=True)
    label_col = jnp.sum(jnp.where(diagonal, label_row, 0.0), axis=1, keepdims=True)
    last_col = count_col.astype(jnp.int32) - 1
    pick = as_half(iota((number, tokens), 1) == iota((number, tokens), 0) * length + last_col)
    pick_position = as_half(iota((number, length), 1) == last_col)
    member = as_half(iota((number, tokens), 1) // length == iota((number, tokens), 0))
    owner = iota((tokens, number), 0) // length == iota((tokens, number), 1)
    spread = as_half(owner)
    count_tok = jnp.sum(jnp.where(owner, count_row, 0.0), axis=1, keepdims=True)
    place_tok = (iota((tokens, 1), 0) % length).astype(jnp.float32)
    first = iota((inner, LANES), 1) * size
    key_heads = as_half((iota((inner, LANES), 0) >= first) & (iota((inner, LANES), 0) < first + size))
    wide_inner = lead + inner
    first = iota((LANES, wide_inner), 0) * size + lead
    value_heads = as_half(
        (iota((LANES, wide_inner), 1) >= first) & (iota((LANES, wide_inner), 1) < first + size)
    )
    lane = iota((1, LANES), 1)
    temper = jnp.zeros((1, LANES), jnp.float32)
    for head in range(heads):
        temper = jnp.where(lane == head, temper_ref[head], temper)

    pair_copy.wait()
    step = width // 3
    for start in range(0, width, step):
        kv_ref[:, start : start + step] = jnp.dot(
            normed_ref[...], pair_ref[:, start : start + step], preferred_element_type=jnp.float32
        ).astype(jnp.bfloat16)
    normed_last = jnp.dot(pick, normed_ref[...], preferred_element_type=jnp.float32).astype(
        jnp.bfloat16
    )
    flat = caption_ref[...].reshape(tokens, width)
    summed_last = jnp.dot(pick, flat, preferred_element_type=jnp.float32) + jnp.dot(
        pick_position, position_ref[...], preferred_element_type=jnp.float32
    )
    query_copy.wait()
    queries = lax.dot_general(
        normed_last, query_ref[...], NT, preferred_element_type=jnp.float32
    )
    query_norm = temper * lax.rsqrt(split_dot(queries * queries, key_heads) + 1e-06)
    query_high = queries.astype(jnp.bfloat16)
    query_low = (queries - query_high.astype(jnp.float32)).astype(jnp.bfloat16)
    norm_high = query_norm.astype(jnp.bfloat16)
    norm_low = (query_norm - norm_high.astype(jnp.float32)).astype(jnp.bfloat16)

    attended = jnp.zeros((number, wide_inner), jnp.float32)
    parts = 2
    some = tokens // parts
    for part in range(parts):
        rows = slice(part * some, (part + 1) * some)
        spread_part = spread[rows]
        query_tok = jnp.dot(
            spread_part, query_high, preferred_element_type=jnp.float32
        ) + jnp.dot(spread_part, query_low, preferred_element_type=jnp.float32)
        norm_tok = jnp.dot(
            spread_part, norm_high, preferred_element_type=jnp.float32
        ) + jnp.dot(spread_part, norm_low, preferred_element_type=jnp.float32)
        keys = kv_ref[rows, 0:inner].astype(jnp.float32)
        products = split_dot(keys * query_tok, key_heads)
        key_square = split_dot(keys * keys, key_heads)
        scores = products * lax.rsqrt(key_square + 1e-06) * norm_tok
        raised = jnp.where(place_tok[rows] < count_tok[rows], jnp.exp(scores), 0.0)
        raised = raised.reshape(some // length, length, LANES)
        probs = raised / jnp.sum(raised, axis=1, keepdims=True)
        probs = probs.reshape(some, LANES).astype(jnp.bfloat16)
        probs_wide = jnp.dot(probs, value_heads, preferred_element_type=jnp.float32)
        values = kv_ref[rows, width - wide_inner : width].astype(jnp.float32)
        weighed = probs_wide * values
        high = weighed.astype(jnp.bfloat16)
        low = (weighed - high.astype(jnp.float32)).astype(jnp.bfloat16)
        attended = (
            attended
            + jnp.dot(member[:, rows], high, preferred_element_type=jnp.float32)
            + jnp.dot(member[:, rows], low, preferred_element_type=jnp.float32)
        )
    out_copy.wait()
    residual = summed_last + jnp.dot(
        attended.astype(jnp.bfloat16), out_ref[...], preferred_element_type=jnp.float32
    )
    gain_out_copy.wait()
    final = layer_norm(residual, gain_out_ref[...]).astype(jnp.bfloat16)
    head_copy.wait()
    pooled = unit_rows(jnp.dot(final, head_ref[...], preferred_element_type=jnp.float32)).astype(
        jnp.bfloat16
    )
    target_copy.wait()
    route = as_half(target_ref[...] == iota((slots, number), 0))
    wide_ref[:, 0:width] = jnp.dot(route, pooled, preferred_element_type=jnp.float32).astype(
        jnp.bfloat16
    )
    label_int = label_col.astype(jnp.int32)
    column = iota((number, AUX), 1)
    aux = jnp.where(
        column == 0,
        label_int // 32,
        jnp.where(column == 1, label_int % 32, jnp.where(column == 2, 1, 0)),
    )
    aux = aux.astype(jnp.float32).astype(jnp.bfloat16)
    wide_ref[:, width : width + AUX] = jnp.dot(
        route, aux, preferred_element_type=jnp.float32
    ).astype(jnp.bfloat16)


def encode(captions, counts, target, label, params, slots):
    position, gain_in, gain_out, query_proj, pair_proj, out_proj, head_proj, temper = params
    number, length, width = captions.shape
    inner = query_proj.shape[1]
    lead = -inner % LANES
    vmem = pl.BlockSpec()
    smem = pl.BlockSpec(memory_space=pltpu.SMEM)
    hbm = pl.BlockSpec(memory_space=pl.ANY)
    return pl.pallas_call(
        tower_kernel,
        out_shape=jax.ShapeDtypeStruct((slots, width + AUX), jnp.bfloat16),
        in_specs=[smem] + [hbm] * 11,
        out_specs=vmem,
        scratch_shapes=[
            pltpu.VMEM((1, number), jnp.int32),
            pltpu.VMEM((1, number), jnp.int32),
            pltpu.VMEM((1, number), jnp.int32),
            pltpu.VMEM((number, length, width), jnp.bfloat16),
            pltpu.VMEM((length, width), jnp.bfloat16),
            pltpu.VMEM((1, width), jnp.float32),
            pltpu.VMEM((1, width), jnp.float32),
            pltpu.VMEM((inner, width), jnp.bfloat16),
            pltpu.VMEM((width, width), jnp.bfloat16),
            pltpu.VMEM((lead + inner, width), jnp.bfloat16),
            pltpu.VMEM((width, width), jnp.bfloat16),
            pltpu.VMEM((number * length, width), jnp.bfloat16),
            pltpu.VMEM((number * length, width), jnp.bfloat16),
            pltpu.SemaphoreType.DMA((10 + BATCHES,)),
        ],
        compiler_params=pltpu.CompilerParams(vmem_limit_bytes=56 * 1024 * 1024),
        cost_estimate=pl.CostEstimate(
            flops=2 * number * length * width * width,
            bytes_accessed=10_000_000,
            transcendentals=number * length * LANES,
        ),
        name="tower",
    )(
        temper,
        counts.reshape(1, number),
        target.reshape(1, number),
        label.reshape(1, number),
        captions,
        position,
        gain_in.reshape(1, width),
        gain_out.reshape(1, width),
        query_proj.T,
        pair_proj,
        out_proj,
        head_proj,
    )


def slope_of(logits, same, live):
    sign = jnp.where(same, 1.0, -1.0)
    return -sign / (1.0 + jnp.exp(sign * logits)) * live


def inverse_norm(values):
    values = values.astype(jnp.float32)
    return lax.rsqrt(jnp.sum(values * values, axis=-1, keepdims=True) + 1e-06)


def aux_rows(aux):
    row, column = iota((8, AUX), 0), iota((8, AUX), 1)
    pick = jnp.where(
        row == 0,
        jnp.where(column == 0, 32.0, jnp.where(column == 1, 1.0, 0.0)),
        jnp.where((row == 1) & (column == 2), 1.0, 0.0),
    ).astype(jnp.bfloat16)
    rows = lax.dot_general(pick, aux, NT, preferred_element_type=jnp.float32)
    return rows[0:1], rows[1:2]


def text_kernel(scale_ref, offset_ref, wide_ref, images_hbm, grad_ref, images_ref, sems):
    total, width = images_hbm.shape
    number = wide_ref.shape[0]
    chunk = total // CHUNKS
    copies = [
        pltpu.make_async_copy(
            images_hbm.at[pl.ds(part * chunk, chunk)],
            images_ref.at[pl.ds(part * chunk, chunk)],
            sems.at[part],
        )
        for part in range(CHUNKS)
    ]
    for copy in copies:
        copy.start()
    scale = scale_ref[0]
    offset = offset_ref[0]
    text = wide_ref[:, 0:width]
    label, live = aux_rows(wide_ref[:, width:])
    grad = jnp.zeros((number, width), jnp.float32)
    for part in range(CHUNKS):
        copies[part].wait()
        images = images_ref[part * chunk : (part + 1) * chunk, :]
        inverse = inverse_norm(images)
        logits = lax.dot_general(images, text, NT, preferred_element_type=jnp.float32)
        logits = (scale * inverse) * logits + offset
        index = (part * chunk + iota((chunk, 1), 0)).astype(jnp.float32)
        slopes = (slope_of(logits, label == index, live) * inverse).astype(jnp.bfloat16)
        grad = grad + lax.dot_general(slopes, images, TN, preferred_element_type=jnp.float32)
    grad_ref[...] = scale * grad


def image_kernel(scale_ref, offset_ref, start_ref, images_ref, *rest):
    number, width = images_ref.shape
    wide_refs, grad_ref = rest[:-1], rest[-1]
    images = images_ref[...]
    scale = scale_ref[0]
    offset = offset_ref[0]
    inverse = scale * inverse_norm(images)
    index = (start_ref[0] + iota((number, 1), 0)).astype(jnp.float32)
    grad = jnp.zeros((number, width), jnp.float32)
    for wide_ref in wide_refs:
        text = wide_ref[:, 0:width]
        label, live = aux_rows(wide_ref[:, width:])
        logits = lax.dot_general(images, text, NT, preferred_element_type=jnp.float32)
        slopes = slope_of(inverse * logits + offset, label == index, live).astype(jnp.bfloat16)
        grad = grad + jnp.dot(slopes, text, preferred_element_type=jnp.float32)
    grad_ref[...] = scale * grad


def text_gradient(wide, image_all, scale, offset):
    total, width = image_all.shape
    number = wide.shape[0]
    smem = pl.BlockSpec(memory_space=pltpu.SMEM)
    vmem = pl.BlockSpec(memory_space=pltpu.VMEM)
    return pl.pallas_call(
        text_kernel,
        out_shape=jax.ShapeDtypeStruct((number, width), jnp.float32),
        in_specs=[smem, smem, vmem, pl.BlockSpec(memory_space=pl.ANY)],
        out_specs=vmem,
        scratch_shapes=[
            pltpu.VMEM((total, width), jnp.bfloat16),
            pltpu.SemaphoreType.DMA((CHUNKS,)),
        ],
        compiler_params=pltpu.CompilerParams(vmem_limit_bytes=56 * 1024 * 1024),
        cost_estimate=pl.CostEstimate(
            flops=4 * total * number * width,
            bytes_accessed=2 * total * width,
            transcendentals=total * number,
        ),
        name="text_gradient",
    )(scale, offset, wide, image_all)


def image_gradient(images, wides, start, scale, offset):
    number, width = images.shape
    texts = sum(wide.shape[0] for wide in wides)
    smem = pl.BlockSpec(memory_space=pltpu.SMEM)
    vmem = pl.BlockSpec(memory_space=pltpu.VMEM)
    return pl.pallas_call(
        image_kernel,
        out_shape=jax.ShapeDtypeStruct((number, width), jnp.float32),
        in_specs=[smem, smem, smem, vmem] + [vmem] * len(wides),
        out_specs=vmem,
        compiler_params=pltpu.CompilerParams(vmem_limit_bytes=24 * 1024 * 1024),
        cost_estimate=pl.CostEstimate(
            flops=4 * texts * number * width,
            bytes_accessed=2 * texts * width,
            transcendentals=texts * number,
        ),
        name="image_gradient",
    )(scale, offset, start, images, *wides)


def loss_grads(wide, images, image_all, scale, offset):
    blocks = lax.axis_size("blk")
    zs = blocks // (XS * CS)
    count = images.shape[0]
    place = lambda z, x, c: (z * XS + x) * CS + c
    lines = [[place(z, x, c) for z in range(zs)] for x in range(XS) for c in range(CS)]
    rings = [[place(z, x, c) for x in range(XS)] for z in range(zs) for c in range(CS)]
    swap = [(place(z, x, c), place(z, x, 1 - c)) for z in range(zs) for x in range(XS) for c in range(CS)]
    first = lax.all_gather(wide, "blk", axis=0, tiled=True, axis_index_groups=lines)
    rows = first.shape[0] // 2
    firsts = [
        lax.all_gather(part, "blk", axis=0, tiled=True, axis_index_groups=rings)
        for part in (first[:rows], first[rows:])
    ]
    seconds = [lax.ppermute(part, "blk", swap) for part in firsts]
    text_sum = text_gradient(wide, image_all, scale, offset)
    start = (lax.axis_index("blk") * count).reshape(1)
    image_sum = image_gradient(images, firsts + seconds, start, scale, offset)
    return text_sum, image_sum


def local(
    captions,
    lengths,
    destination,
    labels,
    images,
    position,
    gain_in,
    gain_out,
    query_proj,
    pair_proj,
    out_proj,
    head_proj,
    temper,
    logit_scale,
    logit_bias,
):
    slots = lax.axis_size("dp")
    params = (position, gain_in, gain_out, query_proj, pair_proj, out_proj, head_proj, temper)
    own = images[0, 0]
    image_all = lax.all_gather(own, "blk", axis=0, tiled=True)
    sent = encode(captions[0, 0], lengths[0, 0], destination[0, 0], labels[0, 0], params, slots)
    wide = lax.all_to_all(sent, "dp", split_axis=0, concat_axis=0, tiled=True)
    text_sum, image_sum = loss_grads(wide, own, image_all, logit_scale, logit_bias)
    return text_sum[None, None], image_sum[None, None]


def solution(mesh):
    return jax.shard_map(
        local,
        mesh=mesh,
        in_specs=(
            P("dp", "blk", None, None, None),
            P("dp", "blk", None),
            P("dp", "blk", None),
            P("dp", "blk", None),
            P("dp", "blk", None, None),
            P(),
            P(),
            P(),
            P(),
            P(),
            P(),
            P(),
            P(),
            P(),
            P(),
        ),
        out_specs=(P("dp", "blk", None, None), P("dp", "blk", None, None)),
        check_vma=False,
    )
```

time: 234 us -> 131 us (0.56)
  waiting for transfers between devices: 81.3 us -> 0.69 us
  blocking collectives: 43.3 us -> 78 us
  starting transfers between devices: 40.2 us -> 12.9 us
  matrix products: 21.5 us -> 0 us
  Pallas kernels: 0 us -> 17.7 us
  other arithmetic: 13.9 us -> 1.55 us
  local copies, waits for them, and re-layouts: 16.2 us -> 3.87 us
    all_to_all x3 -> x0, waiting for transfers between devices: 56 us -> none  [the longest x1 31.5 us: local(): lax.all_to_all(sent, 'dp', split_axis=0, concat_axis=0, tiled=True)]
    unnamed x1 -> x0, blocking collectives: 43.3 us -> none
    all_to_all x0 -> x1, blocking collectives: none -> 40.8 us  [local(): wide = lax.all_to_all(sent, 'dp', split_axis=0, concat_axis=0, tiled=True)]
    all_to_all x3 -> x0, starting transfers between devices: 40.1 us -> none  [the longest x1 24.9 us: local(): lax.all_to_all(sent_count, 'dp', split_axis=0, concat_axis=0, tiled=True)]
    all_gather x0 -> x3, blocking collectives: none -> 37.2 us  [the longest x2 23.1 us: loss_grads(): lax.all_gather(part, 'blk', axis=0, tiled=True, axis_index_groups=rings)]
    all_gather x2 -> x1, waiting for transfers between devices: 25.2 us -> 0.01 us  [local(): image_all = lax.all_gather(own, 'blk', axis=0, tiled=True)]
    dot_general x9 -> x0, matrix products: 21.5 us -> none  [the longest x1 4.35 us: local(): text_sum = jnp.dot(slopes, piece, preferred_element_type=jnp.float32)]
    pallas_call x0 -> x3, Pallas kernels: none -> 17.7 us  [the longest x1 10 us: encode(): pl.pallas_call(tower_kernel, out_shape=jax.ShapeDtypeStruct((slots, width...]
  transfers between devices with their start and end apart: 5 -> 3, of which waited for: 4 -> 0; matrix products, arithmetic and copies ran while one was open for 20% -> 4% of each run, Pallas kernels for 0% -> 10%
where the time goes in v2:
time: 131 us; the launch traced here: 130 us
  blocking collectives  78 us (60%)
  Pallas kernels  17.7 us (14%)
  between operations  15.4 us (12%)
  starting transfers between devices  12.9 us (10%)
  local copies, waits for them, and re-layouts  3.87 us (3%)
  other arithmetic  1.55 us (1%)
    all_to_all x1, blocking collectives, local(): wide = lax.all_to_all(sent, 'dp', split_axis=0, concat_axis=0, tiled=True)  40.8 us
    all_gather x2, blocking collectives, loss_grads(): lax.all_gather(part, 'blk', axis=0, tiled=True, axis_index_groups=rings)  23.1 us
    all_gather x1, blocking collectives, loss_grads(): lax.all_gather(wide, 'blk', axis=0, tiled=True, axis_index_groups=lines)  14.1 us
    ppermute x2, starting transfers between devices, loss_grads(): seconds = [lax.ppermute(part, 'blk', swap) for part in firsts]  12.8 us
    pallas_call x1, Pallas kernels, encode(): pl.pallas_call(tower_kernel, out_shape=jax.ShapeDtypeStruct((slots, width...  10 us
    pallas_call x1, Pallas kernels, text_gradient(): pl.pallas_call(text_kernel, out_shape=jax.ShapeDtypeStruct((number, width...  5.12 us
  transfers between devices with their start and end apart: 3, of which 0 were waited for; matrix products, arithmetic and copies ran while one was open for 4% of the time, Pallas kernels for 10%

profile of v2, /device:TPU:1, one launch (start us, length us, event | category | flops | bytes accessed | tf_op | source)
XLA Modules:
  0.0 130.1 jit_solution(1542716639495950807)
XLA Ops:
  7.2 0.0 all-gather.6.cloned.1.call-start
  7.2 0.7 all-gather.6.cloned.1.call-update
  7.9 1.3 reshape.15.gain_in_hbm
  9.2 1.3 reshape.16.gain_out_hbm
  10.5 10.0 %tower.1 = bf16[32,1280]{1,0:T(8,128)(2,1)} custom-call(f32[8]{0:T(128)} %temper_ref.1, s32[1,24]{1,0:T(1,128)} %bitcast.28, s32[1,24]{1,0:T(1,128)} %bitcast.29, s32[1,24]{1,0:T(1,128)} %bitcast.30, bf16[24,16,1152]{2,1,0:T(8,128)(2,1)} %bitcast.23, bf16[16,1152]{1,0:T(8,128)(2,1)} %position_hbm.1, f32[1,1152]{1,0:T(1,128)} %reshape.15.gain_in_hbm, ...), custom_call_target="tpu_custom_call" | custom-call | flops 1019215872 | bytes 10000000 | tf_op jit(solution)/shard_map/tower/pallas_call | solution.py:242
  20.5 0.0 copy-start
  20.5 0.5 broadcast
  21.0 1.5 %reduce = bf16[32,1280]{1,0:T(8,128)(2,1)S(1)} reduce(bf16[32,1,1280]{2,0,1:T(8,128)(2,1)} %bitcast.24, bf16[]{:T(256)} %broadcast), dimensions={1}, to_apply=%copy.19.reduce_sub_computation | reduce | bytes 163842 | tf_op jit(solution)/shard_map/all_to_all | solution.py:443
  22.6 40.8 %all_to_all.11 = bf16[32,2,640]{2,1,0:T(2,128)(2,1)S(1)} all-to-all(bf16[32,2,640]{2,1,0:T(2,128)(2,1)S(1)} %reshape.24), channel_id=1, replica_groups=mesh['dp'=32,'blk'=32] {'dp'}, dimensions={0} | all-to-all | bytes 163840 | tf_op jit(solution)/shard_map/all_to_all | solution.py:443
  63.4 0.1 reshape.25
  63.5 14.1 %all-gather.1 = bf16[128,1,1280]{2,0,1:T(8,128)(2,1)S(1)} all-gather(bf16[32,1,1280]{2,0,1:T(8,128)(2,1)S(1)} %copy.21), channel_id=3, replica_groups={{0,8,16,24},{1,9,17,25},{2,10,18,26},{3,11,19,27},{4,12,20,28},{5,13,21..., dimensions={0}, use_global_device_ids=true | all-gather | bytes 409600 | tf_op jit(solution)/shard_map/all_gather | solution.py:408
  77.7 11.7 %all-gather.2 = bf16[256,1,1280]{2,0,1:T(8,128)(2,1)S(1)} all-gather(bf16[64,1,1280]{2,0,1:T(8,128)(2,1)S(1)} %get-tuple-element.3), channel_id=4, replica_groups={{0,2,4,6},{1,3,5,7},{8,10,12,14},{9,11,13,15},{16,18,20,22},{17,19,21,2..., dimensions={0}, use_global_device_ids=true | all-gather | bytes 819200 | tf_op jit(solution)/shard_map/all_gather | solution.py:411
  89.3 8.8 %collective-permute-start = (bf16[256,1280]{1,0:T(8,128)(2,1)S(1)}, bf16[256,1280]{1,0:T(8,128)(2,1)S(1)}, u32[]{:S(2)}, u32[]{:S(2)}) collective-permute-start(bf16[256,1280]{1,0:T(8,128)(2,1)S(1)} %bitcast.16), channel_id=1, source_target_pairs={{0,1},{1,0},{2,3},{3,2},{4,5},{5,4},{6,7},{7,6},{8,9},{9,8},{10,11... | collective-permute-start | bytes 1966088 | tf_op jit(solution)/shard_map/ppermute | solution.py:414
  98.2 11.4 %all-gather.3 = bf16[256,1,1280]{2,0,1:T(8,128)(2,1)S(1)} all-gather(bf16[64,1,1280]{2,0,1:T(8,128)(2,1)S(1)} %get-tuple-element.2), channel_id=5, replica_groups={{0,2,4,6},{1,3,5,7},{8,10,12,14},{9,11,13,15},{16,18,20,22},{17,19,21,2..., dimensions={0}, use_global_device_ids=true | all-gather | bytes 819200 | tf_op jit(solution)/shard_map/all_gather | solution.py:411
  109.6 4.0 %collective-permute-start.1 = (bf16[256,1280]{1,0:T(8,128)(2,1)S(1)}, bf16[256,1280]{1,0:T(8,128)(2,1)S(1)}, u32[]{:S(2)}, u32[]{:S(2)}) collective-permute-start(bf16[256,1280]{1,0:T(8,128)(2,1)S(1)} %bitcast.18), channel_id=1, source_target_pairs={{0,1},{1,0},{2,3},{3,2},{4,5},{5,4},{6,7},{7,6},{8,9},{9,8},{10,11... | collective-permute-start | bytes 1966088 | tf_op jit(solution)/shard_map/ppermute | solution.py:414
  114.8 0.6 copy.23
  115.5 0.0 collective-permute-done.rest_2_
  115.5 0.0 collective-permute-done.1.rest_3_
  115.5 0.0 copy-done
  115.5 2.6 %image_gradient.1 = f32[32,1152]{1,0:T(8,128)} custom-call(f32[1]{0:T(128)S(6)} %copy.25.scale_ref, f32[1]{0:T(128)S(6)} %copy.26.offset_ref, s32[1]{0:T(128)} %bitcast.8.start_ref, bf16[32,1152]{1,0:T(8,128)(2,1)S(1)} %bitcast.20, bf16[256,1280]{1,0:T(8,128)(2,1)S(1)} %bitcast.17, bf16[256,1280]{1,0:T(8,128)(2,1)S(1)} %bitcast.19, ...), custom_call_target="tpu_custom_call" | custom-call | flops 150994944 | bytes 2359296 | tf_op jit(solution)/shard_map/image_gradient/pallas_call | solution.py:385
  118.1 0.0 all-gather.6.cloned.1.call-done
  118.1 5.1 %text_gradient.1 = f32[32,1152]{1,0:T(8,128)} custom-call(f32[1]{0:T(128)S(6)} %copy.25.scale_ref, f32[1]{0:T(128)S(6)} %copy.26.offset_ref, bf16[32,1280]{1,0:T(8,128)(2,1)} %bitcast.25, bf16[1024,1152]{1,0:T(8,128)(2,1)} %bitcast.21), custom_call_target="tpu_custom_call" | custom-call | flops 150994944 | bytes 2359296 | tf_op jit(solution)/shard_map/text_gradient/pallas_call | solution.py:361
  (3 shorter events, 0.1 us)
Async XLA Ops:
  7.2 110.9 %all-gather.6.cloned.1.call-start = ((), (), s32[]{:S(2)}) async-start(), calls=%async_computation.1 | async-start | bytes 2433024 | tf_op jit(solution)/shard_map/all_gather | solution.py:441
  20.5 95.0 %copy-start = (bf16[1,1,32,1152]{3,2,1,0:T(8,128)(2,1)S(1)}, bf16[1,1,32,1152]{3,2,1,0:T(8,128)(2,1)}, u32[]{:S(2)}) copy-start(bf16[1,1,32,1152]{3,2,1,0:T(8,128)(2,1)} %param.19) | copy-start | bytes 221188
  89.3 26.2 %collective-permute-start = (bf16[256,1280]{1,0:T(8,128)(2,1)S(1)}, bf16[256,1280]{1,0:T(8,128)(2,1)S(1)}, u32[]{:S(2)}, u32[]{:S(2)}) collective-permute-start(bf16[256,1280]{1,0:T(8,128)(2,1)S(1)} %bitcast.16), channel_id=1, source_target_pairs={{0,1},{1,0},{2,3},{3,2},{4,5},{5,4},{6,7},{7,6},{8,9},{9,8},{10,11... | collective-permute-start | bytes 1966088 | tf_op jit(solution)/shard_map/ppermute | solution.py:414
  109.6 5.9 %collective-permute-start.1 = (bf16[256,1280]{1,0:T(8,128)(2,1)S(1)}, bf16[256,1280]{1,0:T(8,128)(2,1)S(1)}, u32[]{:S(2)}, u32[]{:S(2)}) collective-permute-start(bf16[256,1280]{1,0:T(8,128)(2,1)S(1)} %bitcast.18), channel_id=1, source_target_pairs={{0,1},{1,0},{2,3},{3,2},{4,5},{5,4},{6,7},{7,6},{8,9},{9,8},{10,11... | collective-permute-start | bytes 1966088 | tf_op jit(solution)/shard_map/ppermute | solution.py:414
Sparse Core Ops, SparseCore 0:
  10.7 79.2 all-gather.5

commit v3 on v2

--- a/solution.py
+++ b/solution.py
@@ -112,7 +112,7 @@
 
     position_copy.wait()
     gain_in_copy.wait()
-    gain_in = gain_in_ref[...]
+    gain_in = gain_in_ref[...].reshape(1, width)
     position = position_ref[...].astype(jnp.float32)
     for batch in range(BATCHES):
         start = batch * group
@@ -208,7 +208,7 @@
         attended.astype(jnp.bfloat16), out_ref[...], preferred_element_type=jnp.float32
     )
     gain_out_copy.wait()
-    final = layer_norm(residual, gain_out_ref[...]).astype(jnp.bfloat16)
+    final = layer_norm(residual, gain_out_ref[...].reshape(1, width)).astype(jnp.bfloat16)
     head_copy.wait()
     pooled = unit_rows(jnp.dot(final, head_ref[...], preferred_element_type=jnp.float32)).astype(
         jnp.bfloat16
@@ -250,8 +250,8 @@
             pltpu.VMEM((1, number), jnp.int32),
             pltpu.VMEM((number, length, width), jnp.bfloat16),
             pltpu.VMEM((length, width), jnp.bfloat16),
-            pltpu.VMEM((1, width), jnp.float32),
-            pltpu.VMEM((1, width), jnp.float32),
+            pltpu.VMEM((width,), jnp.float32),
+            pltpu.VMEM((width,), jnp.float32),
             pltpu.VMEM((inner, width), jnp.bfloat16),
             pltpu.VMEM((width, width), jnp.bfloat16),
             pltpu.VMEM((lead + inner, width), jnp.bfloat16),
@@ -274,8 +274,8 @@
         label.reshape(1, number),
         captions,
         position,
-        gain_in.reshape(1, width),
-        gain_out.reshape(1, width),
+        gain_in,
+        gain_out,
         query_proj.T,
         pair_proj,
         out_proj,
@@ -397,6 +397,15 @@
     )(scale, offset, start, images, *wides)
 
 
+def spread_to(rows, groups):
+    members = len(groups[0])
+    blocks = jnp.broadcast_to(rows[None], (members,) + rows.shape)
+    got = lax.all_to_all(
+        blocks, "blk", split_axis=0, concat_axis=0, tiled=True, axis_index_groups=groups
+    )
+    return got.reshape(members * rows.shape[0], rows.shape[1])
+
+
 def loss_grads(wide, images, image_all, scale, offset):
     blocks = lax.axis_size("blk")
     zs = blocks // (XS * CS)
@@ -404,17 +413,15 @@
     place = lambda z, x, c: (z * XS + x) * CS + c
     lines = [[place(z, x, c) for z in range(zs)] for x in range(XS) for c in range(CS)]
     rings = [[place(z, x, c) for x in range(XS)] for z in range(zs) for c in range(CS)]
-    swap = [(place(z, x, c), place(z, x, 1 - c)) for z in range(zs) for x in range(XS) for c in range(CS)]
-    first = lax.all_gather(wide, "blk", axis=0, tiled=True, axis_index_groups=lines)
-    rows = first.shape[0] // 2
-    firsts = [
-        lax.all_gather(part, "blk", axis=0, tiled=True, axis_index_groups=rings)
-        for part in (first[:rows], first[rows:])
+    swap = [
+        (place(z, x, c), place(z, x, 1 - c)) for z in range(zs) for x in range(XS) for c in range(CS)
     ]
-    seconds = [lax.ppermute(part, "blk", swap) for part in firsts]
+    start = (lax.axis_index("blk") * count).reshape(1)
+    first = spread_to(spread_to(wide, lines), rings)
+    second = lax.ppermute(first, "blk", swap)
     text_sum = text_gradient(wide, image_all, scale, offset)
-    start = (lax.axis_index("blk") * count).reshape(1)
-    image_sum = image_gradient(images, firsts + seconds, start, scale, offset)
+    second, text_sum = lax.optimization_barrier((second, text_sum))
+    image_sum = image_gradient(images, [first, second], start, scale, offset)
     return text_sum, image_sum
 
 
@@ -440,7 +447,9 @@
     own = images[0, 0]
     image_all = lax.all_gather(own, "blk", axis=0, tiled=True)
     sent = encode(captions[0, 0], lengths[0, 0], destination[0, 0], labels[0, 0], params, slots)
-    wide = lax.all_to_all(sent, "dp", split_axis=0, concat_axis=0, tiled=True)
+    halves = sent.reshape(slots, 2, sent.shape[1] // 2)
+    wide = lax.all_to_all(halves, "dp", split_axis=0, concat_axis=0, tiled=True)
+    wide = wide.reshape(sent.shape)
     text_sum, image_sum = loss_grads(wide, own, image_all, logit_scale, logit_bias)
     return text_sum[None, None], image_sum[None, None]
 

time: 131 us -> 115 us (0.88)
  starting transfers between devices: 12.9 us -> 5.32 us
  local copies, waits for them, and re-layouts: 3.87 us -> 1.04 us
  blocking collectives: 78 us -> 75.2 us
  other arithmetic: 1.55 us -> 0 us
    all_gather x3 -> x0, blocking collectives: 37.2 us -> none  [the longest x2 23.1 us: loss_grads(): lax.all_gather(part, 'blk', axis=0, tiled=True, axis_index_groups=rings)]
    all_to_all x1 -> x3, blocking collectives: 40.8 us -> 75.2 us  [the longest x1 42.3 us: local(): wide = lax.all_to_all(halves, 'dp', split_axis=0, concat_axis=0, tiled=True)]
    ppermute x2 -> x1, starting transfers between devices: 12.8 us -> 5.29 us  [loss_grads(): second = lax.ppermute(first, 'blk', swap)]
    reshape x2 -> x1, local copies, waits for them, and re-layouts: 2.59 us -> 0.91 us  [local(): halves = sent.reshape(slots, 2, sent.shape[1] // 2)]
    all_to_all x1 -> x0, other arithmetic: 1.55 us -> none  [local(): wide = lax.all_to_all(sent, 'dp', split_axis=0, concat_axis=0, tiled=True)]
  transfers between devices with their start and end apart: 3 -> 2, of which waited for: 0 -> 0; matrix products, arithmetic and copies ran while one was open for 4% -> 1% of each run, Pallas kernels for 10% -> 13%
where the time goes in v3:
time: 115 us
  blocking collectives  75.2 us (65%)
  Pallas kernels  17.2 us (15%)
  between operations  15.4 us (13%)
  starting transfers between devices  5.32 us (5%)
    all_to_all x1, blocking collectives, local(): wide = lax.all_to_all(halves, 'dp', split_axis=0, concat_axis=0, tiled=True)  42.3 us
    all_to_all x2, blocking collectives, spread_to(): lax.all_to_all(blocks, 'blk', split_axis=0, concat_axis=0, tiled=True, ax...  32.9 us
    pallas_call x1, Pallas kernels, encode(): pl.pallas_call(tower_kernel, out_shape=jax.ShapeDtypeStruct((slots, width...  10 us
    ppermute x1, starting transfers between devices, loss_grads(): second = lax.ppermute(first, 'blk', swap)  5.29 us
    pallas_call x1, Pallas kernels, text_gradient(): pl.pallas_call(text_kernel, out_shape=jax.ShapeDtypeStruct((number, width...  5.13 us
  transfers between devices with their start and end apart: 2, of which 0 were waited for; matrix products, arithmetic and copies ran while one was open for 1% of the time, Pallas kernels for 13%

profile of v3, /device:TPU:1, one launch (start us, length us, event | category | flops | bytes accessed | tf_op | source)
XLA Modules:
  0.0 114.9 jit_solution(17986680207412678155)
XLA Ops:
  7.2 0.0 all-gather.3.cloned.1.call-start
  7.2 0.7 all-gather.3.cloned.1.call-update
  7.9 10.0 %tower.1 = bf16[32,1280]{1,0:T(8,128)(2,1)} custom-call(f32[8]{0:T(128)} %temper_ref.1, s32[1,24]{1,0:T(1,128)} %bitcast.26, s32[1,24]{1,0:T(1,128)} %bitcast.27, s32[1,24]{1,0:T(1,128)} %bitcast.28, bf16[24,16,1152]{2,1,0:T(8,128)(2,1)} %bitcast.20, bf16[16,1152]{1,0:T(8,128)(2,1)} %position_hbm.1, f32[1152]{0:T(1024)} %gain_in_hbm.1, f32[1152]{0:T(1024)} %gain_out_hbm.1, ...), custom_call_target="tpu_custom_call" | custom-call | flops 1019215872 | bytes 10000000 | tf_op jit(solution)/shard_map/tower/pallas_call | solution.py:242
  17.9 0.9 reshape.16
  18.8 42.3 %all_to_all.15 = bf16[32,2,640]{2,1,0:T(2,128)(2,1)S(1)} all-to-all(bf16[32,2,640]{2,1,0:T(2,128)(2,1)S(1)} %reshape.16), channel_id=1, replica_groups=mesh['dp'=32,'blk'=32] {'dp'}, dimensions={0} | all-to-all | bytes 163840 | tf_op jit(solution)/shard_map/all_to_all | solution.py:451
  61.2 0.0 copy-start.1
  61.2 13.2 %all_to_all.16 = bf16[4,32,1280]{2,1,0:T(8,128)(2,1)S(1)} all-to-all(bf16[4,32,1280]{2,1,0:T(8,128)(2,1)S(1)} %broadcast_in_dim.21), channel_id=1, replica_groups={{0,8,16,24},{1,9,17,25},{2,10,18,26},{3,11,19,27},{4,12,20,28},{5,13,21..., dimensions={0} | all-to-all | bytes 655360 | tf_op jit(solution)/shard_map/all_to_all | solution.py:403
  74.4 0.1 broadcast_in_dim.23
  74.5 0.0 copy-done.1
  74.5 19.7 %all_to_all.17 = bf16[4,128,1280]{2,1,0:T(8,128)(2,1)S(1)} all-to-all(bf16[4,128,1280]{2,1,0:T(8,128)(2,1)S(1)} %broadcast_in_dim.23), channel_id=1, replica_groups={{0,2,4,6},{1,3,5,7},{8,10,12,14},{9,11,13,15},{16,18,20,22},{17,19,21,2..., dimensions={0} | all-to-all | bytes 2621440 | tf_op jit(solution)/shard_map/all_to_all | solution.py:403
  94.2 0.0 copy-start
  94.2 5.3 %collective-permute-start = (bf16[512,1280]{1,0:T(8,128)(2,1)S(1)}, bf16[512,1280]{1,0:T(8,128)(2,1)S(1)}, u32[]{:S(2)}, u32[]{:S(2)}) collective-permute-start(bf16[512,1280]{1,0:T(8,128)(2,1)S(1)} %bitcast.14), channel_id=1, source_target_pairs={{0,1},{1,0},{2,3},{3,2},{4,5},{5,4},{6,7},{7,6},{8,9},{9,8},{10,11... | collective-permute-start | bytes 3932168 | tf_op jit(solution)/shard_map/ppermute | solution.py:421
  100.8 0.0 all-gather.3.cloned.1.call-done
  100.8 5.1 %text_gradient.1 = f32[32,1152]{1,0:T(8,128)} custom-call(f32[1]{0:T(128)S(6)} %copy.18.scale_ref, f32[1]{0:T(128)S(6)} %copy.19.offset_ref, bf16[32,1280]{1,0:T(8,128)(2,1)} %bitcast.22, bf16[1024,1152]{1,0:T(8,128)(2,1)} %bitcast.17), custom_call_target="tpu_custom_call" | custom-call | flops 150994944 | bytes 2359296 | tf_op jit(solution)/shard_map/text_gradient/pallas_call | solution.py:361
  105.9 0.0 collective-permute-done.rest_1_
  106.0 0.0 copy-done
  106.0 2.0 %image_gradient.1 = f32[32,1152]{1,0:T(8,128)} custom-call(f32[1]{0:T(128)S(6)} %copy.18.scale_ref, f32[1]{0:T(128)S(6)} %copy.19.offset_ref, s32[1]{0:T(128)} %bitcast.9.start_ref, bf16[32,1152]{1,0:T(8,128)(2,1)S(1)} %bitcast.16, bf16[512,1280]{1,0:T(8,128)(2,1)S(1)} %bitcast.15, bf16[512,1280]{1,0:T(8,128)(2,1)S(1)} %collective-permute-done.rest_1_), custom_call_target="tpu_custom_call" | custom-call | flops 150994944 | bytes 2359296 | tf_op jit(solution)/shard_map/image_gradient/pallas_call | solution.py:385
  (2 shorter events, 0.0 us)
Async XLA Ops:
  7.2 93.6 %all-gather.3.cloned.1.call-start = ((), (), s32[]{:S(2)}) async-start(), calls=%async_computation.3 | async-start | bytes 2433024 | tf_op jit(solution)/shard_map/all_gather | solution.py:448
  61.2 13.3 %copy-start.1 = (bf16[4,8,2,640]{3,1,2,0:T(8,128)(2,1)}, bf16[4,8,2,640]{3,1,2,0:T(8,128)(2,1)S(1)}, u32[]{:S(2)}) copy-start(bf16[4,8,2,640]{3,1,2,0:T(8,128)(2,1)S(1)} %copy.17) | copy-start | bytes 245764
  94.2 11.8 %copy-start = (bf16[1,1,32,1152]{3,2,1,0:T(8,128)(2,1)S(1)}, bf16[1,1,32,1152]{3,2,1,0:T(8,128)(2,1)}, u32[]{:S(2)}) copy-start(bf16[1,1,32,1152]{3,2,1,0:T(8,128)(2,1)} %param.19) | copy-start | bytes 221188
  94.2 11.8 %collective-permute-start = (bf16[512,1280]{1,0:T(8,128)(2,1)S(1)}, bf16[512,1280]{1,0:T(8,128)(2,1)S(1)}, u32[]{:S(2)}, u32[]{:S(2)}) collective-permute-start(bf16[512,1280]{1,0:T(8,128)(2,1)S(1)} %bitcast.14), channel_id=1, source_target_pairs={{0,1},{1,0},{2,3},{3,2},{4,5},{5,4},{6,7},{7,6},{8,9},{9,8},{10,11... | collective-permute-start | bytes 3932168 | tf_op jit(solution)/shard_map/ppermute | solution.py:421
Sparse Core Ops, SparseCore 0:
  10.7 80.9 all-gather.2

commit v4 on v3

--- a/solution.py
+++ b/solution.py
@@ -10,7 +10,6 @@
 LANES = 128
 AUX = 128
 BATCHES = 8
-CHUNKS = 4
 NT = (((1,), (1,)), ((), ()))
 TN = (((0,), (0,)), ((), ()))
 
@@ -304,125 +303,109 @@
     return rows[0:1], rows[1:2]
 
 
-def text_kernel(scale_ref, offset_ref, wide_ref, images_hbm, grad_ref, images_ref, sems):
-    total, width = images_hbm.shape
-    number = wide_ref.shape[0]
-    chunk = total // CHUNKS
-    copies = [
-        pltpu.make_async_copy(
-            images_hbm.at[pl.ds(part * chunk, chunk)],
-            images_ref.at[pl.ds(part * chunk, chunk)],
-            sems.at[part],
-        )
-        for part in range(CHUNKS)
-    ]
-    for copy in copies:
-        copy.start()
-    scale = scale_ref[0]
-    offset = offset_ref[0]
+def text_parts_kernel(scale_ref, offset_ref, start_ref, wide_ref, images_ref, parts_ref):
+    number, width = images_ref.shape
+    images = images_ref[...]
     text = wide_ref[:, 0:width]
     label, live = aux_rows(wide_ref[:, width:])
-    grad = jnp.zeros((number, width), jnp.float32)
-    for part in range(CHUNKS):
-        copies[part].wait()
-        images = images_ref[part * chunk : (part + 1) * chunk, :]
-        inverse = inverse_norm(images)
+    inverse = inverse_norm(images)
+    logits = lax.dot_general(images, text, NT, preferred_element_type=jnp.float32)
+    logits = (scale_ref[0] * inverse) * logits + offset_ref[0]
+    index = (start_ref[0] + iota((number, 1), 0)).astype(jnp.float32)
+    slopes = (slope_of(logits, label == index, live) * inverse).astype(jnp.bfloat16)
+    parts_ref[...] = lax.dot_general(
+        slopes, images, TN, preferred_element_type=jnp.float32
+    ).astype(jnp.bfloat16)
+
+
+def image_parts_kernel(scale_ref, offset_ref, start_ref, core_ref, wide_ref, images_ref, parts_ref):
+    number, width = parts_ref.shape
+    count = number // XS
+    text = wide_ref[:, 0:width]
+    label, live = aux_rows(wide_ref[:, width:])
+    for x in range(XS):
+        row = pl.multiple_of((x * CS + core_ref[0]) * count, count)
+        images = images_ref[pl.ds(row, count), :]
         logits = lax.dot_general(images, text, NT, preferred_element_type=jnp.float32)
-        logits = (scale * inverse) * logits + offset
-        index = (part * chunk + iota((chunk, 1), 0)).astype(jnp.float32)
-        slopes = (slope_of(logits, label == index, live) * inverse).astype(jnp.bfloat16)
-        grad = grad + lax.dot_general(slopes, images, TN, preferred_element_type=jnp.float32)
-    grad_ref[...] = scale * grad
-
-
-def image_kernel(scale_ref, offset_ref, start_ref, images_ref, *rest):
-    number, width = images_ref.shape
-    wide_refs, grad_ref = rest[:-1], rest[-1]
-    images = images_ref[...]
-    scale = scale_ref[0]
-    offset = offset_ref[0]
-    inverse = scale * inverse_norm(images)
-    index = (start_ref[0] + iota((number, 1), 0)).astype(jnp.float32)
-    grad = jnp.zeros((number, width), jnp.float32)
-    for wide_ref in wide_refs:
-        text = wide_ref[:, 0:width]
-        label, live = aux_rows(wide_ref[:, width:])
-        logits = lax.dot_general(images, text, NT, preferred_element_type=jnp.float32)
-        slopes = slope_of(inverse * logits + offset, label == index, live).astype(jnp.bfloat16)
-        grad = grad + jnp.dot(slopes, text, preferred_element_type=jnp.float32)
-    grad_ref[...] = scale * grad
-
-
-def text_gradient(wide, image_all, scale, offset):
-    total, width = image_all.shape
-    number = wide.shape[0]
+        logits = (scale_ref[0] * inverse_norm(images)) * logits + offset_ref[0]
+        index = (start_ref[0] + row + iota((count, 1), 0)).astype(jnp.float32)
+        slopes = slope_of(logits, label == index, live).astype(jnp.bfloat16)
+        parts_ref[x * count : (x + 1) * count, :] = jnp.dot(
+            slopes, text, preferred_element_type=jnp.float32
+        ).astype(jnp.bfloat16)
+
+
+def call_parts(kernel, scalars, wide, images, rows, name):
+    number, width = images.shape
     smem = pl.BlockSpec(memory_space=pltpu.SMEM)
     vmem = pl.BlockSpec(memory_space=pltpu.VMEM)
     return pl.pallas_call(
-        text_kernel,
-        out_shape=jax.ShapeDtypeStruct((number, width), jnp.float32),
-        in_specs=[smem, smem, vmem, pl.BlockSpec(memory_space=pl.ANY)],
-        out_specs=vmem,
-        scratch_shapes=[
-            pltpu.VMEM((total, width), jnp.bfloat16),
-            pltpu.SemaphoreType.DMA((CHUNKS,)),
-        ],
-        compiler_params=pltpu.CompilerParams(vmem_limit_bytes=56 * 1024 * 1024),
-        cost_estimate=pl.CostEstimate(
-            flops=4 * total * number * width,
-            bytes_accessed=2 * total * width,
-            transcendentals=total * number,
-        ),
-        name="text_gradient",
-    )(scale, offset, wide, image_all)
-
-
-def image_gradient(images, wides, start, scale, offset):
-    number, width = images.shape
-    texts = sum(wide.shape[0] for wide in wides)
-    smem = pl.BlockSpec(memory_space=pltpu.SMEM)
-    vmem = pl.BlockSpec(memory_space=pltpu.VMEM)
-    return pl.pallas_call(
-        image_kernel,
-        out_shape=jax.ShapeDtypeStruct((number, width), jnp.float32),
-        in_specs=[smem, smem, smem, vmem] + [vmem] * len(wides),
+        kernel,
+        out_shape=jax.ShapeDtypeStruct((rows, width), jnp.bfloat16),
+        in_specs=[smem] * len(scalars) + [vmem, vmem],
         out_specs=vmem,
         compiler_params=pltpu.CompilerParams(vmem_limit_bytes=24 * 1024 * 1024),
         cost_estimate=pl.CostEstimate(
-            flops=4 * texts * number * width,
-            bytes_accessed=2 * texts * width,
-            transcendentals=texts * number,
+            flops=4 * wide.shape[0] * number * width,
+            bytes_accessed=4 * number * width,
+            transcendentals=wide.shape[0] * number,
         ),
-        name="image_gradient",
-    )(scale, offset, start, images, *wides)
+        name=name,
+    )(*scalars, wide, images)
+
+
+def exchange(blocks, groups):
+    return lax.all_to_all(
+        blocks, "blk", split_axis=0, concat_axis=0, tiled=True, axis_index_groups=groups
+    )
 
 
 def spread_to(rows, groups):
     members = len(groups[0])
-    blocks = jnp.broadcast_to(rows[None], (members,) + rows.shape)
-    got = lax.all_to_all(
-        blocks, "blk", split_axis=0, concat_axis=0, tiled=True, axis_index_groups=groups
-    )
+    got = exchange(jnp.broadcast_to(rows[None], (members,) + rows.shape), groups)
     return got.reshape(members * rows.shape[0], rows.shape[1])
 
 
-def loss_grads(wide, images, image_all, scale, offset):
-    blocks = lax.axis_size("blk")
+def groups_of(blocks):
     zs = blocks // (XS * CS)
-    count = images.shape[0]
     place = lambda z, x, c: (z * XS + x) * CS + c
     lines = [[place(z, x, c) for z in range(zs)] for x in range(XS) for c in range(CS)]
     rings = [[place(z, x, c) for x in range(XS)] for z in range(zs) for c in range(CS)]
-    swap = [
-        (place(z, x, c), place(z, x, 1 - c)) for z in range(zs) for x in range(XS) for c in range(CS)
-    ]
-    start = (lax.axis_index("blk") * count).reshape(1)
-    first = spread_to(spread_to(wide, lines), rings)
-    second = lax.ppermute(first, "blk", swap)
-    text_sum = text_gradient(wide, image_all, scale, offset)
-    second, text_sum = lax.optimization_barrier((second, text_sum))
-    image_sum = image_gradient(images, [first, second], start, scale, offset)
-    return text_sum, image_sum
+    pairs = [[place(z, x, c) for c in range(CS)] for z in range(zs) for x in range(XS)]
+    return lines, rings, pairs
+
+
+def both_cores(rows, pairs):
+    return lax.all_gather(rows, "blk", axis=0, tiled=True, axis_index_groups=pairs)
+
+
+def summed_parts(got, scale):
+    return scale * jnp.sum(got.astype(jnp.float32), axis=0)
+
+
+def loss_grads(wide, images, scale, offset, groups):
+    lines, rings, pairs = groups
+    number, width = images.shape
+    count = number // (XS * CS)
+    slots = wide.shape[0]
+    mine = lax.axis_index("blk")
+    core = (mine % CS).reshape(1)
+    start = (mine // (XS * CS) * number).reshape(1)
+    line = spread_to(wide, lines)
+    text_parts = call_parts(
+        text_parts_kernel, (scale, offset, start), line, images, line.shape[0], "text_parts"
+    )
+    text_got = exchange(text_parts.reshape(-1, slots, width), lines)
+    image_parts = call_parts(
+        image_parts_kernel,
+        (scale, offset, start, core),
+        both_cores(line, pairs),
+        images,
+        XS * count,
+        "image_parts",
+    )
+    image_got = exchange(image_parts.reshape(-1, count, width), rings)
+    return summed_parts(text_got, scale), summed_parts(image_got, scale)
 
 
 def local(
@@ -444,13 +427,16 @@
 ):
     slots = lax.axis_size("dp")
     params = (position, gain_in, gain_out, query_proj, pair_proj, out_proj, head_proj, temper)
-    own = images[0, 0]
-    image_all = lax.all_gather(own, "blk", axis=0, tiled=True)
-    sent = encode(captions[0, 0], lengths[0, 0], destination[0, 0], labels[0, 0], params, slots)
+    groups = groups_of(lax.axis_size("blk"))
+    pair = both_cores(images[0, 0], groups[2])
+    rows, pair = lax.optimization_barrier((captions, pair))
+    near = spread_to(pair, groups[1])
+    sent = encode(rows[0, 0], lengths[0, 0], destination[0, 0], labels[0, 0], params, slots)
+    sent, near = lax.optimization_barrier((sent, near))
     halves = sent.reshape(slots, 2, sent.shape[1] // 2)
     wide = lax.all_to_all(halves, "dp", split_axis=0, concat_axis=0, tiled=True)
     wide = wide.reshape(sent.shape)
-    text_sum, image_sum = loss_grads(wide, own, image_all, logit_scale, logit_bias)
+    text_sum, image_sum = loss_grads(wide, near, logit_scale, logit_bias, groups)
     return text_sum[None, None], image_sum[None, None]
 
 

time: 115 us -> 105 us (0.913)
  the two profiles are of different devices: /device:TPU:1 before, /device:TPU:8 now
where the time goes in v4:
time: 105 us; the launch traced here: 104 us
  blocking collectives  45.8 us (44%)
  waiting for transfers between devices  21.7 us (21%)
  starting transfers between devices  16.2 us (15%)
  Pallas kernels  14.5 us (14%)
  local copies, waits for them, and re-layouts  2.52 us (2%)
  between operations  1.98 us (2%)
  other arithmetic  1.42 us (1%)
    all_to_all x1, blocking collectives, local(): wide = lax.all_to_all(halves, 'dp', split_axis=0, concat_axis=0, tiled=True)  41.5 us
    all_to_all x4, waiting for transfers between devices, exchange(): lax.all_to_all(blocks, 'blk', split_axis=0, concat_axis=0, tiled=True, ax...  21.7 us
    all_to_all x4, starting transfers between devices, exchange(): lax.all_to_all(blocks, 'blk', split_axis=0, concat_axis=0, tiled=True, ax...  16.2 us
    pallas_call x1, Pallas kernels, encode(): pl.pallas_call(tower_kernel, out_shape=jax.ShapeDtypeStruct((slots, width...  10 us
    pallas_call x2, Pallas kernels, call_parts(): pl.pallas_call(kernel, out_shape=jax.ShapeDtypeStruct((rows, width), jnp....  4.54 us
    all_gather x2, blocking collectives, both_cores(): lax.all_gather(rows, 'blk', axis=0, tiled=True, axis_index_groups=pairs)  4.39 us
  transfers between devices with their start and end apart: 4, of which 4 were waited for; matrix products, arithmetic and copies ran while one was open for 1% of the time, Pallas kernels for 11%

profile of v4, /device:TPU:8, one launch (start us, length us, event | category | flops | bytes accessed | tf_op | source)
XLA Modules:
  0.0 104.2 jit_solution(6205193927780166975)
XLA Ops:
  0.6 2.1 %all-gather = bf16[1,1,64,1152]{3,2,1,0:T(8,128)(2,1)S(1)} all-gather(bf16[1,1,32,1152]{3,2,1,0:T(8,128)(2,1)} %param.19), channel_id=2, replica_groups={{0,1},{2,3},{4,5},{6,7},{8,9},{10,11},{12,13},{14,15},{16,17},{18,19},{..., dimensions={2}, use_global_device_ids=true | all-gather | bytes 221184 | tf_op jit(solution)/shard_map/all_gather | solution.py:379
  2.8 0.9 broadcast_in_dim.6
  3.6 4.3 %all-to-all-start = ((bf16[4,64,1152]{2,1,0:T(8,128)(2,1)}), bf16[4,64,1152]{2,1,0:T(8,128)(2,1)S(1)}, u32[]{:S(2)}, u32[]{:S(2)}) async-start(bf16[4,64,1152]{2,1,0:T(8,128)(2,1)} %broadcast_in_dim.6), calls=%async_computation | async-start | bytes 1179648 | tf_op jit(solution)/shard_map/all_to_all | solution.py:358
  7.9 10.0 %tower.1 = bf16[32,1280]{1,0:T(8,128)(2,1)} custom-call(f32[8]{0:T(128)} %temper_ref.1, s32[1,24]{1,0:T(1,128)} %bitcast.30, s32[1,24]{1,0:T(1,128)} %bitcast.31, s32[1,24]{1,0:T(1,128)} %bitcast.32, bf16[24,16,1152]{2,1,0:T(8,128)(2,1)} %bitcast.26, bf16[16,1152]{1,0:T(8,128)(2,1)} %position_hbm.1, f32[1152]{0:T(1024)} %gain_in_hbm.1, f32[1152]{0:T(1024)} %gain_out_hbm.1, ...), custom_call_target="tpu_custom_call" | custom-call | flops 1019215872 | bytes 10000000 | tf_op jit(solution)/shard_map/tower/pallas_call | solution.py:241
  17.9 0.5 all-to-all-done
  18.4 0.9 reshape.48
  19.3 41.5 %all_to_all.25 = bf16[32,2,640]{2,1,0:T(2,128)(2,1)S(1)} all-to-all(bf16[32,2,640]{2,1,0:T(2,128)(2,1)S(1)} %reshape.48), channel_id=1, replica_groups=mesh['dp'=32,'blk'=32] {'dp'}, dimensions={0} | all-to-all | bytes 163840 | tf_op jit(solution)/shard_map/all_to_all | solution.py:437
  60.8 0.7 broadcast_in_dim.8
  61.5 3.9 %all-to-all-start.2 = ((bf16[4,32,1280]{2,1,0:T(8,128)(2,1)}), bf16[4,32,1280]{2,1,0:T(8,128)(2,1)S(1)}, u32[]{:S(2)}, u32[]{:S(2)}) async-start(bf16[4,32,1280]{2,1,0:T(8,128)(2,1)} %broadcast_in_dim.8), calls=%async_computation.2 | async-start | bytes 655360 | tf_op jit(solution)/shard_map/all_to_all | solution.py:358
  66.7 7.4 %all-to-all-done.2 = bf16[4,32,1280]{2,1,0:T(8,128)(2,1)S(1)} async-done(((bf16[4,32,1280]{2,1,0:T(8,128)(2,1)}), bf16[4,32,1280]{2,1,0:T(8,128)(2,1)S(1)}, u32[]{:S(2)}, u32[]{:S(2)}) %all-to-all-start.2) | async-done | bytes 327712 | tf_op jit(solution)/shard_map/all_to_all | solution.py:358
  74.1 2.3 %all_gather.7.wide_ref = bf16[256,1280]{1,0:T(8,128)(2,1)S(1)} all-gather(bf16[128,1280]{1,0:T(8,128)(2,1)S(1)} %bitcast.23), channel_id=1, replica_groups={{0,1},{2,3},{4,5},{6,7},{8,9},{10,11},{12,13},{14,15},{16,17},{18,19},{..., dimensions={0}, use_global_device_ids=true | all-gather | bytes 983040 | tf_op jit(solution)/shard_map/all_gather | solution.py:379
  76.4 3.1 %image_parts.1 = bf16[128,1152]{1,0:T(8,128)(2,1)} custom-call(f32[1]{0:T(128)} %copy.18.scale_ref, f32[1]{0:T(128)S(6)} %copy.19.offset_ref, s32[1]{0:T(128)} %bitcast.1.start_ref, s32[1]{0:T(128)} %bitcast.12.core_ref, bf16[256,1280]{1,0:T(8,128)(2,1)S(1)} %all_gather.7.wide_ref, bf16[256,1152]{1,0:T(8,128)(2,1)S(1)} %bitcast.21), custom_call_target="tpu_custom_call" | custom-call | flops 301989888 | bytes 1179648 | tf_op jit(solution)/shard_map/image_parts/pallas_call | solution.py:342
  79.5 4.6 %all-to-all-start.4 = ((bf16[4,32,1152]{2,1,0:T(8,128)(2,1)}), bf16[4,32,1152]{2,1,0:T(8,128)(2,1)S(1)}, u32[]{:S(2)}, u32[]{:S(2)}) async-start(bf16[4,32,1152]{2,1,0:T(8,128)(2,1)} %bitcast.13), calls=%async_computation.4 | async-start | bytes 589824 | tf_op jit(solution)/shard_map/all_to_all | solution.py:358
  84.0 1.5 %text_parts.1 = bf16[128,1152]{1,0:T(8,128)(2,1)} custom-call(f32[1]{0:T(128)} %copy.18.scale_ref, f32[1]{0:T(128)S(6)} %copy.19.offset_ref, s32[1]{0:T(128)} %bitcast.1.start_ref, bf16[128,1280]{1,0:T(8,128)(2,1)S(1)} %bitcast.24, bf16[256,1152]{1,0:T(8,128)(2,1)S(1)} %bitcast.22), custom_call_target="tpu_custom_call" | custom-call | flops 150994944 | bytes 1179648 | tf_op jit(solution)/shard_map/text_parts/pallas_call | solution.py:342
  85.5 5.8 %all-to-all-done.4 = bf16[4,32,1152]{2,1,0:T(8,128)(2,1)S(1)} async-done(((bf16[4,32,1152]{2,1,0:T(8,128)(2,1)}), bf16[4,32,1152]{2,1,0:T(8,128)(2,1)S(1)}, u32[]{:S(2)}, u32[]{:S(2)}) %all-to-all-start.4) | async-done | bytes 294944 | tf_op jit(solution)/shard_map/all_to_all | solution.py:358
  91.4 3.5 %all-to-all-start.3 = ((bf16[4,32,1152]{2,1,0:T(8,128)(2,1)}), bf16[4,32,1152]{2,1,0:T(8,128)(2,1)S(1)}, u32[]{:S(2)}, u32[]{:S(2)}) async-start(bf16[4,32,1152]{2,1,0:T(8,128)(2,1)} %bitcast.10), calls=%async_computation.3 | async-start | bytes 589824 | tf_op jit(solution)/shard_map/all_to_all | solution.py:358
  94.9 0.7 multiply_bitcast_fusion
  95.5 8.0 %all-to-all-done.3 = bf16[4,32,1152]{2,1,0:T(8,128)(2,1)S(1)} async-done(((bf16[4,32,1152]{2,1,0:T(8,128)(2,1)}), bf16[4,32,1152]{2,1,0:T(8,128)(2,1)S(1)}, u32[]{:S(2)}, u32[]{:S(2)}) %all-to-all-start.3) | async-done | bytes 294944 | tf_op jit(solution)/shard_map/all_to_all | solution.py:358
  103.5 0.7 multiply_bitcast_fusion.1
  (3 shorter events, 0.1 us)
Async XLA Ops:
  3.6 14.8 %all-to-all-start = ((bf16[4,64,1152]{2,1,0:T(8,128)(2,1)}), bf16[4,64,1152]{2,1,0:T(8,128)(2,1)S(1)}, u32[]{:S(2)}, u32[]{:S(2)}) async-start(bf16[4,64,1152]{2,1,0:T(8,128)(2,1)} %broadcast_in_dim.6), calls=%async_computation | async-start | bytes 1179648 | tf_op jit(solution)/shard_map/all_to_all | solution.py:358
  61.5 12.6 %all-to-all-start.2 = ((bf16[4,32,1280]{2,1,0:T(8,128)(2,1)}), bf16[4,32,1280]{2,1,0:T(8,128)(2,1)S(1)}, u32[]{:S(2)}, u32[]{:S(2)}) async-start(bf16[4,32,1280]{2,1,0:T(8,128)(2,1)} %broadcast_in_dim.8), calls=%async_computation.2 | async-start | bytes 655360 | tf_op jit(solution)/shard_map/all_to_all | solution.py:358
  79.5 11.9 %all-to-all-start.4 = ((bf16[4,32,1152]{2,1,0:T(8,128)(2,1)}), bf16[4,32,1152]{2,1,0:T(8,128)(2,1)S(1)}, u32[]{:S(2)}, u32[]{:S(2)}) async-start(bf16[4,32,1152]{2,1,0:T(8,128)(2,1)} %bitcast.13), calls=%async_computation.4 | async-start | bytes 589824 | tf_op jit(solution)/shard_map/all_to_all | solution.py:358
  91.4 12.1 %all-to-all-start.3 = ((bf16[4,32,1152]{2,1,0:T(8,128)(2,1)}), bf16[4,32,1152]{2,1,0:T(8,128)(2,1)S(1)}, u32[]{:S(2)}, u32[]{:S(2)}) async-start(bf16[4,32,1152]{2,1,0:T(8,128)(2,1)} %bitcast.10), calls=%async_computation.3 | async-start | bytes 589824 | tf_op jit(solution)/shard_map/all_to_all | solution.py:358

commit v5 on v4

--- a/solution.py
+++ b/solution.py
@@ -305,13 +305,16 @@
 
 def text_parts_kernel(scale_ref, offset_ref, start_ref, wide_ref, images_ref, parts_ref):
     number, width = images_ref.shape
+    count = number // (XS * CS)
     images = images_ref[...]
     text = wide_ref[:, 0:width]
     label, live = aux_rows(wide_ref[:, width:])
     inverse = inverse_norm(images)
     logits = lax.dot_general(images, text, NT, preferred_element_type=jnp.float32)
     logits = (scale_ref[0] * inverse) * logits + offset_ref[0]
-    index = (start_ref[0] + iota((number, 1), 0)).astype(jnp.float32)
+    row = iota((number, 1), 0)
+    place = (row // count % XS) * CS + row // (count * XS)
+    index = (start_ref[0] + place * count + row % count).astype(jnp.float32)
     slopes = (slope_of(logits, label == index, live) * inverse).astype(jnp.bfloat16)
     parts_ref[...] = lax.dot_general(
         slopes, images, TN, preferred_element_type=jnp.float32
@@ -319,20 +322,18 @@
 
 
 def image_parts_kernel(scale_ref, offset_ref, start_ref, core_ref, wide_ref, images_ref, parts_ref):
-    number, width = parts_ref.shape
+    number, width = images_ref.shape
     count = number // XS
+    images = images_ref[...]
     text = wide_ref[:, 0:width]
     label, live = aux_rows(wide_ref[:, width:])
-    for x in range(XS):
-        row = pl.multiple_of((x * CS + core_ref[0]) * count, count)
-        images = images_ref[pl.ds(row, count), :]
-        logits = lax.dot_general(images, text, NT, preferred_element_type=jnp.float32)
-        logits = (scale_ref[0] * inverse_norm(images)) * logits + offset_ref[0]
-        index = (start_ref[0] + row + iota((count, 1), 0)).astype(jnp.float32)
-        slopes = slope_of(logits, label == index, live).astype(jnp.bfloat16)
-        parts_ref[x * count : (x + 1) * count, :] = jnp.dot(
-            slopes, text, preferred_element_type=jnp.float32
-        ).astype(jnp.bfloat16)
+    logits = lax.dot_general(images, text, NT, preferred_element_type=jnp.float32)
+    logits = (scale_ref[0] * inverse_norm(images)) * logits + offset_ref[0]
+    row = iota((number, 1), 0)
+    place = row // count * CS + core_ref[0]
+    index = (start_ref[0] + place * count + row % count).astype(jnp.float32)
+    slopes = slope_of(logits, label == index, live).astype(jnp.bfloat16)
+    parts_ref[...] = jnp.dot(slopes, text, preferred_element_type=jnp.float32).astype(jnp.bfloat16)
 
 
 def call_parts(kernel, scalars, wide, images, rows, name):
@@ -383,27 +384,34 @@
     return scale * jnp.sum(got.astype(jnp.float32), axis=0)
 
 
-def loss_grads(wide, images, scale, offset, groups):
+def loss_grads(wide, near, scale, offset, groups):
     lines, rings, pairs = groups
-    number, width = images.shape
-    count = number // (XS * CS)
+    number, width = near.shape
+    count = number // XS
     slots = wide.shape[0]
     mine = lax.axis_index("blk")
     core = (mine % CS).reshape(1)
-    start = (mine // (XS * CS) * number).reshape(1)
+    start = (mine // (XS * CS) * (number * CS)).reshape(1)
     line = spread_to(wide, lines)
     text_parts = call_parts(
-        text_parts_kernel, (scale, offset, start), line, images, line.shape[0], "text_parts"
-    )
+        text_parts_kernel,
+        (scale, offset, start),
+        line,
+        both_cores(near, pairs),
+        line.shape[0],
+        "text_parts",
+    )
+    text_parts, line = lax.optimization_barrier((text_parts, line))
     text_got = exchange(text_parts.reshape(-1, slots, width), lines)
     image_parts = call_parts(
         image_parts_kernel,
         (scale, offset, start, core),
         both_cores(line, pairs),
-        images,
-        XS * count,
+        near,
+        number,
         "image_parts",
     )
+    text_got, image_parts = lax.optimization_barrier((text_got, image_parts))
     image_got = exchange(image_parts.reshape(-1, count, width), rings)
     return summed_parts(text_got, scale), summed_parts(image_got, scale)
 
@@ -428,13 +436,12 @@
     slots = lax.axis_size("dp")
     params = (position, gain_in, gain_out, query_proj, pair_proj, out_proj, head_proj, temper)
     groups = groups_of(lax.axis_size("blk"))
-    pair = both_cores(images[0, 0], groups[2])
-    rows, pair = lax.optimization_barrier((captions, pair))
-    near = spread_to(pair, groups[1])
-    sent = encode(rows[0, 0], lengths[0, 0], destination[0, 0], labels[0, 0], params, slots)
+    near = spread_to(images[0, 0], groups[1])
+    sent = encode(captions[0, 0], lengths[0, 0], destination[0, 0], labels[0, 0], params, slots)
     sent, near = lax.optimization_barrier((sent, near))
     halves = sent.reshape(slots, 2, sent.shape[1] // 2)
     wide = lax.all_to_all(halves, "dp", split_axis=0, concat_axis=0, tiled=True)
+    wide, near = lax.optimization_barrier((wide, near))
     wide = wide.reshape(sent.shape)
     text_sum, image_sum = loss_grads(wide, near, logit_scale, logit_bias, groups)
     return text_sum[None, None], image_sum[None, None]

time: 105 us -> 97.1 us (0.925)
  waiting for transfers between devices: 21.7 us -> 14.9 us
  Pallas kernels: 14.5 us -> 12.9 us
    all_to_all x4, waiting for transfers between devices: 21.7 us -> 14.9 us  [exchange(): lax.all_to_all(blocks, 'blk', split_axis=0, concat_axis=0, tiled=True, ax...]
    pallas_call x2, Pallas kernels: 4.54 us -> 2.86 us  [call_parts(): pl.pallas_call(kernel, out_shape=jax.ShapeDtypeStruct((rows, width), jnp....]
  transfers between devices with their start and end apart: 4 -> 4, of which waited for: 4 -> 3; matrix products, arithmetic and copies ran while one was open for 1% -> 1% of each run, Pallas kernels for 11% -> 12%
where the time goes in v5:
time: 97.1 us; the launch traced here: 96.5 us
  blocking collectives  46 us (47%)
  starting transfers between devices  16 us (16%)
  waiting for transfers between devices  14.9 us (15%)
  Pallas kernels  12.9 us (13%)
  local copies, waits for them, and re-layouts  3.27 us (3%)
  between operations  1.99 us (2%)
  other arithmetic  1.42 us (1%)
    all_to_all x1, blocking collectives, local(): wide = lax.all_to_all(halves, 'dp', split_axis=0, concat_axis=0, tiled=True)  41.5 us
    all_to_all x4, starting transfers between devices, exchange(): lax.all_to_all(blocks, 'blk', split_axis=0, concat_axis=0, tiled=True, ax...  16 us
    all_to_all x4, waiting for transfers between devices, exchange(): lax.all_to_all(blocks, 'blk', split_axis=0, concat_axis=0, tiled=True, ax...  14.9 us
    pallas_call x1, Pallas kernels, encode(): pl.pallas_call(tower_kernel, out_shape=jax.ShapeDtypeStruct((slots, width...  10 us
    all_gather x2, blocking collectives, both_cores(): lax.all_gather(rows, 'blk', axis=0, tiled=True, axis_index_groups=pairs)  4.5 us
    pallas_call x2, Pallas kernels, call_parts(): pl.pallas_call(kernel, out_shape=jax.ShapeDtypeStruct((rows, width), jnp....  2.86 us
    broadcast_in_dim x2, local copies, waits for them, and re-layouts, spread_to(): jnp.broadcast_to(rows[None], (members,) + rows.shape)  2.35 us
  transfers between devices with their start and end apart: 4, of which 3 were waited for; matrix products, arithmetic and copies ran while one was open for 1% of the time, Pallas kernels for 12%

profile of v5, /device:TPU:8, one launch (start us, length us, event | category | flops | bytes accessed | tf_op | source)
XLA Modules:
  0.0 96.5 jit_solution(9052673932020190265)
XLA Ops:
  0.6 1.6 %broadcast_in_dim.9 = bf16[4,32,1152]{2,1,0:T(8,128)(2,1)} broadcast(bf16[32,1152]{1,0:T(8,128)(2,1)} %bitcast.29), dimensions={1,2} | broadcast | bytes 368640 | tf_op jit(solution)/shard_map/broadcast_in_dim | solution.py:366
  2.2 4.3 %all-to-all-start = ((bf16[4,32,1152]{2,1,0:T(8,128)(2,1)}), bf16[4,32,1152]{2,1,0:T(8,128)(2,1)S(1)}, u32[]{:S(2)}, u32[]{:S(2)}) async-start(bf16[4,32,1152]{2,1,0:T(8,128)(2,1)} %broadcast_in_dim.9), calls=%async_computation | async-start | bytes 589824 | tf_op jit(solution)/shard_map/all_to_all | solution.py:359
  6.5 10.0 %tower.1 = bf16[32,1280]{1,0:T(8,128)(2,1)} custom-call(f32[8]{0:T(128)} %temper_ref.1, s32[1,24]{1,0:T(1,128)} %bitcast.30, s32[1,24]{1,0:T(1,128)} %bitcast.31, s32[1,24]{1,0:T(1,128)} %bitcast.32, bf16[24,16,1152]{2,1,0:T(8,128)(2,1)} %bitcast.26, bf16[16,1152]{1,0:T(8,128)(2,1)} %position_hbm.1, f32[1152]{0:T(1024)} %gain_in_hbm.1, f32[1152]{0:T(1024)} %gain_out_hbm.1, ...), custom_call_target="tpu_custom_call" | custom-call | flops 1019215872 | bytes 10000000 | tf_op jit(solution)/shard_map/tower/pallas_call | solution.py:241
  16.5 0.0 all-to-all-done
  16.6 0.9 reshape.48
  17.5 41.5 %all_to_all.25 = bf16[32,2,640]{2,1,0:T(2,128)(2,1)S(1)} all-to-all(bf16[32,2,640]{2,1,0:T(2,128)(2,1)S(1)} %reshape.48), channel_id=1, replica_groups=mesh['dp'=32,'blk'=32] {'dp'}, dimensions={0} | all-to-all | bytes 163840 | tf_op jit(solution)/shard_map/all_to_all | solution.py:443
  58.9 0.7 broadcast_in_dim.21
  59.7 3.9 %all-to-all-start.2 = ((bf16[4,32,1280]{2,1,0:T(8,128)(2,1)}), bf16[4,32,1280]{2,1,0:T(8,128)(2,1)S(1)}, u32[]{:S(2)}, u32[]{:S(2)}) async-start(bf16[4,32,1280]{2,1,0:T(8,128)(2,1)} %broadcast_in_dim.21), calls=%async_computation.2 | async-start | bytes 655360 | tf_op jit(solution)/shard_map/all_to_all | solution.py:359
  64.9 2.2 %all_gather.6.images_ref = bf16[256,1152]{1,0:T(8,128)(2,1)S(1)} all-gather(bf16[128,1152]{1,0:T(8,128)(2,1)S(1)} %bitcast.23), channel_id=1, replica_groups={{0,1},{2,3},{4,5},{6,7},{8,9},{10,11},{12,13},{14,15},{16,17},{18,19},{..., dimensions={0}, use_global_device_ids=true | all-gather | bytes 884736 | tf_op jit(solution)/shard_map/all_gather | solution.py:380
  67.1 5.4 %all-to-all-done.2 = bf16[4,32,1280]{2,1,0:T(8,128)(2,1)S(1)} async-done(((bf16[4,32,1280]{2,1,0:T(8,128)(2,1)}), bf16[4,32,1280]{2,1,0:T(8,128)(2,1)S(1)}, u32[]{:S(2)}, u32[]{:S(2)}) %all-to-all-start.2) | async-done | bytes 327712 | tf_op jit(solution)/shard_map/all_to_all | solution.py:359
  72.5 1.5 %text_parts.1 = bf16[128,1152]{1,0:T(8,128)(2,1)} custom-call(f32[1]{0:T(128)} %copy.18.scale_ref, f32[1]{0:T(128)S(6)} %copy.19.offset_ref, s32[1]{0:T(128)} %bitcast.1.start_ref, bf16[128,1280]{1,0:T(8,128)(2,1)S(1)} %bitcast.21, bf16[256,1152]{1,0:T(8,128)(2,1)S(1)} %all_gather.6.images_ref), custom_call_target="tpu_custom_call" | custom-call | flops 150994944 | bytes 1179648 | tf_op jit(solution)/shard_map/text_parts/pallas_call | solution.py:343
  74.0 3.5 %all-to-all-start.3 = ((bf16[4,32,1152]{2,1,0:T(8,128)(2,1)}), bf16[4,32,1152]{2,1,0:T(8,128)(2,1)S(1)}, u32[]{:S(2)}, u32[]{:S(2)}) async-start(bf16[4,32,1152]{2,1,0:T(8,128)(2,1)} %bitcast.10), calls=%async_computation.3 | async-start | bytes 589824 | tf_op jit(solution)/shard_map/all_to_all | solution.py:359
  77.5 2.3 %all_gather.7.wide_ref = bf16[256,1280]{1,0:T(8,128)(2,1)S(1)} all-gather(bf16[128,1280]{1,0:T(8,128)(2,1)S(1)} %bitcast.22), channel_id=1, replica_groups={{0,1},{2,3},{4,5},{6,7},{8,9},{10,11},{12,13},{14,15},{16,17},{18,19},{..., dimensions={0}, use_global_device_ids=true | all-gather | bytes 983040 | tf_op jit(solution)/shard_map/all_gather | solution.py:380
  79.8 1.4 %image_parts.1 = bf16[128,1152]{1,0:T(8,128)(2,1)} custom-call(f32[1]{0:T(128)} %copy.18.scale_ref, f32[1]{0:T(128)S(6)} %copy.19.offset_ref, s32[1]{0:T(128)} %bitcast.1.start_ref, s32[1]{0:T(128)} %bitcast.11.core_ref, bf16[256,1280]{1,0:T(8,128)(2,1)S(1)} %all_gather.7.wide_ref, bf16[128,1152]{1,0:T(8,128)(2,1)S(1)} %bitcast.24), custom_call_target="tpu_custom_call" | custom-call | flops 150994944 | bytes 589824 | tf_op jit(solution)/shard_map/image_parts/pallas_call | solution.py:343
  81.1 3.4 %all-to-all-done.3 = bf16[4,32,1152]{2,1,0:T(8,128)(2,1)S(1)} async-done(((bf16[4,32,1152]{2,1,0:T(8,128)(2,1)}), bf16[4,32,1152]{2,1,0:T(8,128)(2,1)S(1)}, u32[]{:S(2)}, u32[]{:S(2)}) %all-to-all-start.3) | async-done | bytes 294944 | tf_op jit(solution)/shard_map/all_to_all | solution.py:359
  84.5 4.4 %all-to-all-start.4 = ((bf16[4,32,1152]{2,1,0:T(8,128)(2,1)}), bf16[4,32,1152]{2,1,0:T(8,128)(2,1)S(1)}, u32[]{:S(2)}, u32[]{:S(2)}) async-start(bf16[4,32,1152]{2,1,0:T(8,128)(2,1)} %bitcast.13), calls=%async_computation.4 | async-start | bytes 589824 | tf_op jit(solution)/shard_map/all_to_all | solution.py:359
  88.9 0.7 multiply_bitcast_fusion.1
  89.6 6.2 %all-to-all-done.4 = bf16[4,32,1152]{2,1,0:T(8,128)(2,1)S(1)} async-done(((bf16[4,32,1152]{2,1,0:T(8,128)(2,1)}), bf16[4,32,1152]{2,1,0:T(8,128)(2,1)S(1)}, u32[]{:S(2)}, u32[]{:S(2)}) %all-to-all-start.4) | async-done | bytes 294944 | tf_op jit(solution)/shard_map/all_to_all | solution.py:359
  95.8 0.7 multiply_bitcast_fusion
  (3 shorter events, 0.1 us)
Async XLA Ops:
  2.2 14.3 %all-to-all-start = ((bf16[4,32,1152]{2,1,0:T(8,128)(2,1)}), bf16[4,32,1152]{2,1,0:T(8,128)(2,1)S(1)}, u32[]{:S(2)}, u32[]{:S(2)}) async-start(bf16[4,32,1152]{2,1,0:T(8,128)(2,1)} %broadcast_in_dim.9), calls=%async_computation | async-start | bytes 589824 | tf_op jit(solution)/shard_map/all_to_all | solution.py:359
  59.7 12.8 %all-to-all-start.2 = ((bf16[4,32,1280]{2,1,0:T(8,128)(2,1)}), bf16[4,32,1280]{2,1,0:T(8,128)(2,1)S(1)}, u32[]{:S(2)}, u32[]{:S(2)}) async-start(bf16[4,32,1280]{2,1,0:T(8,128)(2,1)} %broadcast_in_dim.21), calls=%async_computation.2 | async-start | bytes 655360 | tf_op jit(solution)/shard_map/all_to_all | solution.py:359
  74.0 10.5 %all-to-all-start.3 = ((bf16[4,32,1152]{2,1,0:T(8,128)(2,1)}), bf16[4,32,1152]{2,1,0:T(8,128)(2,1)S(1)}, u32[]{:S(2)}, u32[]{:S(2)}) async-start(bf16[4,32,1152]{2,1,0:T(8,128)(2,1)} %bitcast.10), calls=%async_computation.3 | async-start | bytes 589824 | tf_op jit(solution)/shard_map/all_to_all | solution.py:359
  84.5 11.2 %all-to-all-start.4 = ((bf16[4,32,1152]{2,1,0:T(8,128)(2,1)}), bf16[4,32,1152]{2,1,0:T(8,128)(2,1)S(1)}, u32[]{:S(2)}, u32[]{:S(2)}) async-start(bf16[4,32,1152]{2,1,0:T(8,128)(2,1)} %bitcast.13), calls=%async_computation.4 | async-start | bytes 589824 | tf_op jit(solution)/shard_map/all_to_all | solution.py:359

commit v6 on v5

--- a/solution.py
+++ b/solution.py
@@ -7,9 +7,10 @@
 
 CS = 2
 XS = 4
+ZS = 4
 LANES = 128
 AUX = 128
-BATCHES = 8
+BATCHES = 2
 NT = (((1,), (1,)), ((), ()))
 TN = (((0,), (0,)), ((), ()))
 
@@ -150,7 +151,7 @@
         temper = jnp.where(lane == head, temper_ref[head], temper)
 
     pair_copy.wait()
-    step = width // 3
+    step = width
     for start in range(0, width, step):
         kv_ref[:, start : start + step] = jnp.dot(
             normed_ref[...], pair_ref[:, start : start + step], preferred_element_type=jnp.float32
@@ -173,7 +174,7 @@
     norm_low = (query_norm - norm_high.astype(jnp.float32)).astype(jnp.bfloat16)
 
     attended = jnp.zeros((number, wide_inner), jnp.float32)
-    parts = 2
+    parts = 1
     some = tokens // parts
     for part in range(parts):
         rows = slice(part * some, (part + 1) * some)
@@ -305,7 +306,7 @@
 
 def text_parts_kernel(scale_ref, offset_ref, start_ref, wide_ref, images_ref, parts_ref):
     number, width = images_ref.shape
-    count = number // (XS * CS)
+    count = number // (ZS * CS)
     images = images_ref[...]
     text = wide_ref[:, 0:width]
     label, live = aux_rows(wide_ref[:, width:])
@@ -313,7 +314,7 @@
     logits = lax.dot_general(images, text, NT, preferred_element_type=jnp.float32)
     logits = (scale_ref[0] * inverse) * logits + offset_ref[0]
     row = iota((number, 1), 0)
-    place = (row // count % XS) * CS + row // (count * XS)
+    place = (row // count % ZS) * (XS * CS) + row // (count * ZS)
     index = (start_ref[0] + place * count + row % count).astype(jnp.float32)
     slopes = (slope_of(logits, label == index, live) * inverse).astype(jnp.bfloat16)
     parts_ref[...] = lax.dot_general(
@@ -323,14 +324,14 @@
 
 def image_parts_kernel(scale_ref, offset_ref, start_ref, core_ref, wide_ref, images_ref, parts_ref):
     number, width = images_ref.shape
-    count = number // XS
+    count = number // ZS
     images = images_ref[...]
     text = wide_ref[:, 0:width]
     label, live = aux_rows(wide_ref[:, width:])
     logits = lax.dot_general(images, text, NT, preferred_element_type=jnp.float32)
     logits = (scale_ref[0] * inverse_norm(images)) * logits + offset_ref[0]
     row = iota((number, 1), 0)
-    place = row // count * CS + core_ref[0]
+    place = row // count * (XS * CS) + core_ref[0]
     index = (start_ref[0] + place * count + row % count).astype(jnp.float32)
     slopes = slope_of(logits, label == index, live).astype(jnp.bfloat16)
     parts_ref[...] = jnp.dot(slopes, text, preferred_element_type=jnp.float32).astype(jnp.bfloat16)
@@ -367,12 +368,11 @@
     return got.reshape(members * rows.shape[0], rows.shape[1])
 
 
-def groups_of(blocks):
-    zs = blocks // (XS * CS)
+def groups_of():
     place = lambda z, x, c: (z * XS + x) * CS + c
-    lines = [[place(z, x, c) for z in range(zs)] for x in range(XS) for c in range(CS)]
-    rings = [[place(z, x, c) for x in range(XS)] for z in range(zs) for c in range(CS)]
-    pairs = [[place(z, x, c) for c in range(CS)] for z in range(zs) for x in range(XS)]
+    lines = [[place(z, x, c) for z in range(ZS)] for x in range(XS) for c in range(CS)]
+    rings = [[place(z, x, c) for x in range(XS)] for z in range(ZS) for c in range(CS)]
+    pairs = [[place(z, x, c) for c in range(CS)] for z in range(ZS) for x in range(XS)]
     return lines, rings, pairs
 
 
@@ -387,32 +387,32 @@
 def loss_grads(wide, near, scale, offset, groups):
     lines, rings, pairs = groups
     number, width = near.shape
-    count = number // XS
+    count = number // ZS
     slots = wide.shape[0]
     mine = lax.axis_index("blk")
     core = (mine % CS).reshape(1)
-    start = (mine // (XS * CS) * (number * CS)).reshape(1)
-    line = spread_to(wide, lines)
+    start = (mine // CS % XS * (CS * count)).reshape(1)
+    ring = spread_to(wide, rings)
     text_parts = call_parts(
         text_parts_kernel,
         (scale, offset, start),
-        line,
+        ring,
         both_cores(near, pairs),
-        line.shape[0],
+        ring.shape[0],
         "text_parts",
     )
-    text_parts, line = lax.optimization_barrier((text_parts, line))
-    text_got = exchange(text_parts.reshape(-1, slots, width), lines)
+    text_parts, ring = lax.optimization_barrier((text_parts, ring))
+    text_got = exchange(text_parts.reshape(-1, slots, width), rings)
     image_parts = call_parts(
         image_parts_kernel,
         (scale, offset, start, core),
-        both_cores(line, pairs),
+        both_cores(ring, pairs),
         near,
         number,
         "image_parts",
     )
     text_got, image_parts = lax.optimization_barrier((text_got, image_parts))
-    image_got = exchange(image_parts.reshape(-1, count, width), rings)
+    image_got = exchange(image_parts.reshape(-1, count, width), lines)
     return summed_parts(text_got, scale), summed_parts(image_got, scale)
 
 
@@ -435,8 +435,8 @@
 ):
     slots = lax.axis_size("dp")
     params = (position, gain_in, gain_out, query_proj, pair_proj, out_proj, head_proj, temper)
-    groups = groups_of(lax.axis_size("blk"))
-    near = spread_to(images[0, 0], groups[1])
+    groups = groups_of()
+    near = spread_to(images[0, 0], groups[0])
     sent = encode(captions[0, 0], lengths[0, 0], destination[0, 0], labels[0, 0], params, slots)
     sent, near = lax.optimization_barrier((sent, near))
     halves = sent.reshape(slots, 2, sent.shape[1] // 2)

time: 97.1 us -> 95.2 us (0.980)
  the two profiles are of different devices: /device:TPU:8 before, /device:TPU:2 now
where the time goes in v6:
time: 95.2 us; the launch traced here: 94.6 us
  blocking collectives  43.2 us (45%)
  starting transfers between devices  21 us (22%)
  waiting for transfers between devices  12.3 us (13%)
  Pallas kernels  11.5 us (12%)
  local copies, waits for them, and re-layouts  3.27 us (3%)
  between operations  1.96 us (2%)
  other arithmetic  1.42 us (1%)
    all_to_all x1, blocking collectives, local(): wide = lax.all_to_all(halves, 'dp', split_axis=0, concat_axis=0, tiled=True)  38.7 us
    all_to_all x4, starting transfers between devices, exchange(): lax.all_to_all(blocks, 'blk', split_axis=0, concat_axis=0, tiled=True, ax...  21 us
    all_to_all x4, waiting for transfers between devices, exchange(): lax.all_to_all(blocks, 'blk', split_axis=0, concat_axis=0, tiled=True, ax...  12.3 us
    pallas_call x1, Pallas kernels, encode(): pl.pallas_call(tower_kernel, out_shape=jax.ShapeDtypeStruct((slots, width...  8.67 us
    all_gather x2, blocking collectives, both_cores(): lax.all_gather(rows, 'blk', axis=0, tiled=True, axis_index_groups=pairs)  4.49 us
    pallas_call x2, Pallas kernels, call_parts(): pl.pallas_call(kernel, out_shape=jax.ShapeDtypeStruct((rows, width), jnp....  2.86 us
    broadcast_in_dim x2, local copies, waits for them, and re-layouts, spread_to(): jnp.broadcast_to(rows[None], (members,) + rows.shape)  2.35 us
  transfers between devices with their start and end apart: 4, of which 4 were waited for; matrix products, arithmetic and copies ran while one was open for 1% of the time, Pallas kernels for 11%

profile of v6, /device:TPU:2, one launch (start us, length us, event | category | flops | bytes accessed | tf_op | source)
XLA Modules:
  0.0 94.6 jit_solution(16546474626771882181)
XLA Ops:
  0.6 1.6 %broadcast_in_dim.9 = bf16[4,32,1152]{2,1,0:T(8,128)(2,1)} broadcast(bf16[32,1152]{1,0:T(8,128)(2,1)} %bitcast.29), dimensions={1,2} | broadcast | bytes 368640 | tf_op jit(solution)/shard_map/broadcast_in_dim | solution.py:367
  2.2 7.3 %all-to-all-start = ((bf16[4,32,1152]{2,1,0:T(8,128)(2,1)}), bf16[4,32,1152]{2,1,0:T(8,128)(2,1)S(1)}, u32[]{:S(2)}, u32[]{:S(2)}) async-start(bf16[4,32,1152]{2,1,0:T(8,128)(2,1)} %broadcast_in_dim.9), calls=%async_computation | async-start | bytes 589824 | tf_op jit(solution)/shard_map/all_to_all | solution.py:360
  9.5 8.7 %tower.1 = bf16[32,1280]{1,0:T(8,128)(2,1)} custom-call(f32[8]{0:T(128)} %temper_ref.1, s32[1,24]{1,0:T(1,128)} %bitcast.30, s32[1,24]{1,0:T(1,128)} %bitcast.31, s32[1,24]{1,0:T(1,128)} %bitcast.32, bf16[24,16,1152]{2,1,0:T(8,128)(2,1)} %bitcast.26, bf16[16,1152]{1,0:T(8,128)(2,1)} %position_hbm.1, f32[1152]{0:T(1024)} %gain_in_hbm.1, f32[1152]{0:T(1024)} %gain_out_hbm.1, ...), custom_call_target="tpu_custom_call" | custom-call | flops 1019215872 | bytes 10000000 | tf_op jit(solution)/shard_map/tower/pallas_call | solution.py:242
  18.2 0.9 all-to-all-done
  19.1 0.9 reshape.48
  20.0 38.7 %all_to_all.25 = bf16[32,2,640]{2,1,0:T(2,128)(2,1)S(1)} all-to-all(bf16[32,2,640]{2,1,0:T(2,128)(2,1)S(1)} %reshape.48), channel_id=1, replica_groups=mesh['dp'=32,'blk'=32] {'dp'}, dimensions={0} | all-to-all | bytes 163840 | tf_op jit(solution)/shard_map/all_to_all | solution.py:443
  58.8 0.7 broadcast_in_dim.21
  59.5 4.8 %all-to-all-start.2 = ((bf16[4,32,1280]{2,1,0:T(8,128)(2,1)}), bf16[4,32,1280]{2,1,0:T(8,128)(2,1)S(1)}, u32[]{:S(2)}, u32[]{:S(2)}) async-start(bf16[4,32,1280]{2,1,0:T(8,128)(2,1)} %broadcast_in_dim.21), calls=%async_computation.2 | async-start | bytes 655360 | tf_op jit(solution)/shard_map/all_to_all | solution.py:360
  65.6 2.2 %all_gather.6.images_ref = bf16[256,1152]{1,0:T(8,128)(2,1)S(1)} all-gather(bf16[128,1152]{1,0:T(8,128)(2,1)S(1)} %bitcast.23), channel_id=1, replica_groups={{0,1},{2,3},{4,5},{6,7},{8,9},{10,11},{12,13},{14,15},{16,17},{18,19},{..., dimensions={0}, use_global_device_ids=true | all-gather | bytes 884736 | tf_op jit(solution)/shard_map/all_gather | solution.py:380
  67.8 2.0 %all-to-all-done.2 = bf16[4,32,1280]{2,1,0:T(8,128)(2,1)S(1)} async-done(((bf16[4,32,1280]{2,1,0:T(8,128)(2,1)}), bf16[4,32,1280]{2,1,0:T(8,128)(2,1)S(1)}, u32[]{:S(2)}, u32[]{:S(2)}) %all-to-all-start.2) | async-done | bytes 327712 | tf_op jit(solution)/shard_map/all_to_all | solution.py:360
  69.8 1.5 %text_parts.1 = bf16[128,1152]{1,0:T(8,128)(2,1)} custom-call(f32[1]{0:T(128)} %copy.18.scale_ref, f32[1]{0:T(128)S(6)} %copy.19.offset_ref, s32[1]{0:T(128)} %bitcast.1.start_ref, bf16[128,1280]{1,0:T(8,128)(2,1)S(1)} %bitcast.21, bf16[256,1152]{1,0:T(8,128)(2,1)S(1)} %all_gather.6.images_ref), custom_call_target="tpu_custom_call" | custom-call | flops 150994944 | bytes 1179648 | tf_op jit(solution)/shard_map/text_parts/pallas_call | solution.py:344
  71.3 4.9 %all-to-all-start.3 = ((bf16[4,32,1152]{2,1,0:T(8,128)(2,1)}), bf16[4,32,1152]{2,1,0:T(8,128)(2,1)S(1)}, u32[]{:S(2)}, u32[]{:S(2)}) async-start(bf16[4,32,1152]{2,1,0:T(8,128)(2,1)} %bitcast.10), calls=%async_computation.3 | async-start | bytes 589824 | tf_op jit(solution)/shard_map/all_to_all | solution.py:360
  76.2 2.3 %all_gather.7.wide_ref = bf16[256,1280]{1,0:T(8,128)(2,1)S(1)} all-gather(bf16[128,1280]{1,0:T(8,128)(2,1)S(1)} %bitcast.22), channel_id=1, replica_groups={{0,1},{2,3},{4,5},{6,7},{8,9},{10,11},{12,13},{14,15},{16,17},{18,19},{..., dimensions={0}, use_global_device_ids=true | all-gather | bytes 983040 | tf_op jit(solution)/shard_map/all_gather | solution.py:380
  78.5 1.4 %image_parts.1 = bf16[128,1152]{1,0:T(8,128)(2,1)} custom-call(f32[1]{0:T(128)} %copy.18.scale_ref, f32[1]{0:T(128)S(6)} %copy.19.offset_ref, s32[1]{0:T(128)} %bitcast.1.start_ref, s32[1]{0:T(128)} %bitcast.11.core_ref, bf16[256,1280]{1,0:T(8,128)(2,1)S(1)} %all_gather.7.wide_ref, bf16[128,1152]{1,0:T(8,128)(2,1)S(1)} %bitcast.24), custom_call_target="tpu_custom_call" | custom-call | flops 150994944 | bytes 589824 | tf_op jit(solution)/shard_map/image_parts/pallas_call | solution.py:344
  79.8 1.8 %all-to-all-done.3 = bf16[4,32,1152]{2,1,0:T(8,128)(2,1)S(1)} async-done(((bf16[4,32,1152]{2,1,0:T(8,128)(2,1)}), bf16[4,32,1152]{2,1,0:T(8,128)(2,1)S(1)}, u32[]{:S(2)}, u32[]{:S(2)}) %all-to-all-start.3) | async-done | bytes 294944 | tf_op jit(solution)/shard_map/all_to_all | solution.py:360
  81.6 4.1 %all-to-all-start.4 = ((bf16[4,32,1152]{2,1,0:T(8,128)(2,1)}), bf16[4,32,1152]{2,1,0:T(8,128)(2,1)S(1)}, u32[]{:S(2)}, u32[]{:S(2)}) async-start(bf16[4,32,1152]{2,1,0:T(8,128)(2,1)} %bitcast.13), calls=%async_computation.4 | async-start | bytes 589824 | tf_op jit(solution)/shard_map/all_to_all | solution.py:360
  85.7 0.7 multiply_bitcast_fusion.1
  86.4 7.5 %all-to-all-done.4 = bf16[4,32,1152]{2,1,0:T(8,128)(2,1)S(1)} async-done(((bf16[4,32,1152]{2,1,0:T(8,128)(2,1)}), bf16[4,32,1152]{2,1,0:T(8,128)(2,1)S(1)}, u32[]{:S(2)}, u32[]{:S(2)}) %all-to-all-start.4) | async-done | bytes 294944 | tf_op jit(solution)/shard_map/all_to_all | solution.py:360
  94.0 0.7 multiply_bitcast_fusion
  (3 shorter events, 0.1 us)
Async XLA Ops:
  2.2 16.9 %all-to-all-start = ((bf16[4,32,1152]{2,1,0:T(8,128)(2,1)}), bf16[4,32,1152]{2,1,0:T(8,128)(2,1)S(1)}, u32[]{:S(2)}, u32[]{:S(2)}) async-start(bf16[4,32,1152]{2,1,0:T(8,128)(2,1)} %broadcast_in_dim.9), calls=%async_computation | async-start | bytes 589824 | tf_op jit(solution)/shard_map/all_to_all | solution.py:360
  59.5 10.3 %all-to-all-start.2 = ((bf16[4,32,1280]{2,1,0:T(8,128)(2,1)}), bf16[4,32,1280]{2,1,0:T(8,128)(2,1)S(1)}, u32[]{:S(2)}, u32[]{:S(2)}) async-start(bf16[4,32,1280]{2,1,0:T(8,128)(2,1)} %broadcast_in_dim.21), calls=%async_computation.2 | async-start | bytes 655360 | tf_op jit(solution)/shard_map/all_to_all | solution.py:360
  71.3 10.3 %all-to-all-start.3 = ((bf16[4,32,1152]{2,1,0:T(8,128)(2,1)}), bf16[4,32,1152]{2,1,0:T(8,128)(2,1)S(1)}, u32[]{:S(2)}, u32[]{:S(2)}) async-start(bf16[4,32,1152]{2,1,0:T(8,128)(2,1)} %bitcast.10), calls=%async_computation.3 | async-start | bytes 589824 | tf_op jit(solution)/shard_map/all_to_all | solution.py:360
  81.6 12.3 %all-to-all-start.4 = ((bf16[4,32,1152]{2,1,0:T(8,128)(2,1)}), bf16[4,32,1152]{2,1,0:T(8,128)(2,1)S(1)}, u32[]{:S(2)}, u32[]{:S(2)}) async-start(bf16[4,32,1152]{2,1,0:T(8,128)(2,1)} %bitcast.13), calls=%async_computation.4 | async-start | bytes 589824 | tf_op jit(solution)/shard_map/all_to_all | solution.py:360

commit v7 on v6

--- a/solution.py
+++ b/solution.py
@@ -304,9 +304,15 @@
     return rows[0:1], rows[1:2]
 
 
-def text_parts_kernel(scale_ref, offset_ref, start_ref, wide_ref, images_ref, parts_ref):
+def places(mine_ref):
+    mine = mine_ref[0]
+    return mine // (XS * CS), mine // CS % XS, mine % CS
+
+
+def text_parts_kernel(scale_ref, offset_ref, mine_ref, wide_ref, images_ref, parts_ref):
     number, width = images_ref.shape
     count = number // (ZS * CS)
+    z, x, _ = places(mine_ref)
     images = images_ref[...]
     text = wide_ref[:, 0:width]
     label, live = aux_rows(wide_ref[:, width:])
@@ -314,27 +320,31 @@
     logits = lax.dot_general(images, text, NT, preferred_element_type=jnp.float32)
     logits = (scale_ref[0] * inverse) * logits + offset_ref[0]
     row = iota((number, 1), 0)
-    place = (row // count % ZS) * (XS * CS) + row // (count * ZS)
-    index = (start_ref[0] + place * count + row % count).astype(jnp.float32)
+    place = (((row // count % ZS) ^ z) * XS + x) * CS + row // (count * ZS)
+    index = (place * count + row % count).astype(jnp.float32)
     slopes = (slope_of(logits, label == index, live) * inverse).astype(jnp.bfloat16)
     parts_ref[...] = lax.dot_general(
         slopes, images, TN, preferred_element_type=jnp.float32
     ).astype(jnp.bfloat16)
 
 
-def image_parts_kernel(scale_ref, offset_ref, start_ref, core_ref, wide_ref, images_ref, parts_ref):
+def image_parts_kernel(scale_ref, offset_ref, mine_ref, wide_ref, images_ref, parts_ref):
     number, width = images_ref.shape
     count = number // ZS
+    z, x, core = places(mine_ref)
     images = images_ref[...]
     text = wide_ref[:, 0:width]
     label, live = aux_rows(wide_ref[:, width:])
     logits = lax.dot_general(images, text, NT, preferred_element_type=jnp.float32)
     logits = (scale_ref[0] * inverse_norm(images)) * logits + offset_ref[0]
     row = iota((number, 1), 0)
-    place = row // count * (XS * CS) + core_ref[0]
-    index = (start_ref[0] + place * count + row % count).astype(jnp.float32)
+    place = ((row // count ^ z) * XS + x) * CS + core
+    index = (place * count + row % count).astype(jnp.float32)
     slopes = slope_of(logits, label == index, live).astype(jnp.bfloat16)
-    parts_ref[...] = jnp.dot(slopes, text, preferred_element_type=jnp.float32).astype(jnp.bfloat16)
+    parts = jnp.dot(slopes, text, preferred_element_type=jnp.float32).astype(jnp.bfloat16)
+    for block in range(ZS):
+        first = pl.multiple_of((z ^ block) * count, count)
+        parts_ref[pl.ds(first, count), :] = parts[block * count : (block + 1) * count]
 
 
 def call_parts(kernel, scalars, wide, images, rows, name):
@@ -376,6 +386,17 @@
     return lines, rings, pairs
 
 
+def across(rows, bit):
+    place = lambda z, x, c: (z * XS + x) * CS + c
+    swap = [
+        (place(z, x, c), place(z ^ bit, x, c))
+        for z in range(ZS)
+        for x in range(XS)
+        for c in range(CS)
+    ]
+    return lax.ppermute(rows, "blk", swap)
+
+
 def both_cores(rows, pairs):
     return lax.all_gather(rows, "blk", axis=0, tiled=True, axis_index_groups=pairs)
 
@@ -389,13 +410,11 @@
     number, width = near.shape
     count = number // ZS
     slots = wide.shape[0]
-    mine = lax.axis_index("blk")
-    core = (mine % CS).reshape(1)
-    start = (mine // CS % XS * (CS * count)).reshape(1)
+    mine = lax.axis_index("blk").reshape(1)
     ring = spread_to(wide, rings)
     text_parts = call_parts(
         text_parts_kernel,
-        (scale, offset, start),
+        (scale, offset, mine),
         ring,
         both_cores(near, pairs),
         ring.shape[0],
@@ -405,7 +424,7 @@
     text_got = exchange(text_parts.reshape(-1, slots, width), rings)
     image_parts = call_parts(
         image_parts_kernel,
-        (scale, offset, start, core),
+        (scale, offset, mine),
         both_cores(ring, pairs),
         near,
         number,
@@ -436,12 +455,16 @@
     slots = lax.axis_size("dp")
     params = (position, gain_in, gain_out, query_proj, pair_proj, out_proj, head_proj, temper)
     groups = groups_of()
-    near = spread_to(images[0, 0], groups[0])
+    own = images[0, 0]
+    beside = across(own, 1)
     sent = encode(captions[0, 0], lengths[0, 0], destination[0, 0], labels[0, 0], params, slots)
-    sent, near = lax.optimization_barrier((sent, near))
+    two = jnp.concatenate([own, beside])
+    sent, two = lax.optimization_barrier((sent, two))
+    far = across(two, 2)
     halves = sent.reshape(slots, 2, sent.shape[1] // 2)
     wide = lax.all_to_all(halves, "dp", split_axis=0, concat_axis=0, tiled=True)
-    wide, near = lax.optimization_barrier((wide, near))
+    wide, far = lax.optimization_barrier((wide, far))
+    near = jnp.concatenate([two, far])
     wide = wide.reshape(sent.shape)
     text_sum, image_sum = loss_grads(wide, near, logit_scale, logit_bias, groups)
     return text_sum[None, None], image_sum[None, None]

time: 95.2 us -> 92.6 us (0.973)
  blocking collectives: 43.2 us -> 4.49 us
  starting transfers between devices: 21 us -> 45.9 us
  waiting for transfers between devices: 12.3 us -> 24.1 us
    all_to_all x1 -> x0, blocking collectives: 38.7 us -> none  [local(): wide = lax.all_to_all(halves, 'dp', split_axis=0, concat_axis=0, tiled=True)]
    all_to_all x0 -> x1, starting transfers between devices: none -> 23.5 us  [local(): wide = lax.all_to_all(halves, 'dp', split_axis=0, concat_axis=0, tiled=True)]
    ppermute x0 -> x2, starting transfers between devices: none -> 8.57 us  [across(): return lax.ppermute(rows, 'blk', swap)]
    ppermute x0 -> x2, waiting for transfers between devices: none -> 8.53 us  [across(): return lax.ppermute(rows, 'blk', swap)]
    all_to_all x4 -> x3, starting transfers between devices: 21 us -> 13.9 us  [exchange(): lax.all_to_all(blocks, 'blk', split_axis=0, concat_axis=0, tiled=True, ax...]
    all_to_all x0 -> x1, waiting for transfers between devices: none -> 2.98 us  [local(): wide = lax.all_to_all(halves, 'dp', split_axis=0, concat_axis=0, tiled=True)]
    broadcast_in_dim x2 -> x1, local copies, waits for them, and re-layouts: 2.35 us -> 0.75 us  [spread_to(): jnp.broadcast_to(rows[None], (members,) + rows.shape)]
    all_to_all x4 -> x3, waiting for transfers between devices: 12.3 us -> 12.6 us  [exchange(): lax.all_to_all(blocks, 'blk', split_axis=0, concat_axis=0, tiled=True, ax...]
  transfers between devices with their start and end apart: 4 -> 6, of which waited for: 4 -> 5; matrix products, arithmetic and copies ran while one was open for 1% -> 1% of each run, Pallas kernels for 11% -> 11%
where the time goes in v7:
time: 92.6 us; the launch traced here: 92 us
  starting transfers between devices  45.9 us (50%)
  waiting for transfers between devices  24.1 us (26%)
  Pallas kernels  11.7 us (13%)
  blocking collectives  4.49 us (5%)
  local copies, waits for them, and re-layouts  2.34 us (3%)
  between operations  2.02 us (2%)
  other arithmetic  1.44 us (2%)
    all_to_all x1, starting transfers between devices, local(): wide = lax.all_to_all(halves, 'dp', split_axis=0, concat_axis=0, tiled=True)  23.5 us
    all_to_all x3, starting transfers between devices, exchange(): lax.all_to_all(blocks, 'blk', split_axis=0, concat_axis=0, tiled=True, ax...  13.9 us
    all_to_all x3, waiting for transfers between devices, exchange(): lax.all_to_all(blocks, 'blk', split_axis=0, concat_axis=0, tiled=True, ax...  12.6 us
    pallas_call x1, Pallas kernels, encode(): pl.pallas_call(tower_kernel, out_shape=jax.ShapeDtypeStruct((slots, width...  8.81 us
    ppermute x2, starting transfers between devices, across(): return lax.ppermute(rows, 'blk', swap)  8.57 us
    ppermute x2, waiting for transfers between devices, across(): return lax.ppermute(rows, 'blk', swap)  8.53 us
    all_gather x2, blocking collectives, both_cores(): lax.all_gather(rows, 'blk', axis=0, tiled=True, axis_index_groups=pairs)  4.49 us
    all_to_all x1, waiting for transfers between devices, local(): wide = lax.all_to_all(halves, 'dp', split_axis=0, concat_axis=0, tiled=True)  2.98 us
  transfers between devices with their start and end apart: 6, of which 5 were waited for; matrix products, arithmetic and copies ran while one was open for 1% of the time, Pallas kernels for 11%

profile of v7, /device:TPU:2, one launch (start us, length us, event | category | flops | bytes accessed | tf_op | source)
XLA Modules:
  0.0 92.0 jit_solution(9471195185430611966)
XLA Ops:
  0.6 4.3 %collective-permute-start = (bf16[32,1152]{1,0:T(8,128)(2,1)}, bf16[32,1152]{1,0:T(8,128)(2,1)S(1)}, u32[]{:S(2)}, u32[]{:S(2)}) collective-permute-start(bf16[32,1152]{1,0:T(8,128)(2,1)} %bitcast.25), channel_id=1, source_target_pairs={{0,8},{1,9},{2,10},{3,11},{4,12},{5,13},{6,14},{7,15},{8,0},{9,1},... | collective-permute-start | bytes 221192 | tf_op jit(solution)/shard_map/ppermute | solution.py:397
  4.9 0.0 copy-start
  4.9 8.8 %tower.1 = bf16[32,1280]{1,0:T(8,128)(2,1)} custom-call(f32[8]{0:T(128)} %temper_ref.1, s32[1,24]{1,0:T(1,128)} %bitcast.27, s32[1,24]{1,0:T(1,128)} %bitcast.28, s32[1,24]{1,0:T(1,128)} %bitcast.29, bf16[24,16,1152]{2,1,0:T(8,128)(2,1)} %bitcast.22, bf16[16,1152]{1,0:T(8,128)(2,1)} %position_hbm.1, f32[1152]{0:T(1024)} %gain_in_hbm.1, f32[1152]{0:T(1024)} %gain_out_hbm.1, ...), custom_call_target="tpu_custom_call" | custom-call | flops 1019215872 | bytes 10000000 | tf_op jit(solution)/shard_map/tower/pallas_call | solution.py:242
  13.7 0.0 collective-permute-done
  13.8 0.0 copy-done
  13.8 1.5 %reshape.40 = bf16[32,2,640]{2,1,0:T(2,128)(2,1)} reshape(bf16[32,1280]{1,0:T(8,128)(2,1)} %tower.1) | data formatting | bytes 163840 | tf_op jit(solution)/shard_map/reshape | solution.py:464
  15.3 23.5 %all-to-all-start = ((bf16[32,2,640]{2,1,0:T(2,128)(2,1)}), bf16[32,2,640]{2,1,0:T(2,128)(2,1)S(1)}, u32[]{:S(2)}, u32[]{:S(2)}) async-start(bf16[32,2,640]{2,1,0:T(2,128)(2,1)} %reshape.40), calls=%async_computation | async-start | bytes 163840 | tf_op jit(solution)/shard_map/all_to_all | solution.py:465
  40.1 4.3 %collective-permute-start.1 = (bf16[64,1152]{1,0:T(8,128)(2,1)S(1)}, bf16[64,1152]{1,0:T(8,128)(2,1)S(1)}, u32[]{:S(2)}, u32[]{:S(2)}) collective-permute-start(bf16[64,1152]{1,0:T(8,128)(2,1)S(1)} %pad_maximum_fusion), channel_id=1, source_target_pairs={{0,16},{1,17},{2,18},{3,19},{4,20},{5,21},{6,22},{7,23},{8,24},{9,... | collective-permute-start | bytes 442376 | tf_op jit(solution)/shard_map/ppermute | solution.py:397
  44.4 8.5 %collective-permute-done.1 = bf16[64,1152]{1,0:T(8,128)(2,1)S(1)} collective-permute-done((bf16[64,1152]{1,0:T(8,128)(2,1)S(1)}, bf16[64,1152]{1,0:T(8,128)(2,1)S(1)}, u32[]{:S(2)}, u32[]{:S(2)}) %collective-permute-start.1) | collective-permute-done | bytes 147488 | tf_op jit(solution)/shard_map/ppermute | solution.py:397
  53.0 3.0 %all-to-all-done = bf16[32,2,640]{2,1,0:T(2,128)(2,1)S(1)} async-done(((bf16[32,2,640]{2,1,0:T(2,128)(2,1)}), bf16[32,2,640]{2,1,0:T(2,128)(2,1)S(1)}, u32[]{:S(2)}, u32[]{:S(2)}) %all-to-all-start) | async-done | bytes 81952 | tf_op jit(solution)/shard_map/all_to_all | solution.py:465
  56.0 0.7 broadcast_in_dim.5
  56.7 4.8 %all-to-all-start.1 = ((bf16[4,32,1280]{2,1,0:T(8,128)(2,1)}), bf16[4,32,1280]{2,1,0:T(8,128)(2,1)S(1)}, u32[]{:S(2)}, u32[]{:S(2)}) async-start(bf16[4,32,1280]{2,1,0:T(8,128)(2,1)} %broadcast_in_dim.5), calls=%async_computation.1 | async-start | bytes 655360 | tf_op jit(solution)/shard_map/all_to_all | solution.py:370
  61.6 2.2 %all_gather.6.images_ref = bf16[256,1152]{1,0:T(8,128)(2,1)S(1)} all-gather(bf16[128,1152]{1,0:T(8,128)(2,1)S(1)} %constant_dynamic-update-slice_fusion.images_ref), channel_id=1, replica_groups={{0,1},{2,3},{4,5},{6,7},{8,9},{10,11},{12,13},{14,15},{16,17},{18,19},{..., dimensions={0}, use_global_device_ids=true | all-gather | bytes 884736 | tf_op jit(solution)/shard_map/all_gather | solution.py:401
  63.8 3.3 %all-to-all-done.1 = bf16[4,32,1280]{2,1,0:T(8,128)(2,1)S(1)} async-done(((bf16[4,32,1280]{2,1,0:T(8,128)(2,1)}), bf16[4,32,1280]{2,1,0:T(8,128)(2,1)S(1)}, u32[]{:S(2)}, u32[]{:S(2)}) %all-to-all-start.1) | async-done | bytes 327712 | tf_op jit(solution)/shard_map/all_to_all | solution.py:370
  67.1 1.5 %text_parts.1 = bf16[128,1152]{1,0:T(8,128)(2,1)} custom-call(f32[1]{0:T(128)} %copy.19.scale_ref, f32[1]{0:T(128)S(6)} %copy.20.offset_ref, s32[1]{0:T(128)} %bitcast.1.mine_ref, bf16[128,1280]{1,0:T(8,128)(2,1)S(1)} %bitcast.19, bf16[256,1152]{1,0:T(8,128)(2,1)S(1)} %all_gather.6.images_ref), custom_call_target="tpu_custom_call" | custom-call | flops 150994944 | bytes 1179648 | tf_op jit(solution)/shard_map/text_parts/pallas_call | solution.py:354
  68.6 4.9 %all-to-all-start.2 = ((bf16[4,32,1152]{2,1,0:T(8,128)(2,1)}), bf16[4,32,1152]{2,1,0:T(8,128)(2,1)S(1)}, u32[]{:S(2)}, u32[]{:S(2)}) async-start(bf16[4,32,1152]{2,1,0:T(8,128)(2,1)} %bitcast.9), calls=%async_computation.2 | async-start | bytes 589824 | tf_op jit(solution)/shard_map/all_to_all | solution.py:370
  73.5 2.3 %all_gather.7.wide_ref = bf16[256,1280]{1,0:T(8,128)(2,1)S(1)} all-gather(bf16[128,1280]{1,0:T(8,128)(2,1)S(1)} %bitcast.20), channel_id=1, replica_groups={{0,1},{2,3},{4,5},{6,7},{8,9},{10,11},{12,13},{14,15},{16,17},{18,19},{..., dimensions={0}, use_global_device_ids=true | all-gather | bytes 983040 | tf_op jit(solution)/shard_map/all_gather | solution.py:401
  75.7 1.4 %image_parts.1 = bf16[128,1152]{1,0:T(8,128)(2,1)} custom-call(f32[1]{0:T(128)} %copy.19.scale_ref, f32[1]{0:T(128)S(6)} %copy.20.offset_ref, s32[1]{0:T(128)} %bitcast.1.mine_ref, bf16[256,1280]{1,0:T(8,128)(2,1)S(1)} %all_gather.7.wide_ref, bf16[128,1152]{1,0:T(8,128)(2,1)S(1)} %constant_dynamic-update-slice_fusion.images_ref), custom_call_target="tpu_custom_call" | custom-call | flops 150994944 | bytes 589824 | tf_op jit(solution)/shard_map/image_parts/pallas_call | solution.py:354
  77.1 1.7 %all-to-all-done.2 = bf16[4,32,1152]{2,1,0:T(8,128)(2,1)S(1)} async-done(((bf16[4,32,1152]{2,1,0:T(8,128)(2,1)}), bf16[4,32,1152]{2,1,0:T(8,128)(2,1)S(1)}, u32[]{:S(2)}, u32[]{:S(2)}) %all-to-all-start.2) | async-done | bytes 294944 | tf_op jit(solution)/shard_map/all_to_all | solution.py:370
  78.9 4.2 %all-to-all-start.3 = ((bf16[4,32,1152]{2,1,0:T(8,128)(2,1)}), bf16[4,32,1152]{2,1,0:T(8,128)(2,1)S(1)}, u32[]{:S(2)}, u32[]{:S(2)}) async-start(bf16[4,32,1152]{2,1,0:T(8,128)(2,1)} %bitcast.11), calls=%async_computation.3 | async-start | bytes 589824 | tf_op jit(solution)/shard_map/all_to_all | solution.py:370
  83.1 0.7 multiply_bitcast_fusion.1
  83.8 7.5 %all-to-all-done.3 = bf16[4,32,1152]{2,1,0:T(8,128)(2,1)S(1)} async-done(((bf16[4,32,1152]{2,1,0:T(8,128)(2,1)}), bf16[4,32,1152]{2,1,0:T(8,128)(2,1)S(1)}, u32[]{:S(2)}, u32[]{:S(2)}) %all-to-all-start.3) | async-done | bytes 294944 | tf_op jit(solution)/shard_map/all_to_all | solution.py:370
  91.3 0.7 multiply_bitcast_fusion
  (6 shorter events, 0.1 us)
Async XLA Ops:
  0.6 13.1 %collective-permute-start = (bf16[32,1152]{1,0:T(8,128)(2,1)}, bf16[32,1152]{1,0:T(8,128)(2,1)S(1)}, u32[]{:S(2)}, u32[]{:S(2)}) collective-permute-start(bf16[32,1152]{1,0:T(8,128)(2,1)} %bitcast.25), channel_id=1, source_target_pairs={{0,8},{1,9},{2,10},{3,11},{4,12},{5,13},{6,14},{7,15},{8,0},{9,1},... | collective-permute-start | bytes 221192 | tf_op jit(solution)/shard_map/ppermute | solution.py:397
  4.9 8.8 %copy-start = (bf16[1,1,32,1152]{3,2,1,0:T(8,128)(2,1)S(1)}, bf16[1,1,32,1152]{3,2,1,0:T(8,128)(2,1)}, u32[]{:S(2)}) copy-start(bf16[1,1,32,1152]{3,2,1,0:T(8,128)(2,1)} %param.19) | copy-start | bytes 221188
  15.3 40.6 %all-to-all-start = ((bf16[32,2,640]{2,1,0:T(2,128)(2,1)}), bf16[32,2,640]{2,1,0:T(2,128)(2,1)S(1)}, u32[]{:S(2)}, u32[]{:S(2)}) async-start(bf16[32,2,640]{2,1,0:T(2,128)(2,1)} %reshape.40), calls=%async_computation | async-start | bytes 163840 | tf_op jit(solution)/shard_map/all_to_all | solution.py:465
  40.1 12.8 %collective-permute-start.1 = (bf16[64,1152]{1,0:T(8,128)(2,1)S(1)}, bf16[64,1152]{1,0:T(8,128)(2,1)S(1)}, u32[]{:S(2)}, u32[]{:S(2)}) collective-permute-start(bf16[64,1152]{1,0:T(8,128)(2,1)S(1)} %pad_maximum_fusion), channel_id=1, source_target_pairs={{0,16},{1,17},{2,18},{3,19},{4,20},{5,21},{6,22},{7,23},{8,24},{9,... | collective-permute-start | bytes 442376 | tf_op jit(solution)/shard_map/ppermute | solution.py:397
  56.7 10.4 %all-to-all-start.1 = ((bf16[4,32,1280]{2,1,0:T(8,128)(2,1)}), bf16[4,32,1280]{2,1,0:T(8,128)(2,1)S(1)}, u32[]{:S(2)}, u32[]{:S(2)}) async-start(bf16[4,32,1280]{2,1,0:T(8,128)(2,1)} %broadcast_in_dim.5), calls=%async_computation.1 | async-start | bytes 655360 | tf_op jit(solution)/shard_map/all_to_all | solution.py:370
  68.6 10.3 %all-to-all-start.2 = ((bf16[4,32,1152]{2,1,0:T(8,128)(2,1)}), bf16[4,32,1152]{2,1,0:T(8,128)(2,1)S(1)}, u32[]{:S(2)}, u32[]{:S(2)}) async-start(bf16[4,32,1152]{2,1,0:T(8,128)(2,1)} %bitcast.9), calls=%async_computation.2 | async-start | bytes 589824 | tf_op jit(solution)/shard_map/all_to_all | solution.py:370
  78.9 12.4 %all-to-all-start.3 = ((bf16[4,32,1152]{2,1,0:T(8,128)(2,1)}), bf16[4,32,1152]{2,1,0:T(8,128)(2,1)S(1)}, u32[]{:S(2)}, u32[]{:S(2)}) async-start(bf16[4,32,1152]{2,1,0:T(8,128)(2,1)} %bitcast.11), calls=%async_computation.3 | async-start | bytes 589824 | tf_op jit(solution)/shard_map/all_to_all | solution.py:370

commit v8 on v7

--- a/solution.py
+++ b/solution.py
@@ -463,7 +463,6 @@
     far = across(two, 2)
     halves = sent.reshape(slots, 2, sent.shape[1] // 2)
     wide = lax.all_to_all(halves, "dp", split_axis=0, concat_axis=0, tiled=True)
-    wide, far = lax.optimization_barrier((wide, far))
     near = jnp.concatenate([two, far])
     wide = wide.reshape(sent.shape)
     text_sum, image_sum = loss_grads(wide, near, logit_scale, logit_bias, groups)

time: 92.6 us -> 92.6 us (level)
    all_to_all x1, waiting for transfers between devices: 2.98 us -> 11.5 us  [local(): wide = lax.all_to_all(halves, 'dp', split_axis=0, concat_axis=0, tiled=True)]
    ppermute x2, waiting for transfers between devices: 8.53 us -> 0.01 us  [across(): return lax.ppermute(rows, 'blk', swap)]
  transfers between devices with their start and end apart: 6 -> 6, of which waited for: 5 -> 4; matrix products, arithmetic and copies ran while one was open for 1% -> 2% of each run, Pallas kernels for 11% -> 11%
where the time goes in v8:
time: 92.6 us; the launch traced here: 92 us
  starting transfers between devices  45.9 us (50%)
  waiting for transfers between devices  24.1 us (26%)
  Pallas kernels  11.7 us (13%)
  blocking collectives  4.49 us (5%)
  local copies, waits for them, and re-layouts  2.34 us (3%)
  between operations  2.02 us (2%)
  other arithmetic  1.44 us (2%)
    all_to_all x1, starting transfers between devices, local(): wide = lax.all_to_all(halves, 'dp', split_axis=0, concat_axis=0, tiled=True)  23.5 us
    all_to_all x3, starting transfers between devices, exchange(): lax.all_to_all(blocks, 'blk', split_axis=0, concat_axis=0, tiled=True, ax...  13.9 us
    all_to_all x3, waiting for transfers between devices, exchange(): lax.all_to_all(blocks, 'blk', split_axis=0, concat_axis=0, tiled=True, ax...  12.6 us
    all_to_all x1, waiting for transfers between devices, local(): wide = lax.all_to_all(halves, 'dp', split_axis=0, concat_axis=0, tiled=True)  11.5 us
    pallas_call x1, Pallas kernels, encode(): pl.pallas_call(tower_kernel, out_shape=jax.ShapeDtypeStruct((slots, width...  8.81 us
    ppermute x2, starting transfers between devices, across(): return lax.ppermute(rows, 'blk', swap)  8.57 us
    all_gather x2, blocking collectives, both_cores(): lax.all_gather(rows, 'blk', axis=0, tiled=True, axis_index_groups=pairs)  4.49 us
    pallas_call x2, Pallas kernels, call_parts(): pl.pallas_call(kernel, out_shape=jax.ShapeDtypeStruct((rows, width), jnp....  2.88 us
  transfers between devices with their start and end apart: 6, of which 4 were waited for; matrix products, arithmetic and copies ran while one was open for 2% of the time, Pallas kernels for 11%

profile of v8, /device:TPU:2, one launch (start us, length us, event | category | flops | bytes accessed | tf_op | source)
XLA Modules:
  0.0 92.0 jit_solution(8170403571309318112)
XLA Ops:
  0.6 4.3 %collective-permute-start = (bf16[32,1152]{1,0:T(8,128)(2,1)}, bf16[32,1152]{1,0:T(8,128)(2,1)S(1)}, u32[]{:S(2)}, u32[]{:S(2)}) collective-permute-start(bf16[32,1152]{1,0:T(8,128)(2,1)} %bitcast.25), channel_id=1, source_target_pairs={{0,8},{1,9},{2,10},{3,11},{4,12},{5,13},{6,14},{7,15},{8,0},{9,1},... | collective-permute-start | bytes 221192 | tf_op jit(solution)/shard_map/ppermute | solution.py:397
  4.9 0.0 copy-start
  4.9 8.8 %tower.1 = bf16[32,1280]{1,0:T(8,128)(2,1)} custom-call(f32[8]{0:T(128)} %temper_ref.1, s32[1,24]{1,0:T(1,128)} %bitcast.27, s32[1,24]{1,0:T(1,128)} %bitcast.28, s32[1,24]{1,0:T(1,128)} %bitcast.29, bf16[24,16,1152]{2,1,0:T(8,128)(2,1)} %bitcast.22, bf16[16,1152]{1,0:T(8,128)(2,1)} %position_hbm.1, f32[1152]{0:T(1024)} %gain_in_hbm.1, f32[1152]{0:T(1024)} %gain_out_hbm.1, ...), custom_call_target="tpu_custom_call" | custom-call | flops 1019215872 | bytes 10000000 | tf_op jit(solution)/shard_map/tower/pallas_call | solution.py:242
  13.7 0.0 collective-permute-done
  13.8 0.0 copy-done
  13.8 1.5 %reshape.40 = bf16[32,2,640]{2,1,0:T(2,128)(2,1)} reshape(bf16[32,1280]{1,0:T(8,128)(2,1)} %tower.1) | data formatting | bytes 163840 | tf_op jit(solution)/shard_map/reshape | solution.py:464
  15.3 23.5 %all-to-all-start = ((bf16[32,2,640]{2,1,0:T(2,128)(2,1)}), bf16[32,2,640]{2,1,0:T(2,128)(2,1)S(1)}, u32[]{:S(2)}, u32[]{:S(2)}) async-start(bf16[32,2,640]{2,1,0:T(2,128)(2,1)} %reshape.40), calls=%async_computation | async-start | bytes 163840 | tf_op jit(solution)/shard_map/all_to_all | solution.py:465
  40.1 4.3 %collective-permute-start.1 = (bf16[64,1152]{1,0:T(8,128)(2,1)S(1)}, bf16[64,1152]{1,0:T(8,128)(2,1)S(1)}, u32[]{:S(2)}, u32[]{:S(2)}) collective-permute-start(bf16[64,1152]{1,0:T(8,128)(2,1)S(1)} %pad_maximum_fusion), channel_id=1, source_target_pairs={{0,16},{1,17},{2,18},{3,19},{4,20},{5,21},{6,22},{7,23},{8,24},{9,... | collective-permute-start | bytes 442376 | tf_op jit(solution)/shard_map/ppermute | solution.py:397
  44.4 11.5 %all-to-all-done = bf16[32,2,640]{2,1,0:T(2,128)(2,1)S(1)} async-done(((bf16[32,2,640]{2,1,0:T(2,128)(2,1)}), bf16[32,2,640]{2,1,0:T(2,128)(2,1)S(1)}, u32[]{:S(2)}, u32[]{:S(2)}) %all-to-all-start) | async-done | bytes 81952 | tf_op jit(solution)/shard_map/all_to_all | solution.py:465
  56.0 0.7 broadcast_in_dim.5
  56.7 4.8 %all-to-all-start.1 = ((bf16[4,32,1280]{2,1,0:T(8,128)(2,1)}), bf16[4,32,1280]{2,1,0:T(8,128)(2,1)S(1)}, u32[]{:S(2)}, u32[]{:S(2)}) async-start(bf16[4,32,1280]{2,1,0:T(8,128)(2,1)} %broadcast_in_dim.5), calls=%async_computation.1 | async-start | bytes 655360 | tf_op jit(solution)/shard_map/all_to_all | solution.py:370
  61.5 0.0 collective-permute-done.1
  61.6 2.2 %all_gather.6.images_ref = bf16[256,1152]{1,0:T(8,128)(2,1)S(1)} all-gather(bf16[128,1152]{1,0:T(8,128)(2,1)S(1)} %constant_dynamic-update-slice_fusion.images_ref), channel_id=1, replica_groups={{0,1},{2,3},{4,5},{6,7},{8,9},{10,11},{12,13},{14,15},{16,17},{18,19},{..., dimensions={0}, use_global_device_ids=true | all-gather | bytes 884736 | tf_op jit(solution)/shard_map/all_gather | solution.py:401
  63.8 3.3 %all-to-all-done.1 = bf16[4,32,1280]{2,1,0:T(8,128)(2,1)S(1)} async-done(((bf16[4,32,1280]{2,1,0:T(8,128)(2,1)}), bf16[4,32,1280]{2,1,0:T(8,128)(2,1)S(1)}, u32[]{:S(2)}, u32[]{:S(2)}) %all-to-all-start.1) | async-done | bytes 327712 | tf_op jit(solution)/shard_map/all_to_all | solution.py:370
  67.1 1.5 %text_parts.1 = bf16[128,1152]{1,0:T(8,128)(2,1)} custom-call(f32[1]{0:T(128)} %copy.19.scale_ref, f32[1]{0:T(128)S(6)} %copy.20.offset_ref, s32[1]{0:T(128)} %bitcast.1.mine_ref, bf16[128,1280]{1,0:T(8,128)(2,1)S(1)} %bitcast.19, bf16[256,1152]{1,0:T(8,128)(2,1)S(1)} %all_gather.6.images_ref), custom_call_target="tpu_custom_call" | custom-call | flops 150994944 | bytes 1179648 | tf_op jit(solution)/shard_map/text_parts/pallas_call | solution.py:354
  68.6 4.9 %all-to-all-start.2 = ((bf16[4,32,1152]{2,1,0:T(8,128)(2,1)}), bf16[4,32,1152]{2,1,0:T(8,128)(2,1)S(1)}, u32[]{:S(2)}, u32[]{:S(2)}) async-start(bf16[4,32,1152]{2,1,0:T(8,128)(2,1)} %bitcast.9), calls=%async_computation.2 | async-start | bytes 589824 | tf_op jit(solution)/shard_map/all_to_all | solution.py:370
  73.5 2.3 %all_gather.7.wide_ref = bf16[256,1280]{1,0:T(8,128)(2,1)S(1)} all-gather(bf16[128,1280]{1,0:T(8,128)(2,1)S(1)} %bitcast.20), channel_id=1, replica_groups={{0,1},{2,3},{4,5},{6,7},{8,9},{10,11},{12,13},{14,15},{16,17},{18,19},{..., dimensions={0}, use_global_device_ids=true | all-gather | bytes 983040 | tf_op jit(solution)/shard_map/all_gather | solution.py:401
  75.7 1.4 %image_parts.1 = bf16[128,1152]{1,0:T(8,128)(2,1)} custom-call(f32[1]{0:T(128)} %copy.19.scale_ref, f32[1]{0:T(128)S(6)} %copy.20.offset_ref, s32[1]{0:T(128)} %bitcast.1.mine_ref, bf16[256,1280]{1,0:T(8,128)(2,1)S(1)} %all_gather.7.wide_ref, bf16[128,1152]{1,0:T(8,128)(2,1)S(1)} %constant_dynamic-update-slice_fusion.images_ref), custom_call_target="tpu_custom_call" | custom-call | flops 150994944 | bytes 589824 | tf_op jit(solution)/shard_map/image_parts/pallas_call | solution.py:354
  77.1 1.7 %all-to-all-done.2 = bf16[4,32,1152]{2,1,0:T(8,128)(2,1)S(1)} async-done(((bf16[4,32,1152]{2,1,0:T(8,128)(2,1)}), bf16[4,32,1152]{2,1,0:T(8,128)(2,1)S(1)}, u32[]{:S(2)}, u32[]{:S(2)}) %all-to-all-start.2) | async-done | bytes 294944 | tf_op jit(solution)/shard_map/all_to_all | solution.py:370
  78.9 4.2 %all-to-all-start.3 = ((bf16[4,32,1152]{2,1,0:T(8,128)(2,1)}), bf16[4,32,1152]{2,1,0:T(8,128)(2,1)S(1)}, u32[]{:S(2)}, u32[]{:S(2)}) async-start(bf16[4,32,1152]{2,1,0:T(8,128)(2,1)} %bitcast.11), calls=%async_computation.3 | async-start | bytes 589824 | tf_op jit(solution)/shard_map/all_to_all | solution.py:370
  83.1 0.7 multiply_bitcast_fusion.1
  83.8 7.5 %all-to-all-done.3 = bf16[4,32,1152]{2,1,0:T(8,128)(2,1)S(1)} async-done(((bf16[4,32,1152]{2,1,0:T(8,128)(2,1)}), bf16[4,32,1152]{2,1,0:T(8,128)(2,1)S(1)}, u32[]{:S(2)}, u32[]{:S(2)}) %all-to-all-start.3) | async-done | bytes 294944 | tf_op jit(solution)/shard_map/all_to_all | solution.py:370
  91.3 0.7 multiply_bitcast_fusion
  (6 shorter events, 0.1 us)
Async XLA Ops:
  0.6 13.1 %collective-permute-start = (bf16[32,1152]{1,0:T(8,128)(2,1)}, bf16[32,1152]{1,0:T(8,128)(2,1)S(1)}, u32[]{:S(2)}, u32[]{:S(2)}) collective-permute-start(bf16[32,1152]{1,0:T(8,128)(2,1)} %bitcast.25), channel_id=1, source_target_pairs={{0,8},{1,9},{2,10},{3,11},{4,12},{5,13},{6,14},{7,15},{8,0},{9,1},... | collective-permute-start | bytes 221192 | tf_op jit(solution)/shard_map/ppermute | solution.py:397
  4.9 8.8 %copy-start = (bf16[1,1,32,1152]{3,2,1,0:T(8,128)(2,1)S(1)}, bf16[1,1,32,1152]{3,2,1,0:T(8,128)(2,1)}, u32[]{:S(2)}) copy-start(bf16[1,1,32,1152]{3,2,1,0:T(8,128)(2,1)} %param.19) | copy-start | bytes 221188
  15.3 40.6 %all-to-all-start = ((bf16[32,2,640]{2,1,0:T(2,128)(2,1)}), bf16[32,2,640]{2,1,0:T(2,128)(2,1)S(1)}, u32[]{:S(2)}, u32[]{:S(2)}) async-start(bf16[32,2,640]{2,1,0:T(2,128)(2,1)} %reshape.40), calls=%async_computation | async-start | bytes 163840 | tf_op jit(solution)/shard_map/all_to_all | solution.py:465
  40.1 21.4 %collective-permute-start.1 = (bf16[64,1152]{1,0:T(8,128)(2,1)S(1)}, bf16[64,1152]{1,0:T(8,128)(2,1)S(1)}, u32[]{:S(2)}, u32[]{:S(2)}) collective-permute-start(bf16[64,1152]{1,0:T(8,128)(2,1)S(1)} %pad_maximum_fusion), channel_id=1, source_target_pairs={{0,16},{1,17},{2,18},{3,19},{4,20},{5,21},{6,22},{7,23},{8,24},{9,... | collective-permute-start | bytes 442376 | tf_op jit(solution)/shard_map/ppermute | solution.py:397
  56.7 10.4 %all-to-all-start.1 = ((bf16[4,32,1280]{2,1,0:T(8,128)(2,1)}), bf16[4,32,1280]{2,1,0:T(8,128)(2,1)S(1)}, u32[]{:S(2)}, u32[]{:S(2)}) async-start(bf16[4,32,1280]{2,1,0:T(8,128)(2,1)} %broadcast_in_dim.5), calls=%async_computation.1 | async-start | bytes 655360 | tf_op jit(solution)/shard_map/all_to_all | solution.py:370
  68.6 10.3 %all-to-all-start.2 = ((bf16[4,32,1152]{2,1,0:T(8,128)(2,1)}), bf16[4,32,1152]{2,1,0:T(8,128)(2,1)S(1)}, u32[]{:S(2)}, u32[]{:S(2)}) async-start(bf16[4,32,1152]{2,1,0:T(8,128)(2,1)} %bitcast.9), calls=%async_computation.2 | async-start | bytes 589824 | tf_op jit(solution)/shard_map/all_to_all | solution.py:370
  78.9 12.4 %all-to-all-start.3 = ((bf16[4,32,1152]{2,1,0:T(8,128)(2,1)}), bf16[4,32,1152]{2,1,0:T(8,128)(2,1)S(1)}, u32[]{:S(2)}, u32[]{:S(2)}) async-start(bf16[4,32,1152]{2,1,0:T(8,128)(2,1)} %bitcast.11), calls=%async_computation.3 | async-start | bytes 589824 | tf_op jit(solution)/shard_map/all_to_all | solution.py:370

commit v9 on v8

--- a/solution.py
+++ b/solution.py
@@ -328,7 +328,7 @@
     ).astype(jnp.bfloat16)
 
 
-def image_parts_kernel(scale_ref, offset_ref, mine_ref, wide_ref, images_ref, parts_ref):
+def image_parts_kernel(scale_ref, offset_ref, mine_ref, wide_ref, images_ref, own_ref, *part_refs):
     number, width = images_ref.shape
     count = number // ZS
     z, x, core = places(mine_ref)
@@ -341,21 +341,21 @@
     place = ((row // count ^ z) * XS + x) * CS + core
     index = (place * count + row % count).astype(jnp.float32)
     slopes = slope_of(logits, label == index, live).astype(jnp.bfloat16)
-    parts = jnp.dot(slopes, text, preferred_element_type=jnp.float32).astype(jnp.bfloat16)
-    for block in range(ZS):
-        first = pl.multiple_of((z ^ block) * count, count)
-        parts_ref[pl.ds(first, count), :] = parts[block * count : (block + 1) * count]
-
-
-def call_parts(kernel, scalars, wide, images, rows, name):
+    parts = jnp.dot(slopes, text, preferred_element_type=jnp.float32)
+    own_ref[...] = parts[0:count]
+    for block, part_ref in enumerate(part_refs, 1):
+        part_ref[...] = parts[block * count : (block + 1) * count].astype(jnp.bfloat16)
+
+
+def call_parts(kernel, scalars, wide, images, outs, name):
     number, width = images.shape
     smem = pl.BlockSpec(memory_space=pltpu.SMEM)
     vmem = pl.BlockSpec(memory_space=pltpu.VMEM)
     return pl.pallas_call(
         kernel,
-        out_shape=jax.ShapeDtypeStruct((rows, width), jnp.bfloat16),
+        out_shape=[jax.ShapeDtypeStruct((rows, width), dtype) for rows, dtype in outs],
         in_specs=[smem] * len(scalars) + [vmem, vmem],
-        out_specs=vmem,
+        out_specs=[vmem] * len(outs),
         compiler_params=pltpu.CompilerParams(vmem_limit_bytes=24 * 1024 * 1024),
         cost_estimate=pl.CostEstimate(
             flops=4 * wide.shape[0] * number * width,
@@ -412,27 +412,30 @@
     slots = wide.shape[0]
     mine = lax.axis_index("blk").reshape(1)
     ring = spread_to(wide, rings)
-    text_parts = call_parts(
+    (text_parts,) = call_parts(
         text_parts_kernel,
         (scale, offset, mine),
         ring,
         both_cores(near, pairs),
-        ring.shape[0],
+        [(ring.shape[0], jnp.bfloat16)],
         "text_parts",
     )
     text_parts, ring = lax.optimization_barrier((text_parts, ring))
     text_got = exchange(text_parts.reshape(-1, slots, width), rings)
-    image_parts = call_parts(
+    image_sum, *image_parts = call_parts(
         image_parts_kernel,
         (scale, offset, mine),
         both_cores(ring, pairs),
         near,
-        number,
+        [(count, jnp.float32)] + [(count, jnp.bfloat16)] * (ZS - 1),
         "image_parts",
     )
+    farthest = across(image_parts.pop(), ZS - 1)
     text_got, image_parts = lax.optimization_barrier((text_got, image_parts))
-    image_got = exchange(image_parts.reshape(-1, count, width), lines)
-    return summed_parts(text_got, scale), summed_parts(image_got, scale)
+    got = [across(part, bits) for bits, part in enumerate(image_parts, 1)]
+    for part in [farthest] + got[::-1]:
+        image_sum = image_sum + part.astype(jnp.float32)
+    return summed_parts(text_got, scale), scale * image_sum
 
 
 def local(

time: 92.6 us -> 91.7 us (level)
  the two profiles are of different devices: /device:TPU:2 before, /device:TPU:8 now
where the time goes in v9:
time: 91.7 us; the launch traced here: 91.1 us
  starting transfers between devices  50.4 us (55%)
  waiting for transfers between devices  19.4 us (21%)
  Pallas kernels  11 us (12%)
  blocking collectives  4.5 us (5%)
  local copies, waits for them, and re-layouts  2.35 us (3%)
  between operations  2.07 us (2%)
  other arithmetic  1.43 us (2%)
    all_to_all x1, starting transfers between devices, local(): wide = lax.all_to_all(halves, 'dp', split_axis=0, concat_axis=0, tiled=True)  23.7 us
    ppermute x5, starting transfers between devices, across(): return lax.ppermute(rows, 'blk', swap)  19 us
    all_to_all x1, waiting for transfers between devices, local(): wide = lax.all_to_all(halves, 'dp', split_axis=0, concat_axis=0, tiled=True)  11 us
    pallas_call x1, Pallas kernels, encode(): pl.pallas_call(tower_kernel, out_shape=jax.ShapeDtypeStruct((slots, width...  8.81 us
    all_to_all x2, starting transfers between devices, exchange(): lax.all_to_all(blocks, 'blk', split_axis=0, concat_axis=0, tiled=True, ax...  7.74 us
    all_to_all x2, waiting for transfers between devices, exchange(): lax.all_to_all(blocks, 'blk', split_axis=0, concat_axis=0, tiled=True, ax...  4.78 us
    all_gather x2, blocking collectives, both_cores(): lax.all_gather(rows, 'blk', axis=0, tiled=True, axis_index_groups=pairs)  4.5 us
    ppermute x5, waiting for transfers between devices, across(): return lax.ppermute(rows, 'blk', swap)  3.57 us
  transfers between devices with their start and end apart: 8, of which 4 were waited for; matrix products, arithmetic and copies ran while one was open for 2% of the time, Pallas kernels for 10%

profile of v9, /device:TPU:8, one launch (start us, length us, event | category | flops | bytes accessed | tf_op | source)
XLA Modules:
  0.0 91.1 jit_solution(15610580764138018390)
XLA Ops:
  0.6 4.3 %collective-permute-start = (bf16[32,1152]{1,0:T(8,128)(2,1)}, bf16[32,1152]{1,0:T(8,128)(2,1)S(1)}, u32[]{:S(2)}, u32[]{:S(2)}) collective-permute-start(bf16[32,1152]{1,0:T(8,128)(2,1)} %bitcast.24), channel_id=1, source_target_pairs={{0,8},{1,9},{2,10},{3,11},{4,12},{5,13},{6,14},{7,15},{8,0},{9,1},... | collective-permute-start | bytes 221192 | tf_op jit(solution)/shard_map/ppermute | solution.py:397
  4.9 8.8 %tower.1 = bf16[32,1280]{1,0:T(8,128)(2,1)} custom-call(f32[8]{0:T(128)} %temper_ref.1, s32[1,24]{1,0:T(1,128)} %bitcast.26, s32[1,24]{1,0:T(1,128)} %bitcast.27, s32[1,24]{1,0:T(1,128)} %bitcast.28, bf16[24,16,1152]{2,1,0:T(8,128)(2,1)} %bitcast.21, bf16[16,1152]{1,0:T(8,128)(2,1)} %position_hbm.1, f32[1152]{0:T(1024)} %gain_in_hbm.1, f32[1152]{0:T(1024)} %gain_out_hbm.1, ...), custom_call_target="tpu_custom_call" | custom-call | flops 1019215872 | bytes 10000000 | tf_op jit(solution)/shard_map/tower/pallas_call | solution.py:242
  13.7 0.0 collective-permute-done
  13.8 1.5 %reshape.28 = bf16[32,2,640]{2,1,0:T(2,128)(2,1)} reshape(bf16[32,1280]{1,0:T(8,128)(2,1)} %tower.1) | data formatting | bytes 163840 | tf_op jit(solution)/shard_map/reshape | solution.py:467
  15.3 23.7 %all-to-all-start = ((bf16[32,2,640]{2,1,0:T(2,128)(2,1)}), bf16[32,2,640]{2,1,0:T(2,128)(2,1)S(1)}, u32[]{:S(2)}, u32[]{:S(2)}) async-start(bf16[32,2,640]{2,1,0:T(2,128)(2,1)} %reshape.28), calls=%async_computation | async-start | bytes 163840 | tf_op jit(solution)/shard_map/all_to_all | solution.py:468
  40.3 4.3 %collective-permute-start.1 = (bf16[64,1152]{1,0:T(8,128)(2,1)S(1)}, bf16[64,1152]{1,0:T(8,128)(2,1)S(1)}, u32[]{:S(2)}, u32[]{:S(2)}) collective-permute-start(bf16[64,1152]{1,0:T(8,128)(2,1)S(1)} %pad_maximum_fusion), channel_id=1, source_target_pairs={{0,16},{1,17},{2,18},{3,19},{4,20},{5,21},{6,22},{7,23},{8,24},{9,... | collective-permute-start | bytes 442376 | tf_op jit(solution)/shard_map/ppermute | solution.py:397
  44.7 11.0 %all-to-all-done = bf16[32,2,640]{2,1,0:T(2,128)(2,1)S(1)} async-done(((bf16[32,2,640]{2,1,0:T(2,128)(2,1)}), bf16[32,2,640]{2,1,0:T(2,128)(2,1)S(1)}, u32[]{:S(2)}, u32[]{:S(2)}) %all-to-all-start) | async-done | bytes 81952 | tf_op jit(solution)/shard_map/all_to_all | solution.py:468
  55.7 0.8 broadcast_in_dim.14
  56.4 4.3 %all-to-all-start.1 = ((bf16[4,32,1280]{2,1,0:T(8,128)(2,1)}), bf16[4,32,1280]{2,1,0:T(8,128)(2,1)S(1)}, u32[]{:S(2)}, u32[]{:S(2)}) async-start(bf16[4,32,1280]{2,1,0:T(8,128)(2,1)} %broadcast_in_dim.14), calls=%async_computation.1 | async-start | bytes 655360 | tf_op jit(solution)/shard_map/all_to_all | solution.py:370
  60.7 0.0 collective-permute-done.1
  60.8 2.2 %all_gather.6.images_ref = bf16[256,1152]{1,0:T(8,128)(2,1)S(1)} all-gather(bf16[128,1152]{1,0:T(8,128)(2,1)S(1)} %constant_dynamic-update-slice_fusion.images_ref), channel_id=1, replica_groups={{0,1},{2,3},{4,5},{6,7},{8,9},{10,11},{12,13},{14,15},{16,17},{18,19},{..., dimensions={0}, use_global_device_ids=true | all-gather | bytes 884736 | tf_op jit(solution)/shard_map/all_gather | solution.py:401
  63.0 4.8 %all-to-all-done.1 = bf16[4,32,1280]{2,1,0:T(8,128)(2,1)S(1)} async-done(((bf16[4,32,1280]{2,1,0:T(8,128)(2,1)}), bf16[4,32,1280]{2,1,0:T(8,128)(2,1)S(1)}, u32[]{:S(2)}, u32[]{:S(2)}) %all-to-all-start.1) | async-done | bytes 327712 | tf_op jit(solution)/shard_map/all_to_all | solution.py:370
  67.8 1.5 %text_parts.1 = bf16[128,1152]{1,0:T(8,128)(2,1)} custom-call(f32[1]{0:T(128)} %copy.19.scale_ref, f32[1]{0:T(128)S(6)} %copy.20.offset_ref, s32[1]{0:T(128)} %bitcast.1.mine_ref, bf16[128,1280]{1,0:T(8,128)(2,1)S(1)} %bitcast.18, bf16[256,1152]{1,0:T(8,128)(2,1)S(1)} %all_gather.6.images_ref), custom_call_target="tpu_custom_call" | custom-call | flops 150994944 | bytes 1179648 | tf_op jit(solution)/shard_map/text_parts/pallas_call | solution.py:354
  69.3 3.5 %all-to-all-start.2 = ((bf16[4,32,1152]{2,1,0:T(8,128)(2,1)}), bf16[4,32,1152]{2,1,0:T(8,128)(2,1)S(1)}, u32[]{:S(2)}, u32[]{:S(2)}) async-start(bf16[4,32,1152]{2,1,0:T(8,128)(2,1)} %bitcast.9), calls=%async_computation.2 | async-start | bytes 589824 | tf_op jit(solution)/shard_map/all_to_all | solution.py:370
  72.7 2.3 %all_gather.7.wide_ref = bf16[256,1280]{1,0:T(8,128)(2,1)S(1)} all-gather(bf16[128,1280]{1,0:T(8,128)(2,1)S(1)} %bitcast.19), channel_id=1, replica_groups={{0,1},{2,3},{4,5},{6,7},{8,9},{10,11},{12,13},{14,15},{16,17},{18,19},{..., dimensions={0}, use_global_device_ids=true | all-gather | bytes 983040 | tf_op jit(solution)/shard_map/all_gather | solution.py:401
  75.0 0.7 image_parts.1
  75.7 4.1 %collective-permute-start.2 = (bf16[32,1152]{1,0:T(8,128)(2,1)S(1)}, bf16[32,1152]{1,0:T(8,128)(2,1)S(1)}, u32[]{:S(2)}, u32[]{:S(2)}) collective-permute-start(bf16[32,1152]{1,0:T(8,128)(2,1)S(1)} %get-tuple-element.21), channel_id=1, source_target_pairs={{0,24},{1,25},{2,26},{3,27},{4,28},{5,29},{6,30},{7,31},{8,16},{9,... | collective-permute-start | bytes 221192 | tf_op jit(solution)/shard_map/ppermute | solution.py:397
  79.8 0.0 all-to-all-done.2
  79.8 4.3 %collective-permute-start.3 = (bf16[32,1152]{1,0:T(8,128)(2,1)S(1)}, bf16[32,1152]{1,0:T(8,128)(2,1)S(1)}, u32[]{:S(2)}, u32[]{:S(2)}) collective-permute-start(bf16[32,1152]{1,0:T(8,128)(2,1)S(1)} %get-tuple-element.22), channel_id=1, source_target_pairs={{0,16},{1,17},{2,18},{3,19},{4,20},{5,21},{6,22},{7,23},{8,24},{9,... | collective-permute-start | bytes 221192 | tf_op jit(solution)/shard_map/ppermute | solution.py:397
  84.1 2.0 %collective-permute-start.4 = (bf16[32,1152]{1,0:T(8,128)(2,1)S(1)}, bf16[32,1152]{1,0:T(8,128)(2,1)S(1)}, u32[]{:S(2)}, u32[]{:S(2)}) collective-permute-start(bf16[32,1152]{1,0:T(8,128)(2,1)S(1)} %get-tuple-element.23), channel_id=1, source_target_pairs={{0,8},{1,9},{2,10},{3,11},{4,12},{5,13},{6,14},{7,15},{8,0},{9,1},... | collective-permute-start | bytes 221192 | tf_op jit(solution)/shard_map/ppermute | solution.py:397
  86.1 0.7 multiply_bitcast_fusion.1
  86.8 1.4 %collective-permute-done.3 = bf16[32,1152]{1,0:T(8,128)(2,1)S(1)} collective-permute-done((bf16[32,1152]{1,0:T(8,128)(2,1)S(1)}, bf16[32,1152]{1,0:T(8,128)(2,1)S(1)}, u32[]{:S(2)}, u32[]{:S(2)}) %collective-permute-start.3) | collective-permute-done | bytes 73760 | tf_op jit(solution)/shard_map/ppermute | solution.py:397
  88.2 2.2 %collective-permute-done.4 = bf16[32,1152]{1,0:T(8,128)(2,1)S(1)} collective-permute-done((bf16[32,1152]{1,0:T(8,128)(2,1)S(1)}, bf16[32,1152]{1,0:T(8,128)(2,1)S(1)}, u32[]{:S(2)}, u32[]{:S(2)}) %collective-permute-start.4) | collective-permute-done | bytes 73760 | tf_op jit(solution)/shard_map/ppermute | solution.py:397
  90.4 0.7 multiply_bitcast_fusion
  (8 shorter events, 0.1 us)
Async XLA Ops:
  0.6 13.1 %collective-permute-start = (bf16[32,1152]{1,0:T(8,128)(2,1)}, bf16[32,1152]{1,0:T(8,128)(2,1)S(1)}, u32[]{:S(2)}, u32[]{:S(2)}) collective-permute-start(bf16[32,1152]{1,0:T(8,128)(2,1)} %bitcast.24), channel_id=1, source_target_pairs={{0,8},{1,9},{2,10},{3,11},{4,12},{5,13},{6,14},{7,15},{8,0},{9,1},... | collective-permute-start | bytes 221192 | tf_op jit(solution)/shard_map/ppermute | solution.py:397
  4.9 8.8 %copy-start = (bf16[1,1,32,1152]{3,2,1,0:T(8,128)(2,1)S(1)}, bf16[1,1,32,1152]{3,2,1,0:T(8,128)(2,1)}, u32[]{:S(2)}) copy-start(bf16[1,1,32,1152]{3,2,1,0:T(8,128)(2,1)} %param.19) | copy-start | bytes 221188
  15.3 40.3 %all-to-all-start = ((bf16[32,2,640]{2,1,0:T(2,128)(2,1)}), bf16[32,2,640]{2,1,0:T(2,128)(2,1)S(1)}, u32[]{:S(2)}, u32[]{:S(2)}) async-start(bf16[32,2,640]{2,1,0:T(2,128)(2,1)} %reshape.28), calls=%async_computation | async-start | bytes 163840 | tf_op jit(solution)/shard_map/all_to_all | solution.py:468
  40.3 20.4 %collective-permute-start.1 = (bf16[64,1152]{1,0:T(8,128)(2,1)S(1)}, bf16[64,1152]{1,0:T(8,128)(2,1)S(1)}, u32[]{:S(2)}, u32[]{:S(2)}) collective-permute-start(bf16[64,1152]{1,0:T(8,128)(2,1)S(1)} %pad_maximum_fusion), channel_id=1, source_target_pairs={{0,16},{1,17},{2,18},{3,19},{4,20},{5,21},{6,22},{7,23},{8,24},{9,... | collective-permute-start | bytes 442376 | tf_op jit(solution)/shard_map/ppermute | solution.py:397
  56.4 11.3 %all-to-all-start.1 = ((bf16[4,32,1280]{2,1,0:T(8,128)(2,1)}), bf16[4,32,1280]{2,1,0:T(8,128)(2,1)S(1)}, u32[]{:S(2)}, u32[]{:S(2)}) async-start(bf16[4,32,1280]{2,1,0:T(8,128)(2,1)} %broadcast_in_dim.14), calls=%async_computation.1 | async-start | bytes 655360 | tf_op jit(solution)/shard_map/all_to_all | solution.py:370
  69.3 10.5 %all-to-all-start.2 = ((bf16[4,32,1152]{2,1,0:T(8,128)(2,1)}), bf16[4,32,1152]{2,1,0:T(8,128)(2,1)S(1)}, u32[]{:S(2)}, u32[]{:S(2)}) async-start(bf16[4,32,1152]{2,1,0:T(8,128)(2,1)} %bitcast.9), calls=%async_computation.2 | async-start | bytes 589824 | tf_op jit(solution)/shard_map/all_to_all | solution.py:370
  75.7 11.2 %collective-permute-start.2 = (bf16[32,1152]{1,0:T(8,128)(2,1)S(1)}, bf16[32,1152]{1,0:T(8,128)(2,1)S(1)}, u32[]{:S(2)}, u32[]{:S(2)}) collective-permute-start(bf16[32,1152]{1,0:T(8,128)(2,1)S(1)} %get-tuple-element.21), channel_id=1, source_target_pairs={{0,24},{1,25},{2,26},{3,27},{4,28},{5,29},{6,30},{7,31},{8,16},{9,... | collective-permute-start | bytes 221192 | tf_op jit(solution)/shard_map/ppermute | solution.py:397
  79.8 8.4 %collective-permute-start.3 = (bf16[32,1152]{1,0:T(8,128)(2,1)S(1)}, bf16[32,1152]{1,0:T(8,128)(2,1)S(1)}, u32[]{:S(2)}, u32[]{:S(2)}) collective-permute-start(bf16[32,1152]{1,0:T(8,128)(2,1)S(1)} %get-tuple-element.22), channel_id=1, source_target_pairs={{0,16},{1,17},{2,18},{3,19},{4,20},{5,21},{6,22},{7,23},{8,24},{9,... | collective-permute-start | bytes 221192 | tf_op jit(solution)/shard_map/ppermute | solution.py:397
  84.1 6.2 %collective-permute-start.4 = (bf16[32,1152]{1,0:T(8,128)(2,1)S(1)}, bf16[32,1152]{1,0:T(8,128)(2,1)S(1)}, u32[]{:S(2)}, u32[]{:S(2)}) collective-permute-start(bf16[32,1152]{1,0:T(8,128)(2,1)S(1)} %get-tuple-element.23), channel_id=1, source_target_pairs={{0,8},{1,9},{2,10},{3,11},{4,12},{5,13},{6,14},{7,15},{8,0},{9,1},... | collective-permute-start | bytes 221192 | tf_op jit(solution)/shard_map/ppermute | solution.py:397

commit v10 on v9

--- a/solution.py
+++ b/solution.py
@@ -215,9 +215,6 @@
     )
     target_copy.wait()
     route = as_half(target_ref[...] == iota((slots, number), 0))
-    wide_ref[:, 0:width] = jnp.dot(route, pooled, preferred_element_type=jnp.float32).astype(
-        jnp.bfloat16
-    )
     label_int = label_col.astype(jnp.int32)
     column = iota((number, AUX), 1)
     aux = jnp.where(
@@ -226,9 +223,12 @@
         jnp.where(column == 1, label_int % 32, jnp.where(column == 2, 1, 0)),
     )
     aux = aux.astype(jnp.float32).astype(jnp.bfloat16)
-    wide_ref[:, width : width + AUX] = jnp.dot(
-        route, aux, preferred_element_type=jnp.float32
-    ).astype(jnp.bfloat16)
+    half = wide_ref.shape[2]
+    tail = jnp.concatenate([pooled[:, half:], aux], axis=1)
+    for side, rows in enumerate((pooled[:, :half], tail)):
+        wide_ref[:, side, :] = jnp.dot(route, rows, preferred_element_type=jnp.float32).astype(
+            jnp.bfloat16
+        )
 
 
 def encode(captions, counts, target, label, params, slots):
@@ -241,7 +241,7 @@
     hbm = pl.BlockSpec(memory_space=pl.ANY)
     return pl.pallas_call(
         tower_kernel,
-        out_shape=jax.ShapeDtypeStruct((slots, width + AUX), jnp.bfloat16),
+        out_shape=jax.ShapeDtypeStruct((slots, 2, (width + AUX) // 2), jnp.bfloat16),
         in_specs=[smem] + [hbm] * 11,
         out_specs=vmem,
         scratch_shapes=[
@@ -464,10 +464,9 @@
     two = jnp.concatenate([own, beside])
     sent, two = lax.optimization_barrier((sent, two))
     far = across(two, 2)
-    halves = sent.reshape(slots, 2, sent.shape[1] // 2)
-    wide = lax.all_to_all(halves, "dp", split_axis=0, concat_axis=0, tiled=True)
+    wide = lax.all_to_all(sent, "dp", split_axis=0, concat_axis=0, tiled=True)
     near = jnp.concatenate([two, far])
-    wide = wide.reshape(sent.shape)
+    wide = wide.reshape(slots, -1)
     text_sum, image_sum = loss_grads(wide, near, logit_scale, logit_bias, groups)
     return text_sum[None, None], image_sum[None, None]
 

time: 91.7 us -> 90.1 us (0.983)
  local copies, waits for them, and re-layouts: 2.35 us -> 0.8 us
    reshape x1 -> x0, local copies, waits for them, and re-layouts: 1.55 us -> none  [local(): halves = sent.reshape(slots, 2, sent.shape[1] // 2)]
  transfers between devices with their start and end apart: 8 -> 8, of which waited for: 4 -> 4; matrix products, arithmetic and copies ran while one was open for 2% -> 2% of each run, Pallas kernels for 10% -> 11%
where the time goes in v10:
time: 90.1 us; the launch traced here: 89.6 us
  starting transfers between devices  50.4 us (56%)
  waiting for transfers between devices  19.4 us (22%)
  Pallas kernels  11 us (12%)
  blocking collectives  4.5 us (5%)
  between operations  2.07 us (2%)
  other arithmetic  1.43 us (2%)
    all_to_all x1, starting transfers between devices, local(): wide = lax.all_to_all(sent, 'dp', split_axis=0, concat_axis=0, tiled=True)  23.7 us
    ppermute x5, starting transfers between devices, across(): return lax.ppermute(rows, 'blk', swap)  19 us
    all_to_all x1, waiting for transfers between devices, local(): wide = lax.all_to_all(sent, 'dp', split_axis=0, concat_axis=0, tiled=True)  11 us
    pallas_call x1, Pallas kernels, encode(): pl.pallas_call(tower_kernel, out_shape=jax.ShapeDtypeStruct((slots, 2, (w...  8.84 us
    all_to_all x2, starting transfers between devices, exchange(): lax.all_to_all(blocks, 'blk', split_axis=0, concat_axis=0, tiled=True, ax...  7.74 us
    all_to_all x2, waiting for transfers between devices, exchange(): lax.all_to_all(blocks, 'blk', split_axis=0, concat_axis=0, tiled=True, ax...  4.78 us
    all_gather x2, blocking collectives, both_cores(): lax.all_gather(rows, 'blk', axis=0, tiled=True, axis_index_groups=pairs)  4.5 us
    ppermute x5, waiting for transfers between devices, across(): return lax.ppermute(rows, 'blk', swap)  3.56 us
  transfers between devices with their start and end apart: 8, of which 4 were waited for; matrix products, arithmetic and copies ran while one was open for 2% of the time, Pallas kernels for 11%

profile of v10, /device:TPU:8, one launch (start us, length us, event | category | flops | bytes accessed | tf_op | source)
XLA Modules:
  0.0 89.6 jit_solution(11861544256602563649)
XLA Ops:
  0.6 4.3 %collective-permute-start = (bf16[32,1152]{1,0:T(8,128)(2,1)}, bf16[32,1152]{1,0:T(8,128)(2,1)S(1)}, u32[]{:S(2)}, u32[]{:S(2)}) collective-permute-start(bf16[32,1152]{1,0:T(8,128)(2,1)} %bitcast.24), channel_id=1, source_target_pairs={{0,8},{1,9},{2,10},{3,11},{4,12},{5,13},{6,14},{7,15},{8,0},{9,1},... | collective-permute-start | bytes 221192 | tf_op jit(solution)/shard_map/ppermute | solution.py:397
  4.9 8.8 %tower.1 = bf16[32,2,640]{2,1,0:T(2,128)(2,1)} custom-call(f32[8]{0:T(128)} %temper_ref.1, s32[1,24]{1,0:T(1,128)} %bitcast.26, s32[1,24]{1,0:T(1,128)} %bitcast.27, s32[1,24]{1,0:T(1,128)} %bitcast.28, bf16[24,16,1152]{2,1,0:T(8,128)(2,1)} %bitcast.21, bf16[16,1152]{1,0:T(8,128)(2,1)} %position_hbm.1, f32[1152]{0:T(1024)} %gain_in_hbm.1, ...), custom_call_target="tpu_custom_call" | custom-call | flops 1019215872 | bytes 10000000 | tf_op jit(solution)/shard_map/tower/pallas_call | solution.py:242
  13.8 0.0 collective-permute-done
  13.8 23.7 %all-to-all-start = ((bf16[32,2,640]{2,1,0:T(2,128)(2,1)}), bf16[32,2,640]{2,1,0:T(2,128)(2,1)S(1)}, u32[]{:S(2)}, u32[]{:S(2)}) async-start(bf16[32,2,640]{2,1,0:T(2,128)(2,1)} %tower.1), calls=%async_computation | async-start | bytes 163840 | tf_op jit(solution)/shard_map/all_to_all | solution.py:467
  38.8 4.3 %collective-permute-start.1 = (bf16[64,1152]{1,0:T(8,128)(2,1)S(1)}, bf16[64,1152]{1,0:T(8,128)(2,1)S(1)}, u32[]{:S(2)}, u32[]{:S(2)}) collective-permute-start(bf16[64,1152]{1,0:T(8,128)(2,1)S(1)} %pad_maximum_fusion), channel_id=1, source_target_pairs={{0,16},{1,17},{2,18},{3,19},{4,20},{5,21},{6,22},{7,23},{8,24},{9,... | collective-permute-start | bytes 442376 | tf_op jit(solution)/shard_map/ppermute | solution.py:397
  43.2 11.0 %all-to-all-done = bf16[32,2,640]{2,1,0:T(2,128)(2,1)S(1)} async-done(((bf16[32,2,640]{2,1,0:T(2,128)(2,1)}), bf16[32,2,640]{2,1,0:T(2,128)(2,1)S(1)}, u32[]{:S(2)}, u32[]{:S(2)}) %all-to-all-start) | async-done | bytes 81952 | tf_op jit(solution)/shard_map/all_to_all | solution.py:467
  54.2 0.8 broadcast_in_dim.14
  54.9 4.3 %all-to-all-start.1 = ((bf16[4,32,1280]{2,1,0:T(8,128)(2,1)}), bf16[4,32,1280]{2,1,0:T(8,128)(2,1)S(1)}, u32[]{:S(2)}, u32[]{:S(2)}) async-start(bf16[4,32,1280]{2,1,0:T(8,128)(2,1)} %broadcast_in_dim.14), calls=%async_computation.1 | async-start | bytes 655360 | tf_op jit(solution)/shard_map/all_to_all | solution.py:370
  59.2 0.0 collective-permute-done.1
  59.3 2.2 %all_gather.6.images_ref = bf16[256,1152]{1,0:T(8,128)(2,1)S(1)} all-gather(bf16[128,1152]{1,0:T(8,128)(2,1)S(1)} %constant_dynamic-update-slice_fusion.images_ref), channel_id=1, replica_groups={{0,1},{2,3},{4,5},{6,7},{8,9},{10,11},{12,13},{14,15},{16,17},{18,19},{..., dimensions={0}, use_global_device_ids=true | all-gather | bytes 884736 | tf_op jit(solution)/shard_map/all_gather | solution.py:401
  61.5 4.8 %all-to-all-done.1 = bf16[4,32,1280]{2,1,0:T(8,128)(2,1)S(1)} async-done(((bf16[4,32,1280]{2,1,0:T(8,128)(2,1)}), bf16[4,32,1280]{2,1,0:T(8,128)(2,1)S(1)}, u32[]{:S(2)}, u32[]{:S(2)}) %all-to-all-start.1) | async-done | bytes 327712 | tf_op jit(solution)/shard_map/all_to_all | solution.py:370
  66.3 1.5 %text_parts.1 = bf16[128,1152]{1,0:T(8,128)(2,1)} custom-call(f32[1]{0:T(128)} %copy.19.scale_ref, f32[1]{0:T(128)S(6)} %copy.20.offset_ref, s32[1]{0:T(128)} %bitcast.1.mine_ref, bf16[128,1280]{1,0:T(8,128)(2,1)S(1)} %bitcast.18, bf16[256,1152]{1,0:T(8,128)(2,1)S(1)} %all_gather.6.images_ref), custom_call_target="tpu_custom_call" | custom-call | flops 150994944 | bytes 1179648 | tf_op jit(solution)/shard_map/text_parts/pallas_call | solution.py:354
  67.7 3.5 %all-to-all-start.2 = ((bf16[4,32,1152]{2,1,0:T(8,128)(2,1)}), bf16[4,32,1152]{2,1,0:T(8,128)(2,1)S(1)}, u32[]{:S(2)}, u32[]{:S(2)}) async-start(bf16[4,32,1152]{2,1,0:T(8,128)(2,1)} %bitcast.9), calls=%async_computation.2 | async-start | bytes 589824 | tf_op jit(solution)/shard_map/all_to_all | solution.py:370
  71.2 2.3 %all_gather.7.wide_ref = bf16[256,1280]{1,0:T(8,128)(2,1)S(1)} all-gather(bf16[128,1280]{1,0:T(8,128)(2,1)S(1)} %bitcast.19), channel_id=1, replica_groups={{0,1},{2,3},{4,5},{6,7},{8,9},{10,11},{12,13},{14,15},{16,17},{18,19},{..., dimensions={0}, use_global_device_ids=true | all-gather | bytes 983040 | tf_op jit(solution)/shard_map/all_gather | solution.py:401
  73.5 0.7 image_parts.1
  74.1 4.1 %collective-permute-start.2 = (bf16[32,1152]{1,0:T(8,128)(2,1)S(1)}, bf16[32,1152]{1,0:T(8,128)(2,1)S(1)}, u32[]{:S(2)}, u32[]{:S(2)}) collective-permute-start(bf16[32,1152]{1,0:T(8,128)(2,1)S(1)} %get-tuple-element.21), channel_id=1, source_target_pairs={{0,24},{1,25},{2,26},{3,27},{4,28},{5,29},{6,30},{7,31},{8,16},{9,... | collective-permute-start | bytes 221192 | tf_op jit(solution)/shard_map/ppermute | solution.py:397
  78.2 0.0 all-to-all-done.2
  78.3 4.3 %collective-permute-start.3 = (bf16[32,1152]{1,0:T(8,128)(2,1)S(1)}, bf16[32,1152]{1,0:T(8,128)(2,1)S(1)}, u32[]{:S(2)}, u32[]{:S(2)}) collective-permute-start(bf16[32,1152]{1,0:T(8,128)(2,1)S(1)} %get-tuple-element.22), channel_id=1, source_target_pairs={{0,16},{1,17},{2,18},{3,19},{4,20},{5,21},{6,22},{7,23},{8,24},{9,... | collective-permute-start | bytes 221192 | tf_op jit(solution)/shard_map/ppermute | solution.py:397
  82.6 2.0 %collective-permute-start.4 = (bf16[32,1152]{1,0:T(8,128)(2,1)S(1)}, bf16[32,1152]{1,0:T(8,128)(2,1)S(1)}, u32[]{:S(2)}, u32[]{:S(2)}) collective-permute-start(bf16[32,1152]{1,0:T(8,128)(2,1)S(1)} %get-tuple-element.23), channel_id=1, source_target_pairs={{0,8},{1,9},{2,10},{3,11},{4,12},{5,13},{6,14},{7,15},{8,0},{9,1},... | collective-permute-start | bytes 221192 | tf_op jit(solution)/shard_map/ppermute | solution.py:397
  84.6 0.7 multiply_bitcast_fusion.1
  85.3 0.0 collective-permute-done.2
  85.3 1.4 %collective-permute-done.3 = bf16[32,1152]{1,0:T(8,128)(2,1)S(1)} collective-permute-done((bf16[32,1152]{1,0:T(8,128)(2,1)S(1)}, bf16[32,1152]{1,0:T(8,128)(2,1)S(1)}, u32[]{:S(2)}, u32[]{:S(2)}) %collective-permute-start.3) | collective-permute-done | bytes 73760 | tf_op jit(solution)/shard_map/ppermute | solution.py:397
  86.7 2.2 %collective-permute-done.4 = bf16[32,1152]{1,0:T(8,128)(2,1)S(1)} collective-permute-done((bf16[32,1152]{1,0:T(8,128)(2,1)S(1)}, bf16[32,1152]{1,0:T(8,128)(2,1)S(1)}, u32[]{:S(2)}, u32[]{:S(2)}) %collective-permute-start.4) | collective-permute-done | bytes 73760 | tf_op jit(solution)/shard_map/ppermute | solution.py:397
  88.9 0.7 multiply_bitcast_fusion
  (7 shorter events, 0.1 us)
Async XLA Ops:
  0.6 13.1 %collective-permute-start = (bf16[32,1152]{1,0:T(8,128)(2,1)}, bf16[32,1152]{1,0:T(8,128)(2,1)S(1)}, u32[]{:S(2)}, u32[]{:S(2)}) collective-permute-start(bf16[32,1152]{1,0:T(8,128)(2,1)} %bitcast.24), channel_id=1, source_target_pairs={{0,8},{1,9},{2,10},{3,11},{4,12},{5,13},{6,14},{7,15},{8,0},{9,1},... | collective-permute-start | bytes 221192 | tf_op jit(solution)/shard_map/ppermute | solution.py:397
  4.9 8.9 %copy-start = (bf16[1,1,32,1152]{3,2,1,0:T(8,128)(2,1)S(1)}, bf16[1,1,32,1152]{3,2,1,0:T(8,128)(2,1)}, u32[]{:S(2)}) copy-start(bf16[1,1,32,1152]{3,2,1,0:T(8,128)(2,1)} %param.19) | copy-start | bytes 221188
  13.8 40.4 %all-to-all-start = ((bf16[32,2,640]{2,1,0:T(2,128)(2,1)}), bf16[32,2,640]{2,1,0:T(2,128)(2,1)S(1)}, u32[]{:S(2)}, u32[]{:S(2)}) async-start(bf16[32,2,640]{2,1,0:T(2,128)(2,1)} %tower.1), calls=%async_computation | async-start | bytes 163840 | tf_op jit(solution)/shard_map/all_to_all | solution.py:467
  38.8 20.4 %collective-permute-start.1 = (bf16[64,1152]{1,0:T(8,128)(2,1)S(1)}, bf16[64,1152]{1,0:T(8,128)(2,1)S(1)}, u32[]{:S(2)}, u32[]{:S(2)}) collective-permute-start(bf16[64,1152]{1,0:T(8,128)(2,1)S(1)} %pad_maximum_fusion), channel_id=1, source_target_pairs={{0,16},{1,17},{2,18},{3,19},{4,20},{5,21},{6,22},{7,23},{8,24},{9,... | collective-permute-start | bytes 442376 | tf_op jit(solution)/shard_map/ppermute | solution.py:397
  54.9 11.3 %all-to-all-start.1 = ((bf16[4,32,1280]{2,1,0:T(8,128)(2,1)}), bf16[4,32,1280]{2,1,0:T(8,128)(2,1)S(1)}, u32[]{:S(2)}, u32[]{:S(2)}) async-start(bf16[4,32,1280]{2,1,0:T(8,128)(2,1)} %broadcast_in_dim.14), calls=%async_computation.1 | async-start | bytes 655360 | tf_op jit(solution)/shard_map/all_to_all | solution.py:370
  67.7 10.5 %all-to-all-start.2 = ((bf16[4,32,1152]{2,1,0:T(8,128)(2,1)}), bf16[4,32,1152]{2,1,0:T(8,128)(2,1)S(1)}, u32[]{:S(2)}, u32[]{:S(2)}) async-start(bf16[4,32,1152]{2,1,0:T(8,128)(2,1)} %bitcast.9), calls=%async_computation.2 | async-start | bytes 589824 | tf_op jit(solution)/shard_map/all_to_all | solution.py:370
  74.1 11.2 %collective-permute-start.2 = (bf16[32,1152]{1,0:T(8,128)(2,1)S(1)}, bf16[32,1152]{1,0:T(8,128)(2,1)S(1)}, u32[]{:S(2)}, u32[]{:S(2)}) collective-permute-start(bf16[32,1152]{1,0:T(8,128)(2,1)S(1)} %get-tuple-element.21), channel_id=1, source_target_pairs={{0,24},{1,25},{2,26},{3,27},{4,28},{5,29},{6,30},{7,31},{8,16},{9,... | collective-permute-start | bytes 221192 | tf_op jit(solution)/shard_map/ppermute | solution.py:397
  78.3 8.4 %collective-permute-start.3 = (bf16[32,1152]{1,0:T(8,128)(2,1)S(1)}, bf16[32,1152]{1,0:T(8,128)(2,1)S(1)}, u32[]{:S(2)}, u32[]{:S(2)}) collective-permute-start(bf16[32,1152]{1,0:T(8,128)(2,1)S(1)} %get-tuple-element.22), channel_id=1, source_target_pairs={{0,16},{1,17},{2,18},{3,19},{4,20},{5,21},{6,22},{7,23},{8,24},{9,... | collective-permute-start | bytes 221192 | tf_op jit(solution)/shard_map/ppermute | solution.py:397
  82.6 6.2 %collective-permute-start.4 = (bf16[32,1152]{1,0:T(8,128)(2,1)S(1)}, bf16[32,1152]{1,0:T(8,128)(2,1)S(1)}, u32[]{:S(2)}, u32[]{:S(2)}) collective-permute-start(bf16[32,1152]{1,0:T(8,128)(2,1)S(1)} %get-tuple-element.23), channel_id=1, source_target_pairs={{0,8},{1,9},{2,10},{3,11},{4,12},{5,13},{6,14},{7,15},{8,0},{9,1},... | collective-permute-start | bytes 221192 | tf_op jit(solution)/shard_map/ppermute | solution.py:397
